TPU v7x, 128 devices: a whole 4x4x4 slice. The times are simulated.
128 devices in a mesh: set: 4 (over x), cand: 32 (over z, y, core).
Axes of the slice: x: 4, y: 4, z: 4, core: 2. Of those that a mesh axis runs over, the one named last changes fastest.
Arguments:
- panel_rows: bfloat16 [4, 65536, 512], P('set', 'cand'), may hold values from -10 to 10
- sketch: bfloat16 [4, 512, 32], P('set'), may hold values from -0.25 to 0.25
- accumulator: float32 [4, 256, 256, 256], P('set', 'cand'), may hold values from -6 to 6
- left_block: int32 [4, 32, 128, 2], P('set', 'cand'), may hold values from 0 to 7
- right_block: int32 [4, 32, 128, 2], P('set', 'cand'), may hold values from 0 to 255
- target_slot: int32 [4, 32, 128, 2], P('set', 'cand'), may hold values from 0 to 7
- slot_valid: int32 [4, 32, 128, 2], P('set', 'cand'), may hold values from 0 to 1, as said below
Outputs:
- updated: float32 [4, 256, 256, 256], P('set', 'cand')
Inputs may be any that keep to these rules, and one draw needn't show every extreme that they name: `slot_valid`: padding slots still name blocks; some destination devices receive far more pairs than others.
All inputs are finite; a program needn't handle non-finite values. Where the computation divides by a largest or mean magnitude, that divisor is 1e-20 or more.
Results may differ from a plain program's by a relative error of at most 0.02.
Values may be sent and summed in bfloat16 or wider, within the bound.
No kernel may reach another device: no remote copies, remote signals or barrier semaphores. Data moves between devices by JAX's collectives and lax.ppermute only.
A program may use at most 128 MiB of HBM per device.

v0:
```python
import math

import jax
import jax.numpy as jnp
from jax import lax
from jax.sharding import PartitionSpec as P

W = 512
RANK = 32
BLOCK = 256
NB_DEV = 8
NT_DEV = 8


def per_device(panel_rows, sketch, accumulator, left_block, right_block, target_slot, slot_valid):
    local_rows = panel_rows[0]
    sketched = jnp.dot(local_rows, sketch[0], preferred_element_type=jnp.float32).astype(
        jnp.bfloat16
    )
    sketch_part = lax.dot_general(
        local_rows, sketched, (((0,), (0,)), ((), ())), preferred_element_type=jnp.float32
    )
    summed_sketch = lax.psum(sketch_part, "cand")
    gram_matrix = jnp.dot(summed_sketch.T, summed_sketch, precision=lax.Precision.HIGHEST)
    lower_factor = jnp.linalg.cholesky(gram_matrix)
    basis_rows = jax.scipy.linalg.solve_triangular(
        lower_factor, summed_sketch.T, lower=True
    ).astype(jnp.bfloat16)
    blocks = local_rows.reshape(NB_DEV, BLOCK, W)
    projected = jnp.einsum("rw,nbw->nrb", basis_rows, blocks, preferred_element_type=jnp.float32)
    block_scale = (jnp.max(jnp.abs(projected), axis=(1, 2)) + 1e-06).astype(jnp.bfloat16)
    factor = (projected / block_scale.astype(jnp.float32)[:, None, None]).astype(jnp.bfloat16)
    all_factor, all_scale = (
        lax.all_gather(factor, "cand", axis=0, tiled=True),
        lax.all_gather(block_scale, "cand", axis=0, tiled=True),
    )
    left_index = left_block[0, 0]
    right_index = right_block[0, 0]
    target_index = target_slot[0, 0]
    valid_here = slot_valid[0, 0]
    left_pairs = jnp.take(factor, left_index, axis=0)
    right_pairs = jnp.take(all_factor, right_index, axis=0)
    pair_weight = (
        valid_here.astype(jnp.float32)
        * jnp.take(block_scale, left_index).astype(jnp.float32)
        * jnp.take(all_scale, right_index).astype(jnp.float32)
    ).astype(jnp.bfloat16)
    target_match = target_index[..., None] == jnp.arange(NT_DEV, dtype=jnp.int32)
    weights = jnp.where(target_match, pair_weight[..., None], jnp.zeros((), jnp.bfloat16))
    payload = jnp.stack([left_pairs, right_pairs], axis=2)
    arrived, arrived_weight = (
        lax.all_to_all(payload, ("set", "cand"), split_axis=0, concat_axis=0, tiled=True),
        lax.all_to_all(weights, ("set", "cand"), split_axis=0, concat_axis=0, tiled=True),
    )
    arrived_pairs = arrived.reshape(-1, 2, RANK, BLOCK)
    weight_rows = arrived_weight.reshape(-1, NT_DEV)
    slot_count = arrived_pairs.shape[0]
    slot_weight = jnp.sum(weight_rows.astype(jnp.float32), axis=1)
    target_hot = (weight_rows != 0).astype(jnp.float32)
    scaled_left = (slot_weight[:, None, None] * arrived_pairs[:, 0].astype(jnp.float32)).astype(
        jnp.bfloat16
    )
    right_pairs_in = arrived_pairs[:, 1]
    group = math.gcd(slot_count, 32)
    rounds = slot_count // group
    scaled_groups = scaled_left.reshape(rounds, group, RANK, BLOCK)
    right_groups = right_pairs_in.reshape(rounds, group, RANK, BLOCK)
    hot_groups = target_hot.reshape(rounds, group, NT_DEV)

    def expand(total, pieces):
        scaled_piece, right_piece, hot_piece = pieces
        dense_terms = jnp.einsum(
            "prb,pre->pbe", scaled_piece, right_piece, preferred_element_type=jnp.float32
        )
        return (total + jnp.einsum("pt,pbe->tbe", hot_piece, dense_terms), None)

    empty = jnp.zeros((NT_DEV, BLOCK, BLOCK), jnp.float32)
    summed, unused = lax.scan(expand, empty, (scaled_groups, right_groups, hot_groups))
    return (accumulator[0] - summed)[None]


def solution(mesh):
    placed = (
        P("set", "cand", None),
        P("set", None, None),
        P("set", "cand", None, None),
        P("set", "cand", None, None),
        P("set", "cand", None, None),
        P("set", "cand", None, None),
        P("set", "cand", None, None),
    )
    return jax.shard_map(
        per_device,
        mesh=mesh,
        in_specs=placed,
        out_specs=P("set", "cand", None, None),
        check_vma=False,
    )
```

profile of v0, /device:TPU:6, one launch (start us, length us, event | category | flops | bytes accessed | tf_op | source)
XLA Modules:
  0.0 451.0 jit_solution(12749037604331252965)
XLA Ops:
  10.7 97.8 %all-reduce.3.cloned.1.call-done = f32[512,32]{0,1:T(8,128)} async-done(((f32[512,32]{0,1:T(8,128)}), f32[512,32]{0,1:T(8,128)}) %all-reduce.3.cloned.1.call-update) | async-done | bytes 65552 | tf_op jit(solution)/shard_map/psum | solution.py:23
  109.8 2.9 cholesky.16
  121.5 64.5 %all-reduce = bf16[256]{0:T(256)(128)(2,1)S(1)} all-reduce(bf16[256]{0:T(256)(128)(2,1)S(1)} %dynamic-update-slice.3), channel_id=1, replica_groups=mesh['set'=4,'cand'=32] {'cand'}, use_global_device_ids=true, to_apply=%add | all-reduce | flops 256 | bytes 1024
  188.1 2.8 gather_fusion.1
  191.5 5.1 %fusion.28 = (bf16[128,2]{1,0:T(8,128)(2,1)S(1)}, pred[128,2]{1,0:T(8,128)(4,1)S(1)}, pred[128,2]{1,0:T(8,128)(4,1)S(1)}) fusion(s32[1,1,128,2]{3,2,1,0:T(8,128)S(1)} %copy.37, bf16[128,2]{1,0:T(8,128)(2,1)S(1)} %reshape.173, bf16[]{:T(256)} %bitcast.15, bf16[]{:T(256)} %bitcast.16, bf16[]{:T(256)} %bitcast.17, bf16[]{:T(256)} %bitcast.18, bf16[]{:T(256)} %bitcast.19, ...), kind=kLoop, calls=%fused_computation.41 | loop fusion | flops 9472 | bytes 4624 | tf_op jit(solution)/shard_map/convert_element_type | solution.py:47
  197.6 4.4 all-to-all-start
  202.0 5.0 %gather_fusion.2 = bf16[256,32,256]{2,1,0:T(8,128)(2,1)} fusion(bf16[256,32,256]{2,1,0:T(8,128)(2,1)} %all-gather.2.cloned.1.call-done, s32[1024]{0:T(1024)S(1)} %pad_clamp_fusion.1), kind=kCustom, calls=%fused_computation.2 | custom fusion | bytes 8389632 | tf_op jit(solution)/shard_map/jit(_take)/gather | solution.py:42
  207.0 5.3 %broadcast_select_fusion = (bf16[128,2,1,32,256]{4,3,1,2,0:T(8,128)(2,1)S(1)}, bf16[128,2,1,32,256]{4,3,1,2,0:T(8,128)(2,1)}) fusion(bf16[128,2,1,32,256]{4,3,1,2,0:T(8,128)(2,1)} %bitcast.118, pred[128,2]{1,0:T(8,128)(4,1)S(1)} %get-tuple-element.77, bf16[128,2,1,32,256]{4,3,1,2,0:T(8,128)(2,1)} %bitcast.117, pred[128,2]{1,0:T(8,128)(4,1)S(1)} %get-tuple-element.78), kind=kLoop, calls=%fused_computation.18 | loop fusion | flops 4194304 | bytes 16777728 | tf_op jit(solution)/shard_map/jit(_take)/select_n | solution.py:42
  212.3 6.3 %pad_maximum_fusion = bf16[128,2,2,32,256]{4,3,1,2,0:T(8,128)(2,1)} fusion(bf16[128,2,1,32,256]{4,3,1,2,0:T(8,128)(2,1)S(1)} %get-tuple-element.93, bf16[128,2,1,32,256]{4,3,1,2,0:T(8,128)(2,1)} %get-tuple-element.94), kind=kLoop, calls=%fused_computation.15 | loop fusion | flops 4194304 | bytes 16777216 | tf_op jit(solution)/shard_map/stack | solution.py:50
  218.6 10.2 %all-to-all-start.1 = ((bf16[128,2,2,32,256]{4,3,1,2,0:T(8,128)(2,1)}), bf16[128,2,2,32,256]{4,3,1,2,0:T(8,128)(2,1)}, u32[]{:S(2)}, u32[]{:S(2)}) async-start(bf16[128,2,2,32,256]{4,3,1,2,0:T(8,128)(2,1)} %pad_maximum_fusion), calls=%async_computation.1 | async-start | bytes 16777216 | tf_op jit(solution)/shard_map/all_to_all | solution.py:52
  229.3 105.9 %all-to-all-done.1 = bf16[128,2,2,32,256]{4,3,1,2,0:T(8,128)(2,1)} async-done(((bf16[128,2,2,32,256]{4,3,1,2,0:T(8,128)(2,1)}), bf16[128,2,2,32,256]{4,3,1,2,0:T(8,128)(2,1)}, u32[]{:S(2)}, u32[]{:S(2)}) %all-to-all-start.1) | async-done | bytes 8388640 | tf_op jit(solution)/shard_map/all_to_all | solution.py:52
  335.2 8.0 %copy.45 = bf16[128,2,2,32,256]{4,3,2,1,0:T(8,128)(2,1)} copy(bf16[128,2,2,32,256]{4,3,1,2,0:T(8,128)(2,1)} %all-to-all-done.1) | data formatting | bytes 16777216 | tf_op jit(solution)/shard_map/all_to_all | solution.py:52
  343.3 5.3 %fusion.36 = (bf16[256,1,32,256]{3,2,1,0:T(8,128)(2,1)}, bf16[256,1,32,256]{3,2,1,0:T(8,128)(2,1)S(1)}) fusion(bf16[256,2,32,256]{3,2,1,0:T(8,128)(2,1)} %bitcast.116), kind=kLoop, calls=%fused_computation.66 | loop fusion | bytes 16777216 | tf_op jit(solution)/shard_map/slice | solution.py:63
  348.5 2.7 fusion.13
  351.2 88.5 %while.11 = (s32[]{:T(128)}, f32[8,256,256]{2,0,1:T(8,128)}, bf16[8,32,8]{1,2,0:T(8,128)(2,1)S(1)}, bf16[8,32,32,256]{3,2,1,0:T(8,128)(2,1)}, bf16[8,32,32,256]{3,2,1,0:T(8,128)(2,1)}, /*index=5*/s32[]{:T(128)}, s32[]{:T(128)}) while((s32[]{:T(128)}, f32[8,256,256]{2,0,1:T(8,128)}, bf16[8,32,8]{1,2,0:T(8,128)(2,1)S(1)}, ...), condition=%wide.region_6.7_spmd.clone, body=%wide.region_5.6_spmd.clone.sunk | while | flops 168820736 | bytes 13634651 | solution.py:78
  351.2 4.5 fusion.53
  355.7 6.0 %select_add_fusion.2 = f32[8,256,256]{2,0,1:T(8,128)} fusion(f32[8,256,256]{2,0,1:T(8,128)} %get-tuple-element.134, bf16[32,256,256]{2,1,0:T(8,128)(2,1)} %fusion.53, pred[]{:T(512)S(6)} %compare.63, bf16[8,32,8]{1,2,0:T(8,128)(2,1)S(1)} %get-tuple-element.142, s32[]{:T(128)} %get-tuple-element.133), kind=kOutput, calls=%fused_computation.5.clone.1 | convolution fusion | flops 34603008 | bytes 8390661 | tf_op jit(solution)/shard_map/while/body/eval_jaxpr/pt,pbe->tbe/dot_general | solution.py:75
  361.7 4.5 fusion.53
  366.2 6.7 %select_add_fusion.2 = f32[8,256,256]{2,0,1:T(8,128)} fusion(f32[8,256,256]{2,0,1:T(8,128)} %get-tuple-element.134, bf16[32,256,256]{2,1,0:T(8,128)(2,1)} %fusion.53, pred[]{:T(512)S(6)} %compare.63, bf16[8,32,8]{1,2,0:T(8,128)(2,1)S(1)} %get-tuple-element.142, s32[]{:T(128)} %get-tuple-element.133), kind=kOutput, calls=%fused_computation.5.clone.1 | convolution fusion | flops 34603008 | bytes 8390661 | tf_op jit(solution)/shard_map/while/body/eval_jaxpr/pt,pbe->tbe/dot_general | solution.py:75
  372.8 4.5 fusion.53
  377.3 6.7 %select_add_fusion.2 = f32[8,256,256]{2,0,1:T(8,128)} fusion(f32[8,256,256]{2,0,1:T(8,128)} %get-tuple-element.134, bf16[32,256,256]{2,1,0:T(8,128)(2,1)} %fusion.53, pred[]{:T(512)S(6)} %compare.63, bf16[8,32,8]{1,2,0:T(8,128)(2,1)S(1)} %get-tuple-element.142, s32[]{:T(128)} %get-tuple-element.133), kind=kOutput, calls=%fused_computation.5.clone.1 | convolution fusion | flops 34603008 | bytes 8390661 | tf_op jit(solution)/shard_map/while/body/eval_jaxpr/pt,pbe->tbe/dot_general | solution.py:75
  384.0 4.5 fusion.53
  388.5 6.7 %select_add_fusion.2 = f32[8,256,256]{2,0,1:T(8,128)} fusion(f32[8,256,256]{2,0,1:T(8,128)} %get-tuple-element.134, bf16[32,256,256]{2,1,0:T(8,128)(2,1)} %fusion.53, pred[]{:T(512)S(6)} %compare.63, bf16[8,32,8]{1,2,0:T(8,128)(2,1)S(1)} %get-tuple-element.142, s32[]{:T(128)} %get-tuple-element.133), kind=kOutput, calls=%fused_computation.5.clone.1 | convolution fusion | flops 34603008 | bytes 8390661 | tf_op jit(solution)/shard_map/while/body/eval_jaxpr/pt,pbe->tbe/dot_general | solution.py:75
  395.1 4.5 fusion.53
  399.6 6.7 %select_add_fusion.2 = f32[8,256,256]{2,0,1:T(8,128)} fusion(f32[8,256,256]{2,0,1:T(8,128)} %get-tuple-element.134, bf16[32,256,256]{2,1,0:T(8,128)(2,1)} %fusion.53, pred[]{:T(512)S(6)} %compare.63, bf16[8,32,8]{1,2,0:T(8,128)(2,1)S(1)} %get-tuple-element.142, s32[]{:T(128)} %get-tuple-element.133), kind=kOutput, calls=%fused_computation.5.clone.1 | convolution fusion | flops 34603008 | bytes 8390661 | tf_op jit(solution)/shard_map/while/body/eval_jaxpr/pt,pbe->tbe/dot_general | solution.py:75
  406.3 4.5 fusion.53
  410.8 6.7 %select_add_fusion.2 = f32[8,256,256]{2,0,1:T(8,128)} fusion(f32[8,256,256]{2,0,1:T(8,128)} %get-tuple-element.134, bf16[32,256,256]{2,1,0:T(8,128)(2,1)} %fusion.53, pred[]{:T(512)S(6)} %compare.63, bf16[8,32,8]{1,2,0:T(8,128)(2,1)S(1)} %get-tuple-element.142, s32[]{:T(128)} %get-tuple-element.133), kind=kOutput, calls=%fused_computation.5.clone.1 | convolution fusion | flops 34603008 | bytes 8390661 | tf_op jit(solution)/shard_map/while/body/eval_jaxpr/pt,pbe->tbe/dot_general | solution.py:75
  417.4 4.5 fusion.53
  421.9 6.7 %select_add_fusion.2 = f32[8,256,256]{2,0,1:T(8,128)} fusion(f32[8,256,256]{2,0,1:T(8,128)} %get-tuple-element.134, bf16[32,256,256]{2,1,0:T(8,128)(2,1)} %fusion.53, pred[]{:T(512)S(6)} %compare.63, bf16[8,32,8]{1,2,0:T(8,128)(2,1)S(1)} %get-tuple-element.142, s32[]{:T(128)} %get-tuple-element.133), kind=kOutput, calls=%fused_computation.5.clone.1 | convolution fusion | flops 34603008 | bytes 8390661 | tf_op jit(solution)/shard_map/while/body/eval_jaxpr/pt,pbe->tbe/dot_general | solution.py:75
  428.6 4.5 fusion.53
  433.1 6.7 %select_add_fusion.2 = f32[8,256,256]{2,0,1:T(8,128)} fusion(f32[8,256,256]{2,0,1:T(8,128)} %get-tuple-element.134, bf16[32,256,256]{2,1,0:T(8,128)(2,1)} %fusion.53, pred[]{:T(512)S(6)} %compare.63, bf16[8,32,8]{1,2,0:T(8,128)(2,1)S(1)} %get-tuple-element.142, s32[]{:T(128)} %get-tuple-element.133), kind=kOutput, calls=%fused_computation.5.clone.1 | convolution fusion | flops 34603008 | bytes 8390661 | tf_op jit(solution)/shard_map/while/body/eval_jaxpr/pt,pbe->tbe/dot_general | solution.py:75
  439.7 4.5 fusion.17
  (56 shorter events, 17.6 us)
Async XLA Ops:
  6.5 1.7 copy-start
  6.5 113.4 %copy-start.7 = (u32[128]{0:T(128)S(1)}, u32[128]{0:T(128)}, u32[]{:S(2)}) copy-start(u32[128]{0:T(128)} %constant.134) | copy-start | bytes 1540
  6.5 112.7 %copy-start.3 = (s32[1,1,128,2]{2,3,1,0:T(2,128)S(1)}, s32[1,1,128,2]{2,3,1,0:T(2,128)}, u32[]{:S(2)}) copy-start(s32[1,1,128,2]{2,3,1,0:T(2,128)} %param.13) | copy-start | bytes 3076
  6.5 112.9 %copy-start.4 = (s32[1,1,128,2]{2,3,1,0:T(2,128)S(1)}, s32[1,1,128,2]{2,3,1,0:T(2,128)}, u32[]{:S(2)}) copy-start(s32[1,1,128,2]{2,3,1,0:T(2,128)} %param.12) | copy-start | bytes 3076
  6.5 113.0 %copy-start.5 = (s32[1,1,128,2]{2,3,1,0:T(2,128)S(1)}, s32[1,1,128,2]{2,3,1,0:T(2,128)}, u32[]{:S(2)}) copy-start(s32[1,1,128,2]{2,3,1,0:T(2,128)} %param.15) | copy-start | bytes 3076
  6.5 113.3 %copy-start.6 = (s32[1,1,128,2]{2,3,1,0:T(2,128)S(1)}, s32[1,1,128,2]{2,3,1,0:T(2,128)}, u32[]{:S(2)}) copy-start(s32[1,1,128,2]{2,3,1,0:T(2,128)} %param.14) | copy-start | bytes 3076
  6.6 102.0 %all-reduce.3.cloned.1.call-start = ((), (), s32[]{:S(2)}) async-start(), calls=%async_computation.2 | async-start | bytes 131072 | tf_op jit(solution)/shard_map/psum | solution.py:23
  10.7 191.4 %all-gather.2.cloned.1.call-start = ((), (), s32[]{:S(2)}) async-start(), calls=%async_computation.3 | async-start | bytes 4325376 | tf_op jit(solution)/shard_map/all_gather | solution.py:34
  186.0 2.0 copy-start.2
  197.6 21.0 %all-to-all-start = ((bf16[128,2,8]{2,1,0:T(2,128)(2,1)}), bf16[128,2,8]{2,1,0:T(2,128)(2,1)S(1)}, u32[]{:S(2)}, u32[]{:S(2)}) async-start(bf16[128,2,8]{2,1,0:T(2,128)(2,1)} %compare_select_fusion), calls=%async_computation | async-start | bytes 131072 | tf_op jit(solution)/shard_map/all_to_all | solution.py:53
  218.6 116.6 %all-to-all-start.1 = ((bf16[128,2,2,32,256]{4,3,1,2,0:T(8,128)(2,1)}), bf16[128,2,2,32,256]{4,3,1,2,0:T(8,128)(2,1)}, u32[]{:S(2)}, u32[]{:S(2)}) async-start(bf16[128,2,2,32,256]{4,3,1,2,0:T(8,128)(2,1)} %pad_maximum_fusion), calls=%async_computation.1 | async-start | bytes 16777216 | tf_op jit(solution)/shard_map/all_to_all | solution.py:52
  439.7 4.5 copy-start.1
Sparse Core Ops, SparseCore 0:
  10.8 97.7 all-reduce.2
  119.3 45.2 all-gather.1
where the time goes:
time: 453 us; the launch traced here: 451 us
  waiting for transfers between devices  204 us (45%)
  matrix products  94 us (21%)
  blocking collectives  64.5 us (14%)
  other arithmetic  32.5 us (7%)
  local copies, waits for them, and re-layouts  27.3 us (6%)
  starting transfers between devices  14.7 us (3%)
  between operations  14.2 us (3%)
    all_to_all x1, waiting for transfers between devices, per_device(): lax.all_to_all(payload, ('set', 'cand'), split_axis=0, concat_axis=0, til...  106 us
    psum x1, waiting for transfers between devices, per_device(): summed_sketch = lax.psum(sketch_part, 'cand')  97.8 us
    unnamed x1, blocking collectives  64.5 us
    dot_general x8, matrix products, expand(): return (total + jnp.einsum('pt,pbe->tbe', hot_piece, dense_terms), None)  52.7 us
    dot_general x8, matrix products, expand(): jnp.einsum('prb,pre->pbe', scaled_piece, right_piece, preferred_element_t...  35.8 us
    all_to_all x1, starting transfers between devices, per_device(): lax.all_to_all(payload, ('set', 'cand'), split_axis=0, concat_axis=0, til...  10.2 us
  transfers between devices with their start and end apart: 4, of which 2 were waited for; matrix products, arithmetic and copies ran while one was open for 7% of the time, Pallas kernels for 0%

commit v1 on v0

v1 whole, which is shorter than its diff:
```python
import jax
import jax.numpy as jnp
from jax import lax
from jax.experimental import pallas as pl
from jax.experimental.pallas import tpu as pltpu
from jax.sharding import PartitionSpec as P

W = 512
RANK = 32
BLOCK = 256
NB_DEV = 8
NT_DEV = 8
N_SET = 4
N_CAND = 32
HALF = RANK // 2
ROWS = NB_DEV * BLOCK
A_ROWS = 4 * RANK + 16
B_ROWS = 4 * RANK
MSG = A_ROWS + B_ROWS
SLOTS = 2
PER_CHUNK = 8
LIST = 128
ZERO = NB_DEV * N_CAND
f32, bf16, i32 = jnp.float32, jnp.bfloat16, jnp.int32
VMEM = pl.BlockSpec(memory_space=pltpu.VMEM)
SMEM = pl.BlockSpec(memory_space=pltpu.SMEM)
ANY = pl.BlockSpec(memory_space=pl.ANY)
NT = (((1,), (1,)), ((), ()))
TN = (((0,), (0,)), ((), ()))


def params(mib=40):
    return pltpu.CompilerParams(vmem_limit_bytes=mib * 1024 * 1024)


def from_cand(x, dz, dy, dcore=0):
    pairs = []
    for me in range(N_CAND):
        z, y, core = me // 8, (me // 2) % 4, me % 2
        source = ((z + dz) % 4) * 8 + ((y + dy) % 4) * 2 + (core ^ dcore)
        pairs.append((source, me))
    return lax.ppermute(x, "cand", pairs)


def from_set(x, d):
    return lax.ppermute(x, "set", [((me + d) % N_SET, me) for me in range(N_SET)])


def sketch_kernel(place, rows, sketch, keep, give, total):
    step = pl.program_id(0)

    @pl.when(step == 0)
    def _():
        total[...] = jnp.zeros_like(total)

    sketched = jnp.dot(rows[...], sketch[...], preferred_element_type=f32).astype(bf16)
    total[...] += lax.dot_general(sketched, rows[...], TN, preferred_element_type=f32)

    @pl.when(step == pl.num_programs(0) - 1)
    def _():
        core = place[1] % 2
        keep[...] = total[pl.ds(pl.multiple_of(core * HALF, HALF), HALF), :]
        give[...] = total[pl.ds(pl.multiple_of((1 - core) * HALF, HALF), HALF), :]


def sketch_call(place, rows, sketch):
    step = 512
    half = jax.ShapeDtypeStruct((HALF, W), f32)
    return pl.pallas_call(
        sketch_kernel,
        grid=(ROWS // step,),
        out_shape=(half, half),
        in_specs=[
            SMEM,
            pl.BlockSpec((step, W), lambda i: (i, 0)),
            pl.BlockSpec((W, RANK), lambda i: (0, 0)),
        ],
        out_specs=(pl.BlockSpec((HALF, W), lambda i: (0, 0)),) * 2,
        scratch_shapes=[pltpu.VMEM((RANK, W), f32)],
        compiler_params=params(),
        name="sketch",
    )(place, rows, sketch)


def sum_core_kernel(keep, got, slots, out):
    out[0:HALF, :] = keep[...] + got[...]
    out[HALF:, :] = jnp.zeros((8, W), f32)
    out[HALF:, 0:128] = slots[...]


def sum_y_kernel(r0, r1, r2, r3, out):
    out[0:HALF, :] = (r0[0:HALF, :] + r2[0:HALF, :]) + (r1[0:HALF, :] + r3[0:HALF, :])
    for k, r in enumerate((r0, r1, r2, r3)):
        out[HALF:, k * 128 : (k + 1) * 128] = r[HALF:, 0:128]


def sum_z_kernel(r0, r1, r2, r3, out):
    out[0:HALF, :] = (r0[0:HALF, :] + r2[0:HALF, :]) + (r1[0:HALF, :] + r3[0:HALF, :])
    for k, r in enumerate((r0, r1, r2, r3)):
        out[HALF + 8 * k : HALF + 8 * (k + 1), :] = r[HALF:, :]


def small_call(kernel, rows, name, *args):
    return pl.pallas_call(
        kernel,
        out_shape=jax.ShapeDtypeStruct((rows, W), f32),
        in_specs=[VMEM] * len(args),
        out_specs=VMEM,
        compiler_params=params(),
        name=name,
    )(*args)


def factor_kernel(place, own, other, rows_hbm, out_a, out_b, rows, sem):
    copy = pltpu.make_async_copy(rows_hbm, rows, sem)
    copy.start()
    first = place[1] % 2 == 0
    mine, theirs = own[0:HALF, :], other[0:HALF, :]
    summed = jnp.concatenate(
        [jnp.where(first, mine, theirs), jnp.where(first, theirs, mine)], axis=0
    )
    padded = jnp.concatenate([summed, jnp.zeros((96, W), f32)], axis=0)
    gram = lax.dot_general(
        summed, padded, NT, precision=lax.Precision.HIGHEST, preferred_element_type=f32
    )
    lane = lax.broadcasted_iota(i32, (RANK, 128), 1)
    line = lax.broadcasted_iota(i32, (RANK, 128), 0)
    work = gram + jnp.where(lane == line + RANK, 1.0, 0.0)
    for k in range(RANK - 1):
        column = jnp.broadcast_to(work[:, k : k + 1], (RANK, 128))
        pivot_row = work[k : k + 1, :] / column[k : k + 1, :]
        work = work - jnp.where(line > k, column, 0.0) * pivot_row
    pivots = jnp.sum(jnp.where(lane == line, work, 0.0), axis=1, keepdims=True)
    inverse = work * lax.rsqrt(pivots)
    shifted = jnp.concatenate([jnp.zeros((32, W), f32), summed, jnp.zeros((64, W), f32)], axis=0)
    basis = jnp.dot(
        inverse, shifted, precision=lax.Precision.HIGHEST, preferred_element_type=f32
    ).astype(bf16)
    copy.wait()
    index = lax.broadcasted_iota(i32, (16, BLOCK), 0)
    scales = jnp.zeros((16, BLOCK), f32)
    for b in range(NB_DEV):
        projected = lax.dot_general(
            basis, rows[b * BLOCK : (b + 1) * BLOCK, :], NT, preferred_element_type=f32
        )
        most = jnp.max(jnp.max(jnp.abs(projected), axis=0, keepdims=True), axis=1, keepdims=True)
        scale = (most + 1e-06).astype(bf16).astype(f32)
        factor = (projected / scale).astype(bf16)
        scales = jnp.where(index == b, scale, scales)
        if b < 4:
            out_a[b * RANK : (b + 1) * RANK, :] = factor
        else:
            out_b[(b - 4) * RANK : (b - 3) * RANK, :] = factor
    out_a[4 * RANK :, :] = scales.astype(bf16)


def factor_call(place, own, other, rows):
    return pl.pallas_call(
        factor_kernel,
        out_shape=(
            jax.ShapeDtypeStruct((A_ROWS, BLOCK), bf16),
            jax.ShapeDtypeStruct((B_ROWS, BLOCK), bf16),
        ),
        in_specs=[SMEM, VMEM, VMEM, ANY],
        out_specs=(VMEM, VMEM),
        scratch_shapes=[pltpu.VMEM((ROWS, W), bf16), pltpu.SemaphoreType.DMA],
        compiler_params=params(),
        name="factor",
    )(place, own, other, rows)


def plan_kernel(place, own, other, *refs):
    lists, (gathered, picked_v, picked, at, sem) = refs[:N_SET], refs[N_SET:]
    me_set, me = place[0], place[1]
    me_z, me_y, me_core = me // 8, (me // 2) % 4, me % 2
    for core, r in enumerate((own, other)):
        for z in range(4):
            for y in range(4):
                s = (core * 4 + z) * 4 + y
                gathered[s * 8 : (s + 1) * 8, :] = r[
                    HALF + 8 * z : HALF + 8 * (z + 1), y * 128 : (y + 1) * 128
                ].astype(bf16)
    line = lax.broadcasted_iota(i32, (16, 128), 0)
    lane = lax.broadcasted_iota(i32, (16, 128), 1)
    wanted = ((me_set + line) % N_SET) * N_CAND + me
    hot = jnp.where((lane == wanted) & (line < N_SET), 1.0, 0.0).astype(bf16)
    values = lax.dot_general(hot, gathered[...], NT, preferred_element_type=f32)
    picked_v[...] = values[0:8, :].astype(i32)
    copy = pltpu.make_async_copy(picked_v, picked, sem)
    copy.start()
    copy.wait()
    for gr in range(N_SET):
        out = lists[gr]
        for t in range(NT_DEV):
            at[t] = 0

        def count(s, carry):
            for slot in range(SLOTS):
                t = picked[gr, s * 8 + 4 + slot]
                at[t] = at[t] + picked[gr, s * 8 + 6 + slot]
            return carry

        lax.fori_loop(0, N_CAND, count, 0)
        start = 0
        for t in range(NT_DEV):
            chunks = (at[t] + (PER_CHUNK - 1)) // PER_CHUNK
            out[2 * LIST + t] = chunks
            at[t] = start
            start = start + chunks * PER_CHUNK

        def put(s, carry):
            s_core, s_z, s_y = s // 16, (s // 4) % 4, s % 4
            if gr == 2:
                sender = ((s_z + me_z) % 4) * 8 + ((s_y + me_y) % 4) * 2 + (s_core + me_core) % 2
            else:
                sender = s
            for slot in range(SLOTS):
                left = sender * NB_DEV + picked[gr, s * 8 + slot]
                right = picked[gr, s * 8 + 2 + slot]
                if gr != 2:
                    owner = right // NB_DEV
                    r_z, r_y, r_core = owner // 8, (owner // 2) % 4, owner % 2
                    owner = (
                        ((r_core + me_core) % 2) * 4 + (r_z - me_z + 4) % 4
                    ) * 4 + (r_y - me_y + 4) % 4
                    right = owner * NB_DEV + right % NB_DEV
                t = picked[gr, s * 8 + 4 + slot]
                valid = picked[gr, s * 8 + 6 + slot]

                @pl.when(valid != 0)
                def _():
                    spot = at[t]
                    out[spot] = left
                    out[LIST + spot] = right
                    at[t] = spot + 1

            return carry

        lax.fori_loop(0, N_CAND, put, 0)
        end = 0
        for t in range(NT_DEV):
            end = end + out[2 * LIST + t] * PER_CHUNK

            def fill(spot, carry):
                out[spot] = ZERO
                out[LIST + spot] = 0
                return carry

            lax.fori_loop(at[t], end, fill, 0)


def plan_call(place, own, other):
    return pl.pallas_call(
        plan_kernel,
        out_shape=(jax.ShapeDtypeStruct((1024,), i32),) * N_SET,
        in_specs=[SMEM, VMEM, VMEM],
        out_specs=(SMEM,) * N_SET,
        scratch_shapes=[
            pltpu.VMEM((N_CAND * 8, 128), bf16),
            pltpu.VMEM((8, N_CAND * 8), i32),
            pltpu.SMEM((8, N_CAND * 8), i32),
            pltpu.SMEM((NT_DEV,), i32),
            pltpu.SemaphoreType.DMA,
        ],
        compiler_params=params(),
        name="plan",
    )(place, own, other)


def spread(factors, scales):
    for p in range(N_CAND):
        scales[p * NB_DEV : (p + 1) * NB_DEV, :] = factors[
            p, 4 * RANK : 4 * RANK + 16, 0:128
        ].astype(f32)[0:NB_DEV, :]
    scales[ZERO : ZERO + 8, :] = jnp.zeros((8, 128), f32)


def block_at(factors, b):
    p, j = (b & (ZERO - 1)) // NB_DEV, b % NB_DEV
    off = pl.multiple_of(j * RANK + jnp.where(j >= 4, 16, 0), 16)
    return factors.at[p, pl.ds(off, RANK), :]


def expand(pairs, t, factors, scales, lefts, rights, start, total):
    def chunk(q, carry):
        for k in range(PER_CHUNK):
            spot = start + q * PER_CHUNK + k
            left, right = pairs[spot], pairs[LIST + spot]
            weight = scales[pl.ds(left, 1), :] * scales[pl.ds(right, 1), :]
            weight = weight.astype(bf16).astype(f32)
            weight = jnp.concatenate([weight, weight], axis=1)
            here = slice(k * RANK, (k + 1) * RANK)
            lefts[here, :] = (block_at(factors, left)[...].astype(f32) * weight).astype(bf16)
            rights[here, :] = block_at(factors, right)[...]
        total[...] += lax.dot_general(lefts[...], rights[...], TN, preferred_element_type=f32)
        return carry

    total[...] = jnp.zeros_like(total)
    chunks = pairs[2 * LIST + t]
    lax.fori_loop(0, chunks, chunk, 0)
    return start + chunks * PER_CHUNK


WORK = [
    pltpu.VMEM((N_CAND, MSG, BLOCK), bf16),
    pltpu.VMEM((ZERO + 8, 128), f32),
    pltpu.VMEM((RANK * PER_CHUNK, BLOCK), bf16),
    pltpu.VMEM((RANK * PER_CHUNK, BLOCK), bf16),
    pltpu.VMEM((BLOCK, BLOCK), f32),
]


def collect(pieces, factors, sems):
    copies = []
    for core in range(2):
        for k in range(4):
            a, b = pieces[core * 8 + k], pieces[core * 8 + 4 + k]
            copies.append(
                (a, factors.at[pl.ds(core * 16 + k * 4, 4), pl.ds(0, A_ROWS), :])
            )
            for z in range(4):
                copies.append(
                    (b.at[z], factors.at[core * 16 + z * 4 + k, pl.ds(A_ROWS, B_ROWS), :])
                )
    started = []
    for n, (source, target) in enumerate(copies):
        copy = pltpu.make_async_copy(source, target, sems.at[n])
        copy.start()
        started.append(copy)
    for copy in started:
        copy.wait()


def send_kernel(next_list, last_list, *refs):
    pieces, (to_next, to_last), work = refs[:16], refs[16:18], refs[18:]
    factors, scales, lefts, rights, total, sems = work
    collect(pieces, factors, sems)
    spread(factors, scales)
    start = [0, 0]
    for t in range(NT_DEV):
        for n, (pairs, out) in enumerate(((next_list, to_next), (last_list, to_last))):
            start[n] = expand(pairs, t, factors, scales, lefts, rights, start[n], total)
            out[t] = total[...].astype(bf16)


def send_call(next_list, last_list, pieces):
    out = jax.ShapeDtypeStruct((NT_DEV, BLOCK, BLOCK), bf16)
    return pl.pallas_call(
        send_kernel,
        out_shape=(out, out),
        in_specs=[SMEM, SMEM] + [ANY] * 16,
        out_specs=(VMEM, VMEM),
        scratch_shapes=WORK + [pltpu.SemaphoreType.DMA((40,))],
        compiler_params=params(),
        name="send_pairs",
    )(next_list, last_list, *pieces)


def own_kernel(own_list, base, *refs):
    pieces, out, work = refs[:16], refs[16], refs[17:]
    factors, scales, lefts, rights, total, sems = work
    collect(pieces, factors, sems)
    spread(factors, scales)
    start = 0
    for t in range(NT_DEV):
        start = expand(own_list, t, factors, scales, lefts, rights, start, total)
        out[t] = base[t] - total[...]


def own_call(own_list, base, pieces):
    return pl.pallas_call(
        own_kernel,
        out_shape=jax.ShapeDtypeStruct((NT_DEV, BLOCK, BLOCK), f32),
        in_specs=[SMEM, VMEM] + [ANY] * 16,
        out_specs=VMEM,
        scratch_shapes=WORK + [pltpu.SemaphoreType.DMA((40,))],
        compiler_params=params(),
        name="own_pairs",
    )(own_list, base, *pieces)


def far_kernel(far_list, base, gathered, out, factors, scales, lefts, rights, total, sem):
    copy = pltpu.make_async_copy(gathered, factors, sem)
    copy.start()
    copy.wait()
    spread(factors, scales)
    start = 0
    for t in range(NT_DEV):
        start = expand(far_list, t, factors, scales, lefts, rights, start, total)
        out[t] = base[t] - total[...]


def far_call(far_list, base, gathered):
    return pl.pallas_call(
        far_kernel,
        out_shape=jax.ShapeDtypeStruct((NT_DEV, BLOCK, BLOCK), f32),
        in_specs=[SMEM, VMEM, ANY],
        out_specs=VMEM,
        scratch_shapes=WORK + [pltpu.SemaphoreType.DMA],
        compiler_params=params(),
        name="far_pairs",
    )(far_list, base, gathered)


def per_device(panel_rows, sketch, accumulator, left_block, right_block, target_slot, slot_valid):
    rows = panel_rows[0]
    place = jnp.stack([lax.axis_index("set"), lax.axis_index("cand")]).astype(i32)

    keep, give = sketch_call(place, rows, sketch[0])
    got = from_cand(give, 0, 0, 1)
    slots = jnp.concatenate(
        [x[0, 0].T for x in (left_block, right_block, target_slot, slot_valid)], axis=0
    ).astype(f32)
    part = small_call(sum_core_kernel, HALF + 8, "sum_core", keep, got, slots)
    part = small_call(
        sum_y_kernel, HALF + 8, "sum_y", part, *[from_cand(part, 0, k) for k in (1, 2, 3)]
    )
    own = small_call(
        sum_z_kernel, HALF + 32, "sum_z", part, *[from_cand(part, k, 0) for k in (1, 2, 3)]
    )
    other = from_cand(own, 0, 0, 1)

    part_a, part_b = factor_call(place, own, other, rows)
    far = from_set(jnp.concatenate([part_a, part_b], axis=0), 2)
    all_a = jnp.stack([part_a] + [from_cand(part_a, 0, k) for k in (1, 2, 3)])
    all_b = jnp.stack([part_b] + [from_cand(part_b, k, 0) for k in (1, 2, 3)])
    here = [all_a] + [from_cand(all_a, k, 0) for k in (1, 2, 3)]
    here += [all_b] + [from_cand(all_b, 0, k) for k in (1, 2, 3)]
    pieces = here + [from_cand(x, 0, 0, 1) for x in here]

    own_list, next_list, far_list, last_list = plan_call(place, own, other)
    far_list = from_set(far_list, 2)
    far_all = lax.all_gather(far, "cand", axis=0, tiled=True).reshape(N_CAND, MSG, BLOCK)

    to_next, to_last = send_call(next_list, last_list, pieces)
    from_last = from_set(to_next, 3)
    from_next = from_set(to_last, 1)
    base = own_call(own_list, accumulator[0], pieces)
    base = far_call(far_list, base, far_all)
    return (base - (from_last.astype(f32) + from_next.astype(f32)))[None]


def solution(mesh):
    placed = (
        P("set", "cand", None),
        P("set", None, None),
        P("set", "cand", None, None),
        P("set", "cand", None, None),
        P("set", "cand", None, None),
        P("set", "cand", None, None),
        P("set", "cand", None, None),
    )
    return jax.shard_map(
        per_device,
        mesh=mesh,
        in_specs=placed,
        out_specs=P("set", "cand", None, None),
        check_vma=False,
    )
```

time: 453 us -> 166 us (0.37)
  waiting for transfers between devices: 204 us -> 68.8 us
  matrix products: 94 us -> 0 us
  blocking collectives: 64.5 us -> 0 us
  Pallas kernels: 0 us -> 44.6 us
  other arithmetic: 32.5 us -> 3.42 us
  local copies, waits for them, and re-layouts: 27.3 us -> 5.42 us
  starting transfers between devices: 14.7 us -> 28.7 us
    all_to_all x2 -> x0, waiting for transfers between devices: 106 us -> none  [the longest x1 106 us: per_device(): lax.all_to_all(payload, ('set', 'cand'), split_axis=0, concat_axis=0, til...]
    psum x1 -> x0, waiting for transfers between devices: 97.8 us -> none  [per_device(): summed_sketch = lax.psum(sketch_part, 'cand')]
    dot_general x19 -> x0, matrix products: 92.9 us -> none  [the longest x8 52.7 us: expand(): return (total + jnp.einsum('pt,pbe->tbe', hot_piece, dense_terms), None)]
    ppermute x0 -> x32, waiting for transfers between devices: none -> 68.8 us  [the longest x28 47.1 us: from_cand(): return lax.ppermute(x, 'cand', pairs)]
    unnamed x1 -> x0, blocking collectives: 64.5 us -> none
    pallas_call x0 -> x9, Pallas kernels: none -> 44.6 us  [the longest x1 14.2 us: plan_call(): pl.pallas_call(plan_kernel, out_shape=(jax.ShapeDtypeStruct((1024,), i32)...]
    ppermute x0 -> x32, starting transfers between devices: none -> 28.6 us  [the longest x28 24.8 us: from_cand(): return lax.ppermute(x, 'cand', pairs)]
    all_to_all x2 -> x0, starting transfers between devices: 14.6 us -> none  [the longest x1 10.2 us: per_device(): lax.all_to_all(payload, ('set', 'cand'), split_axis=0, concat_axis=0, til...]
  transfers between devices with their start and end apart: 4 -> 33, of which waited for: 2 -> 16; matrix products, arithmetic and copies ran while one was open for 7% -> 0% of each run, Pallas kernels for 0% -> 23%
where the time goes in v1:
time: 166 us; the launch traced here: 165 us
  waiting for transfers between devices  68.8 us (41%)
  Pallas kernels  44.6 us (27%)
  starting transfers between devices  28.7 us (17%)
  between operations  13.6 us (8%)
  local copies, waits for them, and re-layouts  5.42 us (3%)
  other arithmetic  3.42 us (2%)
    ppermute x28, waiting for transfers between devices, from_cand(): return lax.ppermute(x, 'cand', pairs)  47.1 us
    ppermute x28, starting transfers between devices, from_cand(): return lax.ppermute(x, 'cand', pairs)  24.8 us
    ppermute x4, waiting for transfers between devices, from_set(): lax.ppermute(x, 'set', [((me + d) % N_SET, me) for me in range(N_SET)])  21.7 us
    pallas_call x1, Pallas kernels, plan_call(): pl.pallas_call(plan_kernel, out_shape=(jax.ShapeDtypeStruct((1024,), i32)...  14.2 us
    pallas_call x1, Pallas kernels, send_call(): pl.pallas_call(send_kernel, out_shape=(out, out), in_specs=[SMEM, SMEM] +...  10.5 us
    pallas_call x1, Pallas kernels, own_call(): pl.pallas_call(own_kernel, out_shape=jax.ShapeDtypeStruct((NT_DEV, BLOCK,...  7.86 us
    unnamed x19, local copies, waits for them, and re-layouts  5.42 us
    pallas_call x1, Pallas kernels, factor_call(): pl.pallas_call(factor_kernel, out_shape=(jax.ShapeDtypeStruct((A_ROWS, BL...  4.56 us
  transfers between devices with their start and end apart: 33, of which 16 were waited for; matrix products, arithmetic and copies ran while one was open for 0% of the time, Pallas kernels for 23%

profile of v1, /device:TPU:6, one launch (start us, length us, event | category | flops | bytes accessed | tf_op | source)
XLA Modules:
  0.0 164.5 jit_solution(1650862994324163576)
XLA Ops:
  7.6 1.6 copy-done
  9.2 3.0 %sketch.1 = (f32[16,512]{1,0:T(8,128)S(1)}, f32[16,512]{1,0:T(8,128)S(1)}) custom-call(s32[2]{0:T(128)S(1)} %pad_add_fusion.place, bf16[2048,512]{1,0:T(8,128)(2,1)S(1)} %bitcast.28, bf16[512,32]{1,0:T(8,128)(2,1)S(1)} %bitcast.32), custom_call_target="tpu_custom_call" | custom-call | tf_op jit(solution)/shard_map/sketch/pallas_call | solution.py:69
  12.3 1.1 collective-permute-done.got
  13.4 3.0 %collective-permute-start.1 = (f32[24,512]{1,0:T(8,128)S(1)}, f32[24,512]{1,0:T(8,128)S(1)}, u32[]{:S(2)}, u32[]{:S(2)}) collective-permute-start(f32[24,512]{1,0:T(8,128)S(1)} %sum_core.1.r0), channel_id=1, source_target_pairs={{2,0},{3,1},{4,2},{5,3},{6,4},{7,5},{0,6},{1,7},{10,8},{11,9},{12,... | collective-permute-start | bytes 147464 | tf_op jit(solution)/shard_map/ppermute | solution.py:42
  18.6 3.5 %collective-permute-done.2.r2 = f32[24,512]{1,0:T(8,128)S(1)} collective-permute-done((f32[24,512]{1,0:T(8,128)S(1)}, f32[24,512]{1,0:T(8,128)S(1)}, u32[]{:S(2)}, u32[]{:S(2)}) %collective-permute-start.2) | collective-permute-done | bytes 49184 | tf_op jit(solution)/shard_map/ppermute | solution.py:42
  22.6 4.1 %collective-permute-start.4 = (f32[24,512]{1,0:T(8,128)S(1)}, f32[24,512]{1,0:T(8,128)S(1)}, u32[]{:S(2)}, u32[]{:S(2)}) collective-permute-start(f32[24,512]{1,0:T(8,128)S(1)} %sum_y.1.r0), channel_id=1, source_target_pairs={{8,0},{9,1},{10,2},{11,3},{12,4},{13,5},{14,6},{15,7},{16,8},{17,9... | collective-permute-start | bytes 147464 | tf_op jit(solution)/shard_map/ppermute | solution.py:42
  26.7 1.3 collective-permute-start.6
  28.4 3.9 %collective-permute-done.5.r2 = f32[24,512]{1,0:T(8,128)S(1)} collective-permute-done((f32[24,512]{1,0:T(8,128)S(1)}, f32[24,512]{1,0:T(8,128)S(1)}, u32[]{:S(2)}, u32[]{:S(2)}) %collective-permute-start.5) | collective-permute-done | bytes 49184 | tf_op jit(solution)/shard_map/ppermute | solution.py:42
  32.6 1.3 collective-permute-done.7.other
  33.9 4.6 %factor.1 = (bf16[144,256]{1,0:T(8,128)(2,1)S(1)}, bf16[128,256]{1,0:T(8,128)(2,1)S(1)}) custom-call(s32[2]{0:T(128)S(1)} %pad_add_fusion.place, f32[48,512]{1,0:T(8,128)S(1)} %sum_z.1.own, f32[48,512]{1,0:T(8,128)S(1)} %collective-permute-done.7.other, bf16[2048,512]{1,0:T(8,128)(2,1)S(1)} %bitcast.29), custom_call_target="tpu_custom_call" | custom-call | tf_op jit(solution)/shard_map/factor/pallas_call | solution.py:158
  38.5 1.5 collective-permute-start.29
  40.0 5.8 %collective-permute-done.29 = bf16[272,256]{1,0:T(8,128)(2,1)S(1)} collective-permute-done((bf16[272,256]{1,0:T(8,128)(2,1)S(1)}, bf16[272,256]{1,0:T(8,128)(2,1)S(1)}, u32[]{:S(2)}, u32[]{:S(2)}) %collective-permute-start.29) | collective-permute-done | bytes 139296 | tf_op jit(solution)/shard_map/ppermute | solution.py:46
  48.4 1.3 collective-permute-start.17
  50.3 1.1 collective-permute-start.10
  51.4 2.1 %collective-permute-done.16 = bf16[128,256]{1,0:T(8,128)(2,1)S(1)} collective-permute-done((bf16[128,256]{1,0:T(8,128)(2,1)S(1)}, bf16[128,256]{1,0:T(8,128)(2,1)S(1)}, u32[]{:S(2)}, u32[]{:S(2)}) %collective-permute-start.16) | collective-permute-done | bytes 65568 | tf_op jit(solution)/shard_map/ppermute | solution.py:42
  54.8 1.1 collective-permute-start.19
  55.9 1.3 collective-permute-start.20
  57.2 1.3 collective-permute-start.11
  58.5 12.9 %collective-permute-done.11 = bf16[144,256]{1,0:T(8,128)(2,1)S(1)} collective-permute-done((bf16[144,256]{1,0:T(8,128)(2,1)S(1)}, bf16[144,256]{1,0:T(8,128)(2,1)S(1)}, u32[]{:S(2)}, u32[]{:S(2)}) %collective-permute-start.11) | collective-permute-done | bytes 73760 | tf_op jit(solution)/shard_map/ppermute | solution.py:42
  71.4 2.3 %collective-permute-start.12 = (bf16[4,144,256]{2,1,0:T(8,128)(2,1)S(1)}, bf16[4,144,256]{2,1,0:T(8,128)(2,1)S(1)}, u32[]{:S(2)}, u32[]{:S(2)}) collective-permute-start(bf16[4,144,256]{2,1,0:T(8,128)(2,1)S(1)} %pad_maximum_fusion.refs_0_), channel_id=1, source_target_pairs={{8,0},{9,1},{10,2},{11,3},{12,4},{13,5},{14,6},{15,7},{16,8},{17,9... | collective-permute-start | bytes 884744 | tf_op jit(solution)/shard_map/ppermute | solution.py:42
  74.7 1.0 collective-permute-start.14
  76.3 9.7 %collective-permute-done.12.refs_1_ = bf16[4,144,256]{2,1,0:T(8,128)(2,1)S(1)} collective-permute-done((bf16[4,144,256]{2,1,0:T(8,128)(2,1)S(1)}, bf16[4,144,256]{2,1,0:T(8,128)(2,1)S(1)}, u32[]{:S(2)}, u32[]{:S(2)}) %collective-permute-start.12) | collective-permute-done | bytes 294944 | tf_op jit(solution)/shard_map/ppermute | solution.py:42
  85.9 2.8 %collective-permute-done.13.refs_2_ = bf16[4,144,256]{2,1,0:T(8,128)(2,1)S(1)} collective-permute-done((bf16[4,144,256]{2,1,0:T(8,128)(2,1)S(1)}, bf16[4,144,256]{2,1,0:T(8,128)(2,1)S(1)}, u32[]{:S(2)}, u32[]{:S(2)}) %collective-permute-start.13) | collective-permute-done | bytes 294944 | tf_op jit(solution)/shard_map/ppermute | solution.py:42
  88.8 7.4 %collective-permute-done.14.refs_3_ = bf16[4,144,256]{2,1,0:T(8,128)(2,1)S(1)} collective-permute-done((bf16[4,144,256]{2,1,0:T(8,128)(2,1)S(1)}, bf16[4,144,256]{2,1,0:T(8,128)(2,1)S(1)}, u32[]{:S(2)}, u32[]{:S(2)}) %collective-permute-start.14) | collective-permute-done | bytes 294944 | tf_op jit(solution)/shard_map/ppermute | solution.py:42
  96.8 14.2 %plan.1 = (s32[1024]{0:T(1024)S(1)}, s32[1024]{0:T(1024)S(1)}, s32[1024]{0:T(1024)S(1)}, s32[1024]{0:T(1024)S(1)}) custom-call(s32[2]{0:T(128)S(1)} %pad_add_fusion.place, f32[48,512]{1,0:T(8,128)S(1)} %sum_z.1.own, f32[48,512]{1,0:T(8,128)S(1)} %collective-permute-done.7.other), custom_call_target="tpu_custom_call" | custom-call | tf_op jit(solution)/shard_map/plan/pallas_call | solution.py:253
  111.0 10.5 %send_pairs.1 = (bf16[8,256,256]{2,1,0:T(8,128)(2,1)}, bf16[8,256,256]{2,1,0:T(8,128)(2,1)S(1)}) custom-call(s32[1024]{0:T(1024)S(1)} %get-tuple-element.21.next_list, s32[1024]{0:T(1024)S(1)} %get-tuple-element.22.last_list, bf16[4,144,256]{2,1,0:T(8,128)(2,1)S(1)} %pad_maximum_fusion.refs_0_, bf16[4,144,256]{2,1,0:T(8,128)(2,1)S(1)} %collective-permute-done.12.refs_1_, ...), custom_call_target="tpu_custom_call" | custom-call | tf_op jit(solution)/shard_map/send_pairs/pallas_call | solution.py:348
  121.6 2.0 %collective-permute-start.31 = (bf16[8,256,256]{2,1,0:T(8,128)(2,1)S(1)}, bf16[8,256,256]{2,1,0:T(8,128)(2,1)}, u32[]{:S(2)}, u32[]{:S(2)}) collective-permute-start(bf16[8,256,256]{2,1,0:T(8,128)(2,1)S(1)} %get-tuple-element.24), channel_id=1, source_target_pairs={{32,0},{64,32},{96,64},{0,96},{33,1},{65,33},{97,65},{1,97},{34,2}... | collective-permute-start | bytes 3145736 | tf_op jit(solution)/shard_map/ppermute | solution.py:46
  123.9 7.9 %own_pairs.1.base = f32[8,256,256]{2,1,0:T(8,128)S(1)} custom-call(s32[1024]{0:T(1024)S(1)} %get-tuple-element.18.own_list, f32[8,256,256]{2,1,0:T(8,128)S(1)} %bitcast.31, bf16[4,144,256]{2,1,0:T(8,128)(2,1)S(1)} %pad_maximum_fusion.refs_0_, bf16[4,144,256]{2,1,0:T(8,128)(2,1)S(1)} %collective-permute-done.12.refs_1_, ...), custom_call_target="tpu_custom_call" | custom-call | tf_op jit(solution)/shard_map/own_pairs/pallas_call | solution.py:371
  131.8 15.9 %collective-permute-done.8.far_list = s32[1024]{0:T(1024)S(1)} collective-permute-done((s32[1024]{0:T(1024)S(1)}, s32[1024]{0:T(1024)S(1)}, u32[]{:S(2)}, u32[]{:S(2)}) %collective-permute-start.8) | collective-permute-done | bytes 4128 | tf_op jit(solution)/shard_map/ppermute | solution.py:46
  147.6 2.3 %copy-done.2 = bf16[8704,256]{1,0:T(8,128)(2,1)S(1)} copy-done((bf16[8704,256]{1,0:T(8,128)(2,1)S(1)}, bf16[8704,256]{1,0:T(8,128)(2,1)}, u32[]{:S(2)}) %copy-start.2) | copy-done | bytes 4456472
  149.9 4.5 %far_pairs.1 = f32[8,256,256]{2,1,0:T(8,128)S(1)} custom-call(s32[1024]{0:T(1024)S(1)} %collective-permute-done.8.far_list, f32[8,256,256]{2,1,0:T(8,128)S(1)} %own_pairs.1.base, bf16[32,272,256]{2,1,0:T(8,128)(2,1)S(1)} %bitcast.30), custom_call_target="tpu_custom_call" | custom-call | tf_op jit(solution)/shard_map/far_pairs/pallas_call | solution.py:394
  154.4 3.2 %subtract_bitcast_fusion = f32[1,8,256,256]{3,2,1,0:T(8,128)} fusion(f32[8,256,256]{2,1,0:T(8,128)S(1)} %far_pairs.1, bf16[8,256,256]{2,1,0:T(8,128)(2,1)} %collective-permute-done.31, bf16[8,256,256]{2,1,0:T(8,128)(2,1)} %collective-permute-done.30), kind=kLoop, calls=%fused_computation | loop fusion | flops 2097152 | bytes 6291456 | tf_op jit(solution)/shard_map/broadcast_in_dim | solution.py:440
  (69 shorter events, 11.6 us)
Async XLA Ops:
  6.5 141.1 %all-gather.2.cloned.1.call-start = ((), (), s32[]{:S(2)}) async-start(), calls=%async_computation | async-start | bytes 4595712 | tf_op jit(solution)/shard_map/all_gather | solution.py:433
  13.4 5.1 %collective-permute-start.1 = (f32[24,512]{1,0:T(8,128)S(1)}, f32[24,512]{1,0:T(8,128)S(1)}, u32[]{:S(2)}, u32[]{:S(2)}) collective-permute-start(f32[24,512]{1,0:T(8,128)S(1)} %sum_core.1.r0), channel_id=1, source_target_pairs={{2,0},{3,1},{4,2},{5,3},{6,4},{7,5},{0,6},{1,7},{10,8},{11,9},{12,... | collective-permute-start | bytes 147464 | tf_op jit(solution)/shard_map/ppermute | solution.py:42
  16.4 5.6 %collective-permute-start.2 = (f32[24,512]{1,0:T(8,128)S(1)}, f32[24,512]{1,0:T(8,128)S(1)}, u32[]{:S(2)}, u32[]{:S(2)}) collective-permute-start(f32[24,512]{1,0:T(8,128)S(1)} %sum_core.1.r0), channel_id=1, source_target_pairs={{4,0},{5,1},{6,2},{7,3},{0,4},{1,5},{2,6},{3,7},{12,8},{13,9},{14,... | collective-permute-start | bytes 147464 | tf_op jit(solution)/shard_map/ppermute | solution.py:42
  17.1 5.5 %collective-permute-start.3 = (f32[24,512]{1,0:T(8,128)S(1)}, f32[24,512]{1,0:T(8,128)S(1)}, u32[]{:S(2)}, u32[]{:S(2)}) collective-permute-start(f32[24,512]{1,0:T(8,128)S(1)} %sum_core.1.r0), channel_id=1, source_target_pairs={{6,0},{7,1},{0,2},{1,3},{2,4},{3,5},{4,6},{5,7},{14,8},{15,9},{8,1... | collective-permute-start | bytes 147464 | tf_op jit(solution)/shard_map/ppermute | solution.py:42
  22.6 5.9 %collective-permute-start.4 = (f32[24,512]{1,0:T(8,128)S(1)}, f32[24,512]{1,0:T(8,128)S(1)}, u32[]{:S(2)}, u32[]{:S(2)}) collective-permute-start(f32[24,512]{1,0:T(8,128)S(1)} %sum_y.1.r0), channel_id=1, source_target_pairs={{8,0},{9,1},{10,2},{11,3},{12,4},{13,5},{14,6},{15,7},{16,8},{17,9... | collective-permute-start | bytes 147464 | tf_op jit(solution)/shard_map/ppermute | solution.py:42
  26.7 5.7 %collective-permute-start.5 = (f32[24,512]{1,0:T(8,128)S(1)}, f32[24,512]{1,0:T(8,128)S(1)}, u32[]{:S(2)}, u32[]{:S(2)}) collective-permute-start(f32[24,512]{1,0:T(8,128)S(1)} %sum_y.1.r0), channel_id=1, source_target_pairs={{16,0},{17,1},{18,2},{19,3},{20,4},{21,5},{22,6},{23,7},{24,8},{25... | collective-permute-start | bytes 147464 | tf_op jit(solution)/shard_map/ppermute | solution.py:42
  26.7 5.8 %collective-permute-start.6 = (f32[24,512]{1,0:T(8,128)S(1)}, f32[24,512]{1,0:T(8,128)S(1)}, u32[]{:S(2)}, u32[]{:S(2)}) collective-permute-start(f32[24,512]{1,0:T(8,128)S(1)} %sum_y.1.r0), channel_id=1, source_target_pairs={{24,0},{25,1},{26,2},{27,3},{28,4},{29,5},{30,6},{31,7},{0,8},{1,9... | collective-permute-start | bytes 147464 | tf_op jit(solution)/shard_map/ppermute | solution.py:42
  32.5 1.4 collective-permute-start.7
  38.5 7.3 %collective-permute-start.29 = (bf16[272,256]{1,0:T(8,128)(2,1)S(1)}, bf16[272,256]{1,0:T(8,128)(2,1)S(1)}, u32[]{:S(2)}, u32[]{:S(2)}) collective-permute-start(bf16[272,256]{1,0:T(8,128)(2,1)S(1)} %pad_maximum_fusion.2), channel_id=1, source_target_pairs={{64,0},{96,32},{0,64},{32,96},{65,1},{97,33},{1,65},{33,97},{66,2}... | collective-permute-start | bytes 417800 | tf_op jit(solution)/shard_map/ppermute | solution.py:46
  46.5 4.9 %collective-permute-start.15 = (bf16[128,256]{1,0:T(8,128)(2,1)S(1)}, bf16[128,256]{1,0:T(8,128)(2,1)S(1)}, u32[]{:S(2)}, u32[]{:S(2)}) collective-permute-start(bf16[128,256]{1,0:T(8,128)(2,1)S(1)} %get-tuple-element.20), channel_id=1, source_target_pairs={{8,0},{9,1},{10,2},{11,3},{12,4},{13,5},{14,6},{15,7},{16,8},{17,9... | collective-permute-start | bytes 196616 | tf_op jit(solution)/shard_map/ppermute | solution.py:42
  47.4 6.1 %collective-permute-start.16 = (bf16[128,256]{1,0:T(8,128)(2,1)S(1)}, bf16[128,256]{1,0:T(8,128)(2,1)S(1)}, u32[]{:S(2)}, u32[]{:S(2)}) collective-permute-start(bf16[128,256]{1,0:T(8,128)(2,1)S(1)} %get-tuple-element.20), channel_id=1, source_target_pairs={{16,0},{17,1},{18,2},{19,3},{20,4},{21,5},{22,6},{23,7},{24,8},{25... | collective-permute-start | bytes 196616 | tf_op jit(solution)/shard_map/ppermute | solution.py:42
  48.4 5.7 %collective-permute-start.17 = (bf16[128,256]{1,0:T(8,128)(2,1)S(1)}, bf16[128,256]{1,0:T(8,128)(2,1)S(1)}, u32[]{:S(2)}, u32[]{:S(2)}) collective-permute-start(bf16[128,256]{1,0:T(8,128)(2,1)S(1)} %get-tuple-element.20), channel_id=1, source_target_pairs={{24,0},{25,1},{26,2},{27,3},{28,4},{29,5},{30,6},{31,7},{0,8},{1,9... | collective-permute-start | bytes 196616 | tf_op jit(solution)/shard_map/ppermute | solution.py:42
  49.8 7.4 %collective-permute-start.9 = (bf16[144,256]{1,0:T(8,128)(2,1)S(1)}, bf16[144,256]{1,0:T(8,128)(2,1)S(1)}, u32[]{:S(2)}, u32[]{:S(2)}) collective-permute-start(bf16[144,256]{1,0:T(8,128)(2,1)S(1)} %get-tuple-element.19), channel_id=1, source_target_pairs={{2,0},{3,1},{4,2},{5,3},{6,4},{7,5},{0,6},{1,7},{10,8},{11,9},{12,... | collective-permute-start | bytes 221192 | tf_op jit(solution)/shard_map/ppermute | solution.py:42
  50.3 6.9 %collective-permute-start.10 = (bf16[144,256]{1,0:T(8,128)(2,1)S(1)}, bf16[144,256]{1,0:T(8,128)(2,1)S(1)}, u32[]{:S(2)}, u32[]{:S(2)}) collective-permute-start(bf16[144,256]{1,0:T(8,128)(2,1)S(1)} %get-tuple-element.19), channel_id=1, source_target_pairs={{4,0},{5,1},{6,2},{7,3},{0,4},{1,5},{2,6},{3,7},{12,8},{13,9},{14,... | collective-permute-start | bytes 221192 | tf_op jit(solution)/shard_map/ppermute | solution.py:42
  54.2 19.5 %collective-permute-start.18 = (bf16[4,128,256]{2,1,0:T(8,128)(2,1)S(1)}, bf16[4,128,256]{2,1,0:T(8,128)(2,1)S(1)}, u32[]{:S(2)}, u32[]{:S(2)}) collective-permute-start(bf16[4,128,256]{2,1,0:T(8,128)(2,1)S(1)} %pad_maximum_fusion.1.refs_4_), channel_id=1, source_target_pairs={{2,0},{3,1},{4,2},{5,3},{6,4},{7,5},{0,6},{1,7},{10,8},{11,9},{12,... | collective-permute-start | bytes 786440 | tf_op jit(solution)/shard_map/ppermute | solution.py:42
  54.8 19.9 %collective-permute-start.19 = (bf16[4,128,256]{2,1,0:T(8,128)(2,1)S(1)}, bf16[4,128,256]{2,1,0:T(8,128)(2,1)S(1)}, u32[]{:S(2)}, u32[]{:S(2)}) collective-permute-start(bf16[4,128,256]{2,1,0:T(8,128)(2,1)S(1)} %pad_maximum_fusion.1.refs_4_), channel_id=1, source_target_pairs={{4,0},{5,1},{6,2},{7,3},{0,4},{1,5},{2,6},{3,7},{12,8},{13,9},{14,... | collective-permute-start | bytes 786440 | tf_op jit(solution)/shard_map/ppermute | solution.py:42
  55.9 19.8 %collective-permute-start.20 = (bf16[4,128,256]{2,1,0:T(8,128)(2,1)S(1)}, bf16[4,128,256]{2,1,0:T(8,128)(2,1)S(1)}, u32[]{:S(2)}, u32[]{:S(2)}) collective-permute-start(bf16[4,128,256]{2,1,0:T(8,128)(2,1)S(1)} %pad_maximum_fusion.1.refs_4_), channel_id=1, source_target_pairs={{6,0},{7,1},{0,2},{1,3},{2,4},{3,5},{4,6},{5,7},{14,8},{15,9},{8,1... | collective-permute-start | bytes 786440 | tf_op jit(solution)/shard_map/ppermute | solution.py:42
  57.2 18.6 %collective-permute-start.25 = (bf16[4,128,256]{2,1,0:T(8,128)(2,1)S(1)}, bf16[4,128,256]{2,1,0:T(8,128)(2,1)S(1)}, u32[]{:S(2)}, u32[]{:S(2)}) collective-permute-start(bf16[4,128,256]{2,1,0:T(8,128)(2,1)S(1)} %pad_maximum_fusion.1.refs_4_), channel_id=1, source_target_pairs={{1,0},{0,1},{3,2},{2,3},{5,4},{4,5},{7,6},{6,7},{9,8},{8,9},{11,10... | collective-permute-start | bytes 786440 | tf_op jit(solution)/shard_map/ppermute | solution.py:42
  57.2 14.2 %collective-permute-start.11 = (bf16[144,256]{1,0:T(8,128)(2,1)S(1)}, bf16[144,256]{1,0:T(8,128)(2,1)S(1)}, u32[]{:S(2)}, u32[]{:S(2)}) collective-permute-start(bf16[144,256]{1,0:T(8,128)(2,1)S(1)} %get-tuple-element.19), channel_id=1, source_target_pairs={{6,0},{7,1},{0,2},{1,3},{2,4},{3,5},{4,6},{5,7},{14,8},{15,9},{8,1... | collective-permute-start | bytes 221192 | tf_op jit(solution)/shard_map/ppermute | solution.py:42
  71.4 14.5 %collective-permute-start.12 = (bf16[4,144,256]{2,1,0:T(8,128)(2,1)S(1)}, bf16[4,144,256]{2,1,0:T(8,128)(2,1)S(1)}, u32[]{:S(2)}, u32[]{:S(2)}) collective-permute-start(bf16[4,144,256]{2,1,0:T(8,128)(2,1)S(1)} %pad_maximum_fusion.refs_0_), channel_id=1, source_target_pairs={{8,0},{9,1},{10,2},{11,3},{12,4},{13,5},{14,6},{15,7},{16,8},{17,9... | collective-permute-start | bytes 884744 | tf_op jit(solution)/shard_map/ppermute | solution.py:42
  73.7 15.1 %collective-permute-start.13 = (bf16[4,144,256]{2,1,0:T(8,128)(2,1)S(1)}, bf16[4,144,256]{2,1,0:T(8,128)(2,1)S(1)}, u32[]{:S(2)}, u32[]{:S(2)}) collective-permute-start(bf16[4,144,256]{2,1,0:T(8,128)(2,1)S(1)} %pad_maximum_fusion.refs_0_), channel_id=1, source_target_pairs={{16,0},{17,1},{18,2},{19,3},{20,4},{21,5},{22,6},{23,7},{24,8},{25... | collective-permute-start | bytes 884744 | tf_op jit(solution)/shard_map/ppermute | solution.py:42
  74.7 21.5 %collective-permute-start.14 = (bf16[4,144,256]{2,1,0:T(8,128)(2,1)S(1)}, bf16[4,144,256]{2,1,0:T(8,128)(2,1)S(1)}, u32[]{:S(2)}, u32[]{:S(2)}) collective-permute-start(bf16[4,144,256]{2,1,0:T(8,128)(2,1)S(1)} %pad_maximum_fusion.refs_0_), channel_id=1, source_target_pairs={{24,0},{25,1},{26,2},{27,3},{28,4},{29,5},{30,6},{31,7},{0,8},{1,9... | collective-permute-start | bytes 884744 | tf_op jit(solution)/shard_map/ppermute | solution.py:42
  75.7 20.4 %collective-permute-start.21 = (bf16[4,144,256]{2,1,0:T(8,128)(2,1)S(1)}, bf16[4,144,256]{2,1,0:T(8,128)(2,1)S(1)}, u32[]{:S(2)}, u32[]{:S(2)}) collective-permute-start(bf16[4,144,256]{2,1,0:T(8,128)(2,1)S(1)} %pad_maximum_fusion.refs_0_), channel_id=1, source_target_pairs={{1,0},{0,1},{3,2},{2,3},{5,4},{4,5},{7,6},{6,7},{9,8},{8,9},{11,10... | collective-permute-start | bytes 884744 | tf_op jit(solution)/shard_map/ppermute | solution.py:42
  75.7 20.9 %collective-permute-start.26 = (bf16[4,128,256]{2,1,0:T(8,128)(2,1)S(1)}, bf16[4,128,256]{2,1,0:T(8,128)(2,1)S(1)}, u32[]{:S(2)}, u32[]{:S(2)}) collective-permute-start(bf16[4,128,256]{2,1,0:T(8,128)(2,1)S(1)} %collective-permute-done.18.refs_5_), channel_id=1, source_target_pairs={{1,0},{0,1},{3,2},{2,3},{5,4},{4,5},{7,6},{6,7},{9,8},{8,9},{11,10... | collective-permute-start | bytes 786440 | tf_op jit(solution)/shard_map/ppermute | solution.py:42
  85.9 25.0 %collective-permute-start.22 = (bf16[4,144,256]{2,1,0:T(8,128)(2,1)S(1)}, bf16[4,144,256]{2,1,0:T(8,128)(2,1)S(1)}, u32[]{:S(2)}, u32[]{:S(2)}) collective-permute-start(bf16[4,144,256]{2,1,0:T(8,128)(2,1)S(1)} %collective-permute-done.12.refs_1_), channel_id=1, source_target_pairs={{1,0},{0,1},{3,2},{2,3},{5,4},{4,5},{7,6},{6,7},{9,8},{8,9},{11,10... | collective-permute-start | bytes 884744 | tf_op jit(solution)/shard_map/ppermute | solution.py:42
  88.8 22.2 %collective-permute-start.23 = (bf16[4,144,256]{2,1,0:T(8,128)(2,1)S(1)}, bf16[4,144,256]{2,1,0:T(8,128)(2,1)S(1)}, u32[]{:S(2)}, u32[]{:S(2)}) collective-permute-start(bf16[4,144,256]{2,1,0:T(8,128)(2,1)S(1)} %collective-permute-done.13.refs_2_), channel_id=1, source_target_pairs={{1,0},{0,1},{3,2},{2,3},{5,4},{4,5},{7,6},{6,7},{9,8},{8,9},{11,10... | collective-permute-start | bytes 884744 | tf_op jit(solution)/shard_map/ppermute | solution.py:42
  96.2 14.8 %collective-permute-start.24 = (bf16[4,144,256]{2,1,0:T(8,128)(2,1)S(1)}, bf16[4,144,256]{2,1,0:T(8,128)(2,1)S(1)}, u32[]{:S(2)}, u32[]{:S(2)}) collective-permute-start(bf16[4,144,256]{2,1,0:T(8,128)(2,1)S(1)} %collective-permute-done.14.refs_3_), channel_id=1, source_target_pairs={{1,0},{0,1},{3,2},{2,3},{5,4},{4,5},{7,6},{6,7},{9,8},{8,9},{11,10... | collective-permute-start | bytes 884744 | tf_op jit(solution)/shard_map/ppermute | solution.py:42
  96.2 14.8 %collective-permute-start.27 = (bf16[4,128,256]{2,1,0:T(8,128)(2,1)S(1)}, bf16[4,128,256]{2,1,0:T(8,128)(2,1)S(1)}, u32[]{:S(2)}, u32[]{:S(2)}) collective-permute-start(bf16[4,128,256]{2,1,0:T(8,128)(2,1)S(1)} %collective-permute-done.19.refs_6_), channel_id=1, source_target_pairs={{1,0},{0,1},{3,2},{2,3},{5,4},{4,5},{7,6},{6,7},{9,8},{8,9},{11,10... | collective-permute-start | bytes 786440 | tf_op jit(solution)/shard_map/ppermute | solution.py:42
  96.7 14.3 %collective-permute-start.28 = (bf16[4,128,256]{2,1,0:T(8,128)(2,1)S(1)}, bf16[4,128,256]{2,1,0:T(8,128)(2,1)S(1)}, u32[]{:S(2)}, u32[]{:S(2)}) collective-permute-start(bf16[4,128,256]{2,1,0:T(8,128)(2,1)S(1)} %collective-permute-done.20.refs_7_), channel_id=1, source_target_pairs={{1,0},{0,1},{3,2},{2,3},{5,4},{4,5},{7,6},{6,7},{9,8},{8,9},{11,10... | collective-permute-start | bytes 786440 | tf_op jit(solution)/shard_map/ppermute | solution.py:42
  121.5 32.9 %collective-permute-start.30 = (bf16[8,256,256]{2,1,0:T(8,128)(2,1)}, bf16[8,256,256]{2,1,0:T(8,128)(2,1)}, u32[]{:S(2)}, u32[]{:S(2)}) collective-permute-start(bf16[8,256,256]{2,1,0:T(8,128)(2,1)} %get-tuple-element.23), channel_id=1, source_target_pairs={{96,0},{0,32},{32,64},{64,96},{97,1},{1,33},{33,65},{65,97},{98,2}... | collective-permute-start | bytes 3145736 | tf_op jit(solution)/shard_map/ppermute | solution.py:46
  121.6 32.8 %collective-permute-start.31 = (bf16[8,256,256]{2,1,0:T(8,128)(2,1)S(1)}, bf16[8,256,256]{2,1,0:T(8,128)(2,1)}, u32[]{:S(2)}, u32[]{:S(2)}) collective-permute-start(bf16[8,256,256]{2,1,0:T(8,128)(2,1)S(1)} %get-tuple-element.24), channel_id=1, source_target_pairs={{32,0},{64,32},{96,64},{0,96},{33,1},{65,33},{97,65},{1,97},{34,2}... | collective-permute-start | bytes 3145736 | tf_op jit(solution)/shard_map/ppermute | solution.py:46
  123.6 24.0 %collective-permute-start.8 = (s32[1024]{0:T(1024)S(1)}, s32[1024]{0:T(1024)S(1)}, u32[]{:S(2)}, u32[]{:S(2)}) collective-permute-start(s32[1024]{0:T(1024)S(1)} %get-tuple-element.17), channel_id=1, source_target_pairs={{64,0},{96,32},{0,64},{32,96},{65,1},{97,33},{1,65},{33,97},{66,2}... | collective-permute-start | bytes 12296 | tf_op jit(solution)/shard_map/ppermute | solution.py:46
  (10 other events, 66.2 us)
Sparse Core Ops, SparseCore 0:
  46.6 53.8 all-gather.1

commit v2 on v1

v2 whole, which is shorter than its diff:
```python
import jax
import jax.numpy as jnp
from jax import lax
from jax.experimental import pallas as pl
from jax.experimental.pallas import tpu as pltpu
from jax.sharding import PartitionSpec as P

W = 512
RANK = 32
BLOCK = 256
NB_DEV = 8
NT_DEV = 8
N_SET = 4
N_CAND = 32
HALF = RANK // 2
ROWS = NB_DEV * BLOCK
MSG = NB_DEV * RANK + 16
SLOTS = 2
PER_CHUNK = 8
ENTRIES = N_CAND * SLOTS
ZERO = NB_DEV * N_CAND
LAST_US = 10
f32, bf16, i32 = jnp.float32, jnp.bfloat16, jnp.int32
VMEM = pl.BlockSpec(memory_space=pltpu.VMEM)
SMEM = pl.BlockSpec(memory_space=pltpu.SMEM)
ANY = pl.BlockSpec(memory_space=pl.ANY)
NT = (((1,), (1,)), ((), ()))
TN = (((0,), (0,)), ((), ()))


def params(mib=40):
    return pltpu.CompilerParams(vmem_limit_bytes=mib * 1024 * 1024)


def from_cand(x, leg, k, far=False):
    pairs = []
    for me in range(N_CAND):
        z, y, core = me // 8, (me // 2) % 4, me % 2
        if leg == core:
            y = (y + k) % 4
        else:
            z = (z + k) % 4
        pairs.append((z * 8 + y * 2 + core, me))
    if not far:
        return lax.ppermute(x, "cand", pairs)
    pairs = [
        ((me_set + 2) % N_SET * N_CAND + source, me_set * N_CAND + me)
        for me_set in range(N_SET)
        for source, me in pairs
    ]
    return lax.ppermute(x, ("set", "cand"), pairs)


def from_core(x):
    return lax.ppermute(x, "cand", [(me ^ 1, me) for me in range(N_CAND)])


def from_set(x, d):
    return lax.ppermute(x, "set", [((me + d) % N_SET, me) for me in range(N_SET)])


def sketch_kernel(place, rows, sketch, keep, give, total):
    step = pl.program_id(0)

    @pl.when(step == 0)
    def _():
        total[...] = jnp.zeros_like(total)

    sketched = lax.dot_general(sketch[...], rows[...], NT, preferred_element_type=f32)
    total[...] += jnp.dot(sketched.astype(bf16), rows[...], preferred_element_type=f32)

    @pl.when(step == pl.num_programs(0) - 1)
    def _():
        core = place[1] % 2
        keep[...] = total[pl.ds(pl.multiple_of(core * HALF, HALF), HALF), :]
        give[...] = total[pl.ds(pl.multiple_of((1 - core) * HALF, HALF), HALF), :]


def sketch_call(place, rows, sketch):
    step = 512
    half = jax.ShapeDtypeStruct((HALF, W), f32)
    return pl.pallas_call(
        sketch_kernel,
        grid=(ROWS // step,),
        out_shape=(half, half),
        in_specs=[
            SMEM,
            pl.BlockSpec((step, W), lambda i: (i, 0)),
            pl.BlockSpec((RANK, W), lambda i: (0, 0)),
        ],
        out_specs=(pl.BlockSpec((HALF, W), lambda i: (0, 0)),) * 2,
        scratch_shapes=[pltpu.VMEM((RANK, W), f32)],
        compiler_params=params(62),
        name="sketch",
    )(place, rows, sketch)


def sum_core_kernel(keep, got, slots, out):
    out[0:HALF, :] = keep[...] + got[...]
    out[HALF:, :] = jnp.zeros((8, W), f32)
    out[HALF:, 0:128] = slots[...]


def sum_first_kernel(r0, r1, r2, r3, out):
    out[0:HALF, :] = (r0[0:HALF, :] + r2[0:HALF, :]) + (r1[0:HALF, :] + r3[0:HALF, :])
    for k, r in enumerate((r0, r1, r2, r3)):
        out[HALF:, k * 128 : (k + 1) * 128] = r[HALF:, 0:128]


def sum_second_kernel(r0, r1, r2, r3, out):
    out[0:HALF, :] = (r0[0:HALF, :] + r2[0:HALF, :]) + (r1[0:HALF, :] + r3[0:HALF, :])
    for k, r in enumerate((r0, r1, r2, r3)):
        out[HALF + 8 * k : HALF + 8 * (k + 1), :] = r[HALF:, :]


def small_call(kernel, rows, name, *args):
    return pl.pallas_call(
        kernel,
        out_shape=jax.ShapeDtypeStruct((rows, W), f32),
        in_specs=[VMEM] * len(args),
        out_specs=VMEM,
        compiler_params=params(),
        name=name,
    )(*args)


def factor_kernel(place, own, other, rows_hbm, out, rows, sem):
    copy = pltpu.make_async_copy(rows_hbm, rows, sem)
    copy.start()
    first = place[1] % 2 == 0
    mine, theirs = own[0:HALF, :], other[0:HALF, :]
    summed = jnp.concatenate(
        [jnp.where(first, mine, theirs), jnp.where(first, theirs, mine)], axis=0
    )
    padded = jnp.concatenate([summed, jnp.zeros((96, W), f32)], axis=0)
    gram = lax.dot_general(
        summed, padded, NT, precision=lax.Precision.HIGHEST, preferred_element_type=f32
    )
    lane = lax.broadcasted_iota(i32, (RANK, 128), 1)
    line = lax.broadcasted_iota(i32, (RANK, 128), 0)
    work = gram + jnp.where(lane == line + RANK, 1.0, 0.0)
    for k in range(RANK - 1):
        column = jnp.broadcast_to(work[:, k : k + 1], (RANK, 128))
        pivot_row = work[k : k + 1, :] / column[k : k + 1, :]
        work = work - jnp.where(line > k, column, 0.0) * pivot_row
    pivots = jnp.sum(jnp.where(lane == line, work, 0.0), axis=1, keepdims=True)
    inverse = work * lax.rsqrt(pivots)
    shifted = jnp.concatenate([jnp.zeros((32, W), f32), summed, jnp.zeros((64, W), f32)], axis=0)
    basis = jnp.dot(
        inverse, shifted, precision=lax.Precision.HIGHEST, preferred_element_type=f32
    ).astype(bf16)
    copy.wait()
    index = lax.broadcasted_iota(i32, (16, BLOCK), 0)
    scales = jnp.zeros((16, BLOCK), f32)
    for b in range(NB_DEV):
        projected = lax.dot_general(
            basis, rows[b * BLOCK : (b + 1) * BLOCK, :], NT, preferred_element_type=f32
        )
        most = jnp.max(jnp.max(jnp.abs(projected), axis=0, keepdims=True), axis=1, keepdims=True)
        scale = (most + 1e-06).astype(bf16).astype(f32)
        factor = (projected / scale).astype(bf16)
        scales = jnp.where(index == b, scale, scales)
        out[b * RANK : (b + 1) * RANK, :] = factor
    out[NB_DEV * RANK :, :] = scales.astype(bf16)


def factor_call(place, own, other, rows):
    return pl.pallas_call(
        factor_kernel,
        out_shape=jax.ShapeDtypeStruct((MSG, BLOCK), bf16),
        in_specs=[SMEM, VMEM, VMEM, ANY],
        out_specs=VMEM,
        scratch_shapes=[pltpu.VMEM((ROWS, W), bf16), pltpu.SemaphoreType.DMA],
        compiler_params=params(),
        name="factor",
    )(place, own, other, rows)


def touch_call(x, us, *after):
    return pl.pallas_call(
        lambda *refs: None,
        out_shape=jax.ShapeDtypeStruct(x.shape, x.dtype),
        in_specs=[ANY] * (1 + len(after)),
        out_specs=ANY,
        input_output_aliases={0: 0},
        compiler_params=params(),
        cost_estimate=pl.CostEstimate(
            flops=0, bytes_accessed=int(us * 3.0e6), transcendentals=0
        ),
        name="touch",
    )(x, *after)


def join_kernel(*refs):
    parts, out, sems = refs[:4], refs[-2], refs[-1]
    copies = [pltpu.make_async_copy(parts[k], out.at[k], sems.at[k]) for k in range(4)]
    for copy in copies:
        copy.start()
    for copy in copies:
        copy.wait()


def join_call(parts, *after):
    return pl.pallas_call(
        join_kernel,
        out_shape=jax.ShapeDtypeStruct((4, MSG, BLOCK), bf16),
        in_specs=[ANY] * (4 + len(after)),
        out_specs=ANY,
        scratch_shapes=[pltpu.SemaphoreType.DMA((4,))],
        compiler_params=params(),
        name="join",
    )(*parts, *after)


def plan_kernel(place, own, other, *refs):
    outs, gathered = refs[:N_SET], refs[N_SET]
    me_set, me = place[0], place[1]
    me_z, me_y, me_core = me // 8, (me // 2) % 4, me % 2
    for core, r in enumerate((own, other)):
        for second in range(4):
            for first in range(4):
                s = (core * 4 + second) * 4 + first
                gathered[s * 8 : (s + 1) * 8, :] = r[
                    HALF + 8 * second : HALF + 8 * (second + 1), first * 128 : (first + 1) * 128
                ]
    fields = jnp.concatenate(
        [gathered[pl.ds(n, N_CAND, stride=8), :] for n in range(8)], axis=0
    ).astype(bf16)
    line = lax.broadcasted_iota(i32, (16, 128), 0)
    lane = lax.broadcasted_iota(i32, (16, 128), 1)
    wanted = ((me_set + line) % N_SET) * N_CAND + me
    hot = jnp.where((lane == wanted) & (line < N_SET), 1.0, 0.0).astype(bf16)
    across = lax.dot_general(hot, fields, NT, preferred_element_type=f32)
    down = lax.dot_general(fields, hot, NT, preferred_element_type=f32)
    n = ENTRIES
    sender = lax.broadcasted_iota(i32, (16, n), 1) % N_CAND
    left = across[:, 0:n] + (sender * NB_DEV - ZERO).astype(f32)
    block = across[:, n : 2 * n].astype(i32)
    owner = block // NB_DEV
    z, y, core = owner // 8, (owner // 2) % 4, owner % 2
    z, y = (z - me_z + 4) % 4, (y - me_y + 4) % 4
    at = jnp.where(core == 0, z * 4 + y, y * 4 + z) + ((core + me_core) % 2) * 16
    right = (at * NB_DEV + block % NB_DEV).astype(f32)
    target = jnp.where(across[:, 3 * n :] != 0, across[:, 2 * n : 3 * n], NT_DEV)
    target_down = jnp.where(down[3 * n :, :] != 0, down[2 * n : 3 * n, :], NT_DEV)
    before = lax.broadcasted_iota(i32, (n, n), 1) < lax.broadcasted_iota(i32, (n, n), 0)
    spots = lax.broadcasted_iota(i32, (n, 128), 1).astype(f32)
    spot = lax.broadcasted_iota(i32, (1, 128), 1)
    line = lax.broadcasted_iota(i32, (8, 128), 0)
    row = lax.broadcasted_iota(i32, (16, n), 0)
    for gr in range(N_SET):
        t_down, t_across = target_down[:, gr : gr + 1], target[gr : gr + 1, :]
        rank = jnp.sum(
            jnp.where((t_down == t_across) & before, 1.0, 0.0), axis=1, keepdims=True
        )
        count = jnp.sum(jnp.where(t_down == spots, 1.0, 0.0), axis=0, keepdims=True)
        chunks = (count.astype(i32) + (PER_CHUNK - 1)) // PER_CHUNK
        chunks = jnp.where(spot < NT_DEV, chunks, 0).astype(f32)
        start = jnp.sum(jnp.where(spots < t_down, chunks, 0.0), axis=1, keepdims=True)
        place_of = jnp.where(t_down < NT_DEV, start * PER_CHUNK + rank, 1000.0)
        chosen = jnp.where(place_of == spots, 1.0, 0.0).astype(bf16)
        both = jnp.where(
            row == 0, left[gr : gr + 1, :], jnp.where(row == 1, right[gr : gr + 1, :], 0.0)
        ).astype(bf16)
        lists = jnp.dot(both, chosen, preferred_element_type=f32)[0:8, :]
        lists = jnp.where(line == 0, lists + ZERO, jnp.where(line == 2, chunks, lists))
        outs[gr][...] = lists.astype(i32)


def plan_call(place, own, other, *after):
    return pl.pallas_call(
        lambda *refs: plan_kernel(*refs[:3], *refs[3 + len(after) :]),
        out_shape=(jax.ShapeDtypeStruct((8, 128), i32),) * N_SET,
        in_specs=[SMEM, VMEM, VMEM] + [ANY] * len(after),
        out_specs=(VMEM,) * N_SET,
        scratch_shapes=[pltpu.VMEM((N_CAND * 8, 128), f32)],
        compiler_params=params(),
        name="plan",
    )(place, own, other, *after)


def collect(pieces, factors, scales, sems):
    copies = [
        pltpu.make_async_copy(piece, factors.at[pl.ds(4 * n, 4)], sems.at[n])
        for n, piece in enumerate(pieces)
    ]
    for copy in copies:
        copy.start()
    for copy in copies:
        copy.wait()
    for p in range(N_CAND):
        scales[p * NB_DEV : (p + 1) * NB_DEV, :] = factors[p, NB_DEV * RANK :, 0:128].astype(f32)[
            0:NB_DEV, :
        ]
    scales[ZERO : ZERO + 8, :] = jnp.zeros((8, 128), f32)


def block_at(factors, b):
    at = pl.multiple_of((b % NB_DEV) * RANK, RANK)
    return factors.at[(b // NB_DEV) % N_CAND, pl.ds(at, RANK), :]


def expand(pairs, t, factors, scales, lefts, rights, start, total):
    def chunk(q, carry):
        for k in range(PER_CHUNK):
            spot = start + q * PER_CHUNK + k
            left, right = pairs[0, spot], pairs[1, spot]
            weight = scales[pl.ds(left, 1), :] * scales[pl.ds(right, 1), :]
            weight = weight.astype(bf16).astype(f32)
            weight = jnp.concatenate([weight, weight], axis=1)
            here = slice(k * RANK, (k + 1) * RANK)
            lefts[here, :] = (block_at(factors, left)[...].astype(f32) * weight).astype(bf16)
            rights[here, :] = block_at(factors, right)[...]
        total[...] += lax.dot_general(lefts[...], rights[...], TN, preferred_element_type=f32)
        return carry

    total[...] = jnp.zeros_like(total)
    chunks = pairs[2, t]
    lax.fori_loop(0, chunks, chunk, 0)
    return start + chunks * PER_CHUNK


WORK = [
    pltpu.VMEM((N_CAND, MSG, BLOCK), bf16),
    pltpu.VMEM((ZERO + 8, 128), f32),
    pltpu.VMEM((RANK * PER_CHUNK, BLOCK), bf16),
    pltpu.VMEM((RANK * PER_CHUNK, BLOCK), bf16),
    pltpu.VMEM((BLOCK, BLOCK), f32),
    pltpu.SemaphoreType.DMA((8,)),
]


def send_call(next_list, last_list, pieces, cuts):
    n = len(cuts) - 1

    def kernel(next_list, last_list, *refs):
        pieces, outs, work = refs[:8], refs[8 : 8 + 2 * n], refs[8 + 2 * n :]
        factors, scales, lefts, rights, total, sems = work
        collect(pieces, factors, scales, sems)
        for side, pairs in enumerate((next_list, last_list)):
            start = 0
            for t in range(cuts[0]):
                start = start + pairs[2, t] * PER_CHUNK
            for part in range(n):
                for t in range(cuts[part], cuts[part + 1]):
                    start = expand(pairs, t, factors, scales, lefts, rights, start, total)
                    outs[2 * part + side][t - cuts[part]] = total[...].astype(bf16)

    shapes = [
        jax.ShapeDtypeStruct((cuts[part + 1] - cuts[part], BLOCK, BLOCK), bf16)
        for part in range(n)
        for side in range(2)
    ]
    return pl.pallas_call(
        kernel,
        out_shape=shapes,
        in_specs=[SMEM, SMEM] + [ANY] * 8,
        out_specs=[VMEM] * (2 * n),
        scratch_shapes=WORK,
        compiler_params=params(),
        name="send_pairs",
    )(next_list, last_list, *pieces)


def keep_call(pairs, base, pieces, *after):
    def kernel(pairs, base, *refs):
        pieces, (out, *work) = refs[:8], refs[8 + len(after) :]
        factors, scales, lefts, rights, total, sems = work
        collect(pieces, factors, scales, sems)
        start = 0
        for t in range(NT_DEV):
            start = expand(pairs, t, factors, scales, lefts, rights, start, total)
            out[t] = base[t] - total[...]

    return pl.pallas_call(
        kernel,
        out_shape=jax.ShapeDtypeStruct((NT_DEV, BLOCK, BLOCK), f32),
        in_specs=[SMEM, VMEM] + [ANY] * (8 + len(after)),
        out_specs=VMEM,
        scratch_shapes=WORK,
        compiler_params=params(),
        name="keep_pairs",
    )(pairs, base, *pieces, *after)


def final_call(base, parts, cuts):
    def kernel(base, *refs):
        parts, out, sems = refs[: len(parts_in)], refs[-2], refs[-1]
        copies = []
        for n in range(len(cuts) - 1):
            one, two = parts[2 * n], parts[2 * n + 1]
            for t in range(cuts[n], cuts[n + 1]):
                k = t - cuts[n]
                base[t] = base[t] - (one[k].astype(f32) + two[k].astype(f32))
                copy = pltpu.make_async_copy(base.at[t], out.at[t], sems.at[t])
                copy.start()
                copies.append(copy)
        for copy in copies:
            copy.wait()

    parts_in = parts
    return pl.pallas_call(
        kernel,
        out_shape=jax.ShapeDtypeStruct((NT_DEV, BLOCK, BLOCK), f32),
        in_specs=[VMEM] * (1 + len(parts)),
        out_specs=ANY,
        scratch_shapes=[pltpu.SemaphoreType.DMA((NT_DEV,))],
        compiler_params=params(),
        name="final",
    )(base, *parts)


def per_device(panel_rows, sketch, accumulator, left_block, right_block, target_slot, slot_valid):
    rows = panel_rows[0]
    place = jnp.stack([lax.axis_index("set"), lax.axis_index("cand")]).astype(i32)

    keep, give = sketch_call(place, rows, sketch[0].T)
    got = from_core(give)
    slots = jnp.concatenate(
        [x[0, 0].T for x in (left_block, right_block, target_slot, slot_valid)], axis=0
    ).astype(f32)
    part = small_call(sum_core_kernel, HALF + 8, "sum_core", keep, got, slots)
    part = small_call(
        sum_first_kernel, HALF + 8, "sum_first", part, *[from_cand(part, 0, k) for k in (1, 2, 3)]
    )
    own = small_call(
        sum_second_kernel, HALF + 32, "sum_second", part, *[from_cand(part, 1, k) for k in (1, 2, 3)]
    )
    other = from_core(own)

    mine = factor_call(place, own, other, rows)
    line = join_call([mine] + [from_cand(mine, 0, k) for k in (1, 2, 3)])
    here = [line] + [from_cand(line, 1, k) for k in (1, 2, 3)]
    pieces = here + [from_core(x) for x in here]

    far_line = join_call([from_cand(mine, 0, k, far=True) for k in range(4)])
    own_list, next_list, far_list, last_list = plan_call(place, own, other, line)
    far_list = from_set(far_list, 2)

    cuts = (0, 8)
    to_next, to_last = send_call(next_list, last_list, pieces, cuts)
    arrived = [touch_call(x, LAST_US) for x in (from_set(to_next, 3), from_set(to_last, 1))]

    far_here = [far_line] + [from_cand(far_line, 1, k) for k in (1, 2, 3)]
    far_pieces = far_here + [from_core(x) for x in far_here]
    base = keep_call(own_list, accumulator[0], pieces, to_next)
    base = keep_call(far_list, base, far_pieces)
    base = final_call(base, arrived, cuts)
    return base[None]


def solution(mesh):
    placed = (
        P("set", "cand", None),
        P("set", None, None),
        P("set", "cand", None, None),
        P("set", "cand", None, None),
        P("set", "cand", None, None),
        P("set", "cand", None, None),
        P("set", "cand", None, None),
    )
    return jax.shard_map(
        per_device,
        mesh=mesh,
        in_specs=placed,
        out_specs=P("set", "cand", None, None),
        check_vma=False,
    )
```

time: 166 us -> 111 us (0.67)
  waiting for transfers between devices: 68.8 us -> 42 us
  Pallas kernels: 44.6 us -> 29.5 us
  between operations: 13.6 us -> 0.37 us
  starting transfers between devices: 28.7 us -> 34.8 us
  local copies, waits for them, and re-layouts: 5.42 us -> 2.37 us
  other arithmetic: 3.42 us -> 0.61 us
    ppermute x28 -> x15, waiting for transfers between devices: 47.1 us -> 17.7 us  [from_cand(): return lax.ppermute(x, 'cand', pairs)]
    pallas_call x5 -> x10, Pallas kernels: 41.6 us -> 25.4 us  [the longest x2 8.85 us: keep_call(): pl.pallas_call(kernel, out_shape=jax.ShapeDtypeStruct((NT_DEV, BLOCK, BLO...]
    ppermute x0 -> x14, waiting for transfers between devices: none -> 11.9 us  [the longest x4 9.19 us: from_cand(): return lax.ppermute(x, ('set', 'cand'), pairs)]
    ppermute x0 -> x14, starting transfers between devices: none -> 9.47 us  [the longest x4 8.27 us: from_cand(): return lax.ppermute(x, ('set', 'cand'), pairs)]
    ppermute x4 -> x3, waiting for transfers between devices: 21.7 us -> 12.5 us  [from_set(): lax.ppermute(x, 'set', [((me + d) % N_SET, me) for me in range(N_SET)])]
    ppermute x28 -> x15, starting transfers between devices: 24.8 us -> 20.3 us  [from_cand(): return lax.ppermute(x, 'cand', pairs)]
    broadcast_in_dim x1 -> x0, other arithmetic: 3.25 us -> none  [per_device(): return (base - (from_last.astype(f32) + from_next.astype(f32)))[None]]
    unnamed x19 -> x16, local copies, waits for them, and re-layouts: 5.42 us -> 2.37 us
  transfers between devices with their start and end apart: 33 -> 32, of which waited for: 16 -> 19; matrix products, arithmetic and copies ran while one was open for 0% -> 0% of each run, Pallas kernels for 23% -> 17%
where the time goes in v2:
time: 111 us; the launch traced here: 110 us
  waiting for transfers between devices  42 us (38%)
  starting transfers between devices  34.8 us (31%)
  Pallas kernels  29.5 us (27%)
  local copies, waits for them, and re-layouts  2.37 us (2%)
    ppermute x15, starting transfers between devices, from_cand(): return lax.ppermute(x, 'cand', pairs)  20.3 us
    ppermute x15, waiting for transfers between devices, from_cand(): return lax.ppermute(x, 'cand', pairs)  17.7 us
    ppermute x3, waiting for transfers between devices, from_set(): lax.ppermute(x, 'set', [((me + d) % N_SET, me) for me in range(N_SET)])  12.5 us
    ppermute x4, waiting for transfers between devices, from_cand(): return lax.ppermute(x, ('set', 'cand'), pairs)  9.19 us
    pallas_call x2, Pallas kernels, keep_call(): pl.pallas_call(kernel, out_shape=jax.ShapeDtypeStruct((NT_DEV, BLOCK, BLO...  8.85 us
    ppermute x4, starting transfers between devices, from_cand(): return lax.ppermute(x, ('set', 'cand'), pairs)  8.27 us
    pallas_call x1, Pallas kernels, send_call(): pl.pallas_call(kernel, out_shape=shapes, in_specs=[SMEM, SMEM] + [ANY] *...  7.89 us
    ppermute x3, starting transfers between devices, from_set(): lax.ppermute(x, 'set', [((me + d) % N_SET, me) for me in range(N_SET)])  5.01 us
  transfers between devices with their start and end apart: 32, of which 19 were waited for; matrix products, arithmetic and copies ran while one was open for 0% of the time, Pallas kernels for 17%

profile of v2, /device:TPU:6, one launch (start us, length us, event | category | flops | bytes accessed | tf_op | source)
XLA Modules:
  0.0 109.6 jit_solution(9793394435762643139)
XLA Ops:
  0.6 4.1 %sketch.1 = (f32[16,512]{1,0:T(8,128)}, f32[16,512]{1,0:T(8,128)}) custom-call(s32[2]{0:T(128)} %pad_add_fusion.place.refs_0_, bf16[2048,512]{1,0:T(8,128)(2,1)} %bitcast.20, bf16[32,512]{1,0:T(8,128)(2,1)} %bitcast.23), custom_call_target="tpu_custom_call" | custom-call | tf_op jit(solution)/shard_map/sketch/pallas_call | solution.py:82
  4.7 1.4 %collective-permute-done.got = f32[16,512]{1,0:T(8,128)S(1)} collective-permute-done((f32[16,512]{1,0:T(8,128)}, f32[16,512]{1,0:T(8,128)S(1)}, u32[]{:S(2)}, u32[]{:S(2)}) %collective-permute-start) | collective-permute-done | bytes 32800 | tf_op jit(solution)/shard_map/ppermute | solution.py:55
  6.9 3.0 %collective-permute-start.1 = (f32[24,512]{1,0:T(8,128)S(1)}, f32[24,512]{1,0:T(8,128)S(1)}, u32[]{:S(2)}, u32[]{:S(2)}) collective-permute-start(f32[24,512]{1,0:T(8,128)S(1)} %sum_core.1.r0), channel_id=1, source_target_pairs={{2,0},{9,1},{4,2},{11,3},{6,4},{13,5},{0,6},{15,7},{10,8},{17,9},{... | collective-permute-start | bytes 147464 | tf_op jit(solution)/shard_map/ppermute | solution.py:45
  11.6 3.9 %collective-permute-done.2.r2 = f32[24,512]{1,0:T(8,128)S(1)} collective-permute-done((f32[24,512]{1,0:T(8,128)S(1)}, f32[24,512]{1,0:T(8,128)S(1)}, u32[]{:S(2)}, u32[]{:S(2)}) %collective-permute-start.2) | collective-permute-done | bytes 49184 | tf_op jit(solution)/shard_map/ppermute | solution.py:45
  16.0 4.1 %collective-permute-start.4 = (f32[24,512]{1,0:T(8,128)S(1)}, f32[24,512]{1,0:T(8,128)S(1)}, u32[]{:S(2)}, u32[]{:S(2)}) collective-permute-start(f32[24,512]{1,0:T(8,128)S(1)} %sum_first.1.r0), channel_id=1, source_target_pairs={{8,0},{3,1},{10,2},{5,3},{12,4},{7,5},{14,6},{1,7},{16,8},{11,9},{... | collective-permute-start | bytes 147464 | tf_op jit(solution)/shard_map/ppermute | solution.py:45
  20.1 1.3 %collective-permute-start.6 = (f32[24,512]{1,0:T(8,128)S(1)}, f32[24,512]{1,0:T(8,128)S(1)}, u32[]{:S(2)}, u32[]{:S(2)}) collective-permute-start(f32[24,512]{1,0:T(8,128)S(1)} %sum_first.1.r0), channel_id=1, source_target_pairs={{24,0},{7,1},{26,2},{1,3},{28,4},{3,5},{30,6},{5,7},{0,8},{15,9},{... | collective-permute-start | bytes 147464 | tf_op jit(solution)/shard_map/ppermute | solution.py:45
  21.9 3.9 %collective-permute-done.5.r2 = f32[24,512]{1,0:T(8,128)S(1)} collective-permute-done((f32[24,512]{1,0:T(8,128)S(1)}, f32[24,512]{1,0:T(8,128)S(1)}, u32[]{:S(2)}, u32[]{:S(2)}) %collective-permute-start.5) | collective-permute-done | bytes 49184 | tf_op jit(solution)/shard_map/ppermute | solution.py:45
  26.1 1.3 %collective-permute-done.7.other.refs_2_ = f32[48,512]{1,0:T(8,128)S(1)} collective-permute-done((f32[48,512]{1,0:T(8,128)S(1)}, f32[48,512]{1,0:T(8,128)S(1)}, u32[]{:S(2)}, u32[]{:S(2)}) %collective-permute-start.7) | collective-permute-done | bytes 98336 | tf_op jit(solution)/shard_map/ppermute | solution.py:55
  27.4 1.6 %copy-done = bf16[1,2048,512]{2,1,0:T(8,128)(2,1)S(1)} copy-done((bf16[1,2048,512]{2,1,0:T(8,128)(2,1)S(1)}, bf16[1,2048,512]{2,1,0:T(8,128)(2,1)}, u32[]{:S(2)}) %copy-start) | copy-done | bytes 2097176
  29.0 4.6 %factor.1.refs_0_ = bf16[272,256]{1,0:T(8,128)(2,1)S(1)} custom-call(s32[2]{0:T(128)S(1)} %copy-done.3, f32[48,512]{1,0:T(8,128)S(1)} %sum_second.1.own.refs_1_, f32[48,512]{1,0:T(8,128)S(1)} %collective-permute-done.7.other.refs_2_, bf16[2048,512]{1,0:T(8,128)(2,1)S(1)} %bitcast.21), custom_call_target="tpu_custom_call" | custom-call | tf_op jit(solution)/shard_map/factor/pallas_call | solution.py:168
  33.6 3.2 %collective-permute-start.8 = (bf16[272,256]{1,0:T(8,128)(2,1)S(1)}, bf16[272,256]{1,0:T(8,128)(2,1)S(1)}, u32[]{:S(2)}, u32[]{:S(2)}) collective-permute-start(bf16[272,256]{1,0:T(8,128)(2,1)S(1)} %factor.1.refs_0_), channel_id=1, source_target_pairs={{2,0},{9,1},{4,2},{11,3},{6,4},{13,5},{0,6},{15,7},{10,8},{17,9},{... | collective-permute-start | bytes 417800 | tf_op jit(solution)/shard_map/ppermute | solution.py:45
  37.1 2.7 %collective-permute-done.10.refs_3_ = bf16[272,256]{1,0:T(8,128)(2,1)S(1)} collective-permute-done((bf16[272,256]{1,0:T(8,128)(2,1)S(1)}, bf16[272,256]{1,0:T(8,128)(2,1)S(1)}, u32[]{:S(2)}, u32[]{:S(2)}) %collective-permute-start.10) | collective-permute-done | bytes 139296 | tf_op jit(solution)/shard_map/ppermute | solution.py:45
  40.9 2.5 %collective-permute-done.9.refs_2_ = bf16[272,256]{1,0:T(8,128)(2,1)S(1)} collective-permute-done((bf16[272,256]{1,0:T(8,128)(2,1)S(1)}, bf16[272,256]{1,0:T(8,128)(2,1)S(1)}, u32[]{:S(2)}, u32[]{:S(2)}) %collective-permute-start.9) | collective-permute-done | bytes 139296 | tf_op jit(solution)/shard_map/ppermute | solution.py:45
  46.1 1.3 %collective-permute-start.14 = (bf16[4,272,256]{2,1,0:T(8,128)(2,1)S(1)}, bf16[4,272,256]{2,1,0:T(8,128)(2,1)S(1)}, u32[]{:S(2)}, u32[]{:S(2)}) collective-permute-start(bf16[4,272,256]{2,1,0:T(8,128)(2,1)S(1)} %join.2.refs_3_.refs_0_), channel_id=1, source_target_pairs={{24,0},{7,1},{26,2},{1,3},{28,4},{3,5},{30,6},{5,7},{0,8},{15,9},{... | collective-permute-start | bytes 1671176 | tf_op jit(solution)/shard_map/ppermute | solution.py:45
  47.4 1.4 %collective-permute-start.19 = (bf16[272,256]{1,0:T(8,128)(2,1)S(1)}, bf16[272,256]{1,0:T(8,128)(2,1)S(1)}, u32[]{:S(2)}, u32[]{:S(2)}) collective-permute-start(bf16[272,256]{1,0:T(8,128)(2,1)S(1)} %factor.1.refs_0_), channel_id=1, source_target_pairs={{64,0},{65,1},{66,2},{67,3},{68,4},{69,5},{70,6},{71,7},{72,8},{73... | collective-permute-start | bytes 417800 | tf_op jit(solution)/shard_map/ppermute | solution.py:51
  48.8 2.8 %collective-permute-start.20 = (bf16[272,256]{1,0:T(8,128)(2,1)S(1)}, bf16[272,256]{1,0:T(8,128)(2,1)S(1)}, u32[]{:S(2)}, u32[]{:S(2)}) collective-permute-start(bf16[272,256]{1,0:T(8,128)(2,1)S(1)} %factor.1.refs_0_), channel_id=1, source_target_pairs={{66,0},{73,1},{68,2},{75,3},{70,4},{77,5},{64,6},{79,7},{74,8},{81... | collective-permute-start | bytes 417800 | tf_op jit(solution)/shard_map/ppermute | solution.py:51
  51.6 2.4 %collective-permute-done.19.refs_0_ = bf16[272,256]{1,0:T(8,128)(2,1)S(1)} collective-permute-done((bf16[272,256]{1,0:T(8,128)(2,1)S(1)}, bf16[272,256]{1,0:T(8,128)(2,1)S(1)}, u32[]{:S(2)}, u32[]{:S(2)}) %collective-permute-start.19) | collective-permute-done | bytes 139296 | tf_op jit(solution)/shard_map/ppermute | solution.py:51
  54.0 2.3 %collective-permute-start.21 = (bf16[272,256]{1,0:T(8,128)(2,1)S(1)}, bf16[272,256]{1,0:T(8,128)(2,1)S(1)}, u32[]{:S(2)}, u32[]{:S(2)}) collective-permute-start(bf16[272,256]{1,0:T(8,128)(2,1)S(1)} %factor.1.refs_0_), channel_id=1, source_target_pairs={{68,0},{81,1},{70,2},{83,3},{64,4},{85,5},{66,6},{87,7},{76,8},{89... | collective-permute-start | bytes 417800 | tf_op jit(solution)/shard_map/ppermute | solution.py:51
  56.3 1.4 %collective-permute-done.20.refs_1_ = bf16[272,256]{1,0:T(8,128)(2,1)S(1)} collective-permute-done((bf16[272,256]{1,0:T(8,128)(2,1)S(1)}, bf16[272,256]{1,0:T(8,128)(2,1)S(1)}, u32[]{:S(2)}, u32[]{:S(2)}) %collective-permute-start.20) | collective-permute-done | bytes 139296 | tf_op jit(solution)/shard_map/ppermute | solution.py:51
  57.7 1.7 %collective-permute-start.22 = (bf16[272,256]{1,0:T(8,128)(2,1)S(1)}, bf16[272,256]{1,0:T(8,128)(2,1)S(1)}, u32[]{:S(2)}, u32[]{:S(2)}) collective-permute-start(bf16[272,256]{1,0:T(8,128)(2,1)S(1)} %factor.1.refs_0_), channel_id=1, source_target_pairs={{70,0},{89,1},{64,2},{91,3},{66,4},{93,5},{68,6},{95,7},{78,8},{65... | collective-permute-start | bytes 417800 | tf_op jit(solution)/shard_map/ppermute | solution.py:51
  59.5 4.0 %collective-permute-done.21.refs_2_ = bf16[272,256]{1,0:T(8,128)(2,1)S(1)} collective-permute-done((bf16[272,256]{1,0:T(8,128)(2,1)S(1)}, bf16[272,256]{1,0:T(8,128)(2,1)S(1)}, u32[]{:S(2)}, u32[]{:S(2)}) %collective-permute-start.21) | collective-permute-done | bytes 139296 | tf_op jit(solution)/shard_map/ppermute | solution.py:51
  65.0 1.4 %collective-permute-done.22.refs_3_ = bf16[272,256]{1,0:T(8,128)(2,1)S(1)} collective-permute-done((bf16[272,256]{1,0:T(8,128)(2,1)S(1)}, bf16[272,256]{1,0:T(8,128)(2,1)S(1)}, u32[]{:S(2)}, u32[]{:S(2)}) %collective-permute-start.22) | collective-permute-done | bytes 139296 | tf_op jit(solution)/shard_map/ppermute | solution.py:51
  67.1 2.0 %collective-permute-start.23 = (bf16[4,272,256]{2,1,0:T(8,128)(2,1)S(1)}, bf16[4,272,256]{2,1,0:T(8,128)(2,1)S(1)}, u32[]{:S(2)}, u32[]{:S(2)}) collective-permute-start(bf16[4,272,256]{2,1,0:T(8,128)(2,1)S(1)} %join.3.refs_0_), channel_id=1, source_target_pairs={{8,0},{3,1},{10,2},{5,3},{12,4},{7,5},{14,6},{1,7},{16,8},{11,9},{... | collective-permute-start | bytes 1671176 | tf_op jit(solution)/shard_map/ppermute | solution.py:45
  71.8 2.9 %collective-permute-start.11 = (s32[8,128]{1,0:T(8,128)S(1)}, s32[8,128]{1,0:T(8,128)S(1)}, u32[]{:S(2)}, u32[]{:S(2)}) collective-permute-start(s32[8,128]{1,0:T(8,128)S(1)} %get-tuple-element.15), channel_id=1, source_target_pairs={{64,0},{96,32},{0,64},{32,96},{65,1},{97,33},{1,65},{33,97},{66,2}... | collective-permute-start | bytes 12296 | tf_op jit(solution)/shard_map/ppermute | solution.py:59
  74.8 7.9 %send_pairs.1 = (bf16[8,256,256]{2,1,0:T(8,128)(2,1)S(1)}, bf16[8,256,256]{2,1,0:T(8,128)(2,1)S(1)}) custom-call(s32[8,128]{1,0:T(8,128)S(1)} %get-tuple-element.17.next_list, s32[8,128]{1,0:T(8,128)S(1)} %get-tuple-element.18.last_list, bf16[4,272,256]{2,1,0:T(8,128)(2,1)S(1)} %join.2.refs_3_.refs_0_, ...), custom_call_target="tpu_custom_call" | custom-call | tf_op jit(solution)/shard_map/send_pairs/pallas_call | solution.py:354
  82.8 2.0 %collective-permute-start.31 = (bf16[8,256,256]{2,1,0:T(8,128)(2,1)S(1)}, bf16[8,256,256]{2,1,0:T(8,128)(2,1)S(1)}, u32[]{:S(2)}, u32[]{:S(2)}) collective-permute-start(bf16[8,256,256]{2,1,0:T(8,128)(2,1)S(1)} %get-tuple-element.20), channel_id=1, source_target_pairs={{32,0},{64,32},{96,64},{0,96},{33,1},{65,33},{97,65},{1,97},{34,2}... | collective-permute-start | bytes 3145736 | tf_op jit(solution)/shard_map/ppermute | solution.py:59
  84.8 1.4 %collective-permute-done.25.refs_3_ = bf16[4,272,256]{2,1,0:T(8,128)(2,1)S(1)} collective-permute-done((bf16[4,272,256]{2,1,0:T(8,128)(2,1)S(1)}, bf16[4,272,256]{2,1,0:T(8,128)(2,1)S(1)}, u32[]{:S(2)}, u32[]{:S(2)}) %collective-permute-start.25) | collective-permute-done | bytes 557088 | tf_op jit(solution)/shard_map/ppermute | solution.py:45
  86.7 4.4 %keep_pairs.2.base = f32[8,256,256]{2,1,0:T(8,128)S(1)} custom-call(s32[8,128]{1,0:T(8,128)S(1)} %get-tuple-element.16.pairs, f32[8,256,256]{2,1,0:T(8,128)S(1)} %bitcast.22, bf16[4,272,256]{2,1,0:T(8,128)(2,1)S(1)} %join.2.refs_3_.refs_0_, bf16[4,272,256]{2,1,0:T(8,128)(2,1)S(1)} %collective-permute-done.12.refs_1_, ...), custom_call_target="tpu_custom_call" | custom-call | tf_op jit(solution)/shard_map/keep_pairs/pallas_call | solution.py:375
  91.1 4.4 %keep_pairs.3.base = f32[8,256,256]{2,1,0:T(8,128)S(1)} custom-call(s32[8,128]{1,0:T(8,128)S(1)} %collective-permute-done.11.pairs, f32[8,256,256]{2,1,0:T(8,128)S(1)} %keep_pairs.2.base, bf16[4,272,256]{2,1,0:T(8,128)(2,1)S(1)} %join.3.refs_0_, bf16[4,272,256]{2,1,0:T(8,128)(2,1)S(1)} %collective-permute-done.23.refs_1_, ...), custom_call_target="tpu_custom_call" | custom-call | tf_op jit(solution)/shard_map/keep_pairs/pallas_call | solution.py:375
  95.6 11.2 %collective-permute-done.30.refs_0_ = bf16[8,256,256]{2,1,0:T(8,128)(2,1)S(1)} collective-permute-done((bf16[8,256,256]{2,1,0:T(8,128)(2,1)S(1)}, bf16[8,256,256]{2,1,0:T(8,128)(2,1)S(1)}, u32[]{:S(2)}, u32[]{:S(2)}) %collective-permute-start.30) | collective-permute-done | bytes 1048608 | tf_op jit(solution)/shard_map/ppermute | solution.py:59
  106.7 1.3 %collective-permute-done.31.refs_0_ = bf16[8,256,256]{2,1,0:T(8,128)(2,1)S(1)} collective-permute-done((bf16[8,256,256]{2,1,0:T(8,128)(2,1)S(1)}, bf16[8,256,256]{2,1,0:T(8,128)(2,1)S(1)}, u32[]{:S(2)}, u32[]{:S(2)}) %collective-permute-start.31) | collective-permute-done | bytes 1048608 | tf_op jit(solution)/shard_map/ppermute | solution.py:59
  108.0 1.4 %final.1 = f32[8,256,256]{2,1,0:T(8,128)} custom-call(f32[8,256,256]{2,1,0:T(8,128)S(1)} %keep_pairs.3.base, bf16[8,256,256]{2,1,0:T(8,128)(2,1)S(1)} %touch.2.refs_0_, bf16[8,256,256]{2,1,0:T(8,128)(2,1)S(1)} %touch.3.refs_1_), custom_call_target="tpu_custom_call" | custom-call | tf_op jit(solution)/shard_map/final/pallas_call | solution.py:402
  (64 shorter events, 14.0 us)
Async XLA Ops:
  4.7 1.4 %collective-permute-start = (f32[16,512]{1,0:T(8,128)}, f32[16,512]{1,0:T(8,128)S(1)}, u32[]{:S(2)}, u32[]{:S(2)}) collective-permute-start(f32[16,512]{1,0:T(8,128)} %get-tuple-element.14), channel_id=1, source_target_pairs={{1,0},{0,1},{3,2},{2,3},{5,4},{4,5},{7,6},{6,7},{9,8},{8,9},{11,10... | collective-permute-start | bytes 98312 | tf_op jit(solution)/shard_map/ppermute | solution.py:55
  6.9 4.8 %collective-permute-start.1 = (f32[24,512]{1,0:T(8,128)S(1)}, f32[24,512]{1,0:T(8,128)S(1)}, u32[]{:S(2)}, u32[]{:S(2)}) collective-permute-start(f32[24,512]{1,0:T(8,128)S(1)} %sum_core.1.r0), channel_id=1, source_target_pairs={{2,0},{9,1},{4,2},{11,3},{6,4},{13,5},{0,6},{15,7},{10,8},{17,9},{... | collective-permute-start | bytes 147464 | tf_op jit(solution)/shard_map/ppermute | solution.py:45
  9.9 5.6 %collective-permute-start.2 = (f32[24,512]{1,0:T(8,128)S(1)}, f32[24,512]{1,0:T(8,128)S(1)}, u32[]{:S(2)}, u32[]{:S(2)}) collective-permute-start(f32[24,512]{1,0:T(8,128)S(1)} %sum_core.1.r0), channel_id=1, source_target_pairs={{4,0},{17,1},{6,2},{19,3},{0,4},{21,5},{2,6},{23,7},{12,8},{25,9},... | collective-permute-start | bytes 147464 | tf_op jit(solution)/shard_map/ppermute | solution.py:45
  10.5 5.5 %collective-permute-start.3 = (f32[24,512]{1,0:T(8,128)S(1)}, f32[24,512]{1,0:T(8,128)S(1)}, u32[]{:S(2)}, u32[]{:S(2)}) collective-permute-start(f32[24,512]{1,0:T(8,128)S(1)} %sum_core.1.r0), channel_id=1, source_target_pairs={{6,0},{25,1},{0,2},{27,3},{2,4},{29,5},{4,6},{31,7},{14,8},{1,9},{... | collective-permute-start | bytes 147464 | tf_op jit(solution)/shard_map/ppermute | solution.py:45
  16.0 5.9 %collective-permute-start.4 = (f32[24,512]{1,0:T(8,128)S(1)}, f32[24,512]{1,0:T(8,128)S(1)}, u32[]{:S(2)}, u32[]{:S(2)}) collective-permute-start(f32[24,512]{1,0:T(8,128)S(1)} %sum_first.1.r0), channel_id=1, source_target_pairs={{8,0},{3,1},{10,2},{5,3},{12,4},{7,5},{14,6},{1,7},{16,8},{11,9},{... | collective-permute-start | bytes 147464 | tf_op jit(solution)/shard_map/ppermute | solution.py:45
  20.1 5.7 %collective-permute-start.5 = (f32[24,512]{1,0:T(8,128)S(1)}, f32[24,512]{1,0:T(8,128)S(1)}, u32[]{:S(2)}, u32[]{:S(2)}) collective-permute-start(f32[24,512]{1,0:T(8,128)S(1)} %sum_first.1.r0), channel_id=1, source_target_pairs={{16,0},{5,1},{18,2},{7,3},{20,4},{1,5},{22,6},{3,7},{24,8},{13,9},... | collective-permute-start | bytes 147464 | tf_op jit(solution)/shard_map/ppermute | solution.py:45
  20.1 5.8 %collective-permute-start.6 = (f32[24,512]{1,0:T(8,128)S(1)}, f32[24,512]{1,0:T(8,128)S(1)}, u32[]{:S(2)}, u32[]{:S(2)}) collective-permute-start(f32[24,512]{1,0:T(8,128)S(1)} %sum_first.1.r0), channel_id=1, source_target_pairs={{24,0},{7,1},{26,2},{1,3},{28,4},{3,5},{30,6},{5,7},{0,8},{15,9},{... | collective-permute-start | bytes 147464 | tf_op jit(solution)/shard_map/ppermute | solution.py:45
  26.0 1.4 %collective-permute-start.7 = (f32[48,512]{1,0:T(8,128)S(1)}, f32[48,512]{1,0:T(8,128)S(1)}, u32[]{:S(2)}, u32[]{:S(2)}) collective-permute-start(f32[48,512]{1,0:T(8,128)S(1)} %sum_second.1.own.refs_1_), channel_id=1, source_target_pairs={{1,0},{0,1},{3,2},{2,3},{5,4},{4,5},{7,6},{6,7},{9,8},{8,9},{11,10... | collective-permute-start | bytes 294920 | tf_op jit(solution)/shard_map/ppermute | solution.py:55
  33.5 6.3 %collective-permute-start.10 = (bf16[272,256]{1,0:T(8,128)(2,1)S(1)}, bf16[272,256]{1,0:T(8,128)(2,1)S(1)}, u32[]{:S(2)}, u32[]{:S(2)}) collective-permute-start(bf16[272,256]{1,0:T(8,128)(2,1)S(1)} %factor.1.refs_0_), channel_id=1, source_target_pairs={{6,0},{25,1},{0,2},{27,3},{2,4},{29,5},{4,6},{31,7},{14,8},{1,9},{... | collective-permute-start | bytes 417800 | tf_op jit(solution)/shard_map/ppermute | solution.py:45
  33.6 7.3 %collective-permute-start.8 = (bf16[272,256]{1,0:T(8,128)(2,1)S(1)}, bf16[272,256]{1,0:T(8,128)(2,1)S(1)}, u32[]{:S(2)}, u32[]{:S(2)}) collective-permute-start(bf16[272,256]{1,0:T(8,128)(2,1)S(1)} %factor.1.refs_0_), channel_id=1, source_target_pairs={{2,0},{9,1},{4,2},{11,3},{6,4},{13,5},{0,6},{15,7},{10,8},{17,9},{... | collective-permute-start | bytes 417800 | tf_op jit(solution)/shard_map/ppermute | solution.py:45
  36.8 6.6 %collective-permute-start.9 = (bf16[272,256]{1,0:T(8,128)(2,1)S(1)}, bf16[272,256]{1,0:T(8,128)(2,1)S(1)}, u32[]{:S(2)}, u32[]{:S(2)}) collective-permute-start(bf16[272,256]{1,0:T(8,128)(2,1)S(1)} %factor.1.refs_0_), channel_id=1, source_target_pairs={{4,0},{17,1},{6,2},{19,3},{0,4},{21,5},{2,6},{23,7},{12,8},{25,9},... | collective-permute-start | bytes 417800 | tf_op jit(solution)/shard_map/ppermute | solution.py:45
  44.1 19.4 %collective-permute-start.12 = (bf16[4,272,256]{2,1,0:T(8,128)(2,1)S(1)}, bf16[4,272,256]{2,1,0:T(8,128)(2,1)S(1)}, u32[]{:S(2)}, u32[]{:S(2)}) collective-permute-start(bf16[4,272,256]{2,1,0:T(8,128)(2,1)S(1)} %join.2.refs_3_.refs_0_), channel_id=1, source_target_pairs={{8,0},{3,1},{10,2},{5,3},{12,4},{7,5},{14,6},{1,7},{16,8},{11,9},{... | collective-permute-start | bytes 1671176 | tf_op jit(solution)/shard_map/ppermute | solution.py:45
  45.0 19.0 %collective-permute-start.13 = (bf16[4,272,256]{2,1,0:T(8,128)(2,1)S(1)}, bf16[4,272,256]{2,1,0:T(8,128)(2,1)S(1)}, u32[]{:S(2)}, u32[]{:S(2)}) collective-permute-start(bf16[4,272,256]{2,1,0:T(8,128)(2,1)S(1)} %join.2.refs_3_.refs_0_), channel_id=1, source_target_pairs={{16,0},{5,1},{18,2},{7,3},{20,4},{1,5},{22,6},{3,7},{24,8},{13,9},... | collective-permute-start | bytes 1671176 | tf_op jit(solution)/shard_map/ppermute | solution.py:45
  46.1 19.0 %collective-permute-start.14 = (bf16[4,272,256]{2,1,0:T(8,128)(2,1)S(1)}, bf16[4,272,256]{2,1,0:T(8,128)(2,1)S(1)}, u32[]{:S(2)}, u32[]{:S(2)}) collective-permute-start(bf16[4,272,256]{2,1,0:T(8,128)(2,1)S(1)} %join.2.refs_3_.refs_0_), channel_id=1, source_target_pairs={{24,0},{7,1},{26,2},{1,3},{28,4},{3,5},{30,6},{5,7},{0,8},{15,9},{... | collective-permute-start | bytes 1671176 | tf_op jit(solution)/shard_map/ppermute | solution.py:45
  47.4 6.6 %collective-permute-start.19 = (bf16[272,256]{1,0:T(8,128)(2,1)S(1)}, bf16[272,256]{1,0:T(8,128)(2,1)S(1)}, u32[]{:S(2)}, u32[]{:S(2)}) collective-permute-start(bf16[272,256]{1,0:T(8,128)(2,1)S(1)} %factor.1.refs_0_), channel_id=1, source_target_pairs={{64,0},{65,1},{66,2},{67,3},{68,4},{69,5},{70,6},{71,7},{72,8},{73... | collective-permute-start | bytes 417800 | tf_op jit(solution)/shard_map/ppermute | solution.py:51
  48.8 8.9 %collective-permute-start.20 = (bf16[272,256]{1,0:T(8,128)(2,1)S(1)}, bf16[272,256]{1,0:T(8,128)(2,1)S(1)}, u32[]{:S(2)}, u32[]{:S(2)}) collective-permute-start(bf16[272,256]{1,0:T(8,128)(2,1)S(1)} %factor.1.refs_0_), channel_id=1, source_target_pairs={{66,0},{73,1},{68,2},{75,3},{70,4},{77,5},{64,6},{79,7},{74,8},{81... | collective-permute-start | bytes 417800 | tf_op jit(solution)/shard_map/ppermute | solution.py:51
  54.0 9.6 %collective-permute-start.21 = (bf16[272,256]{1,0:T(8,128)(2,1)S(1)}, bf16[272,256]{1,0:T(8,128)(2,1)S(1)}, u32[]{:S(2)}, u32[]{:S(2)}) collective-permute-start(bf16[272,256]{1,0:T(8,128)(2,1)S(1)} %factor.1.refs_0_), channel_id=1, source_target_pairs={{68,0},{81,1},{70,2},{83,3},{64,4},{85,5},{66,6},{87,7},{76,8},{89... | collective-permute-start | bytes 417800 | tf_op jit(solution)/shard_map/ppermute | solution.py:51
  57.7 8.7 %collective-permute-start.22 = (bf16[272,256]{1,0:T(8,128)(2,1)S(1)}, bf16[272,256]{1,0:T(8,128)(2,1)S(1)}, u32[]{:S(2)}, u32[]{:S(2)}) collective-permute-start(bf16[272,256]{1,0:T(8,128)(2,1)S(1)} %factor.1.refs_0_), channel_id=1, source_target_pairs={{70,0},{89,1},{64,2},{91,3},{66,4},{93,5},{68,6},{95,7},{78,8},{65... | collective-permute-start | bytes 417800 | tf_op jit(solution)/shard_map/ppermute | solution.py:51
  63.5 5.6 %collective-permute-start.15 = (bf16[4,272,256]{2,1,0:T(8,128)(2,1)S(1)}, bf16[4,272,256]{2,1,0:T(8,128)(2,1)S(1)}, u32[]{:S(2)}, u32[]{:S(2)}) collective-permute-start(bf16[4,272,256]{2,1,0:T(8,128)(2,1)S(1)} %join.2.refs_3_.refs_0_), channel_id=1, source_target_pairs={{1,0},{0,1},{3,2},{2,3},{5,4},{4,5},{7,6},{6,7},{9,8},{8,9},{11,10... | collective-permute-start | bytes 1671176 | tf_op jit(solution)/shard_map/ppermute | solution.py:55
  63.5 6.0 %collective-permute-start.16 = (bf16[4,272,256]{2,1,0:T(8,128)(2,1)S(1)}, bf16[4,272,256]{2,1,0:T(8,128)(2,1)S(1)}, u32[]{:S(2)}, u32[]{:S(2)}) collective-permute-start(bf16[4,272,256]{2,1,0:T(8,128)(2,1)S(1)} %collective-permute-done.12.refs_1_), channel_id=1, source_target_pairs={{1,0},{0,1},{3,2},{2,3},{5,4},{4,5},{7,6},{6,7},{9,8},{8,9},{11,10... | collective-permute-start | bytes 1671176 | tf_op jit(solution)/shard_map/ppermute | solution.py:55
  64.0 6.6 %collective-permute-start.17 = (bf16[4,272,256]{2,1,0:T(8,128)(2,1)S(1)}, bf16[4,272,256]{2,1,0:T(8,128)(2,1)S(1)}, u32[]{:S(2)}, u32[]{:S(2)}) collective-permute-start(bf16[4,272,256]{2,1,0:T(8,128)(2,1)S(1)} %collective-permute-done.13.refs_2_), channel_id=1, source_target_pairs={{1,0},{0,1},{3,2},{2,3},{5,4},{4,5},{7,6},{6,7},{9,8},{8,9},{11,10... | collective-permute-start | bytes 1671176 | tf_op jit(solution)/shard_map/ppermute | solution.py:55
  65.0 6.8 %collective-permute-start.18 = (bf16[4,272,256]{2,1,0:T(8,128)(2,1)S(1)}, bf16[4,272,256]{2,1,0:T(8,128)(2,1)S(1)}, u32[]{:S(2)}, u32[]{:S(2)}) collective-permute-start(bf16[4,272,256]{2,1,0:T(8,128)(2,1)S(1)} %collective-permute-done.14.refs_3_), channel_id=1, source_target_pairs={{1,0},{0,1},{3,2},{2,3},{5,4},{4,5},{7,6},{6,7},{9,8},{8,9},{11,10... | collective-permute-start | bytes 1671176 | tf_op jit(solution)/shard_map/ppermute | solution.py:55
  67.1 15.6 %collective-permute-start.23 = (bf16[4,272,256]{2,1,0:T(8,128)(2,1)S(1)}, bf16[4,272,256]{2,1,0:T(8,128)(2,1)S(1)}, u32[]{:S(2)}, u32[]{:S(2)}) collective-permute-start(bf16[4,272,256]{2,1,0:T(8,128)(2,1)S(1)} %join.3.refs_0_), channel_id=1, source_target_pairs={{8,0},{3,1},{10,2},{5,3},{12,4},{7,5},{14,6},{1,7},{16,8},{11,9},{... | collective-permute-start | bytes 1671176 | tf_op jit(solution)/shard_map/ppermute | solution.py:45
  69.1 15.6 %collective-permute-start.24 = (bf16[4,272,256]{2,1,0:T(8,128)(2,1)S(1)}, bf16[4,272,256]{2,1,0:T(8,128)(2,1)S(1)}, u32[]{:S(2)}, u32[]{:S(2)}) collective-permute-start(bf16[4,272,256]{2,1,0:T(8,128)(2,1)S(1)} %join.3.refs_0_), channel_id=1, source_target_pairs={{16,0},{5,1},{18,2},{7,3},{20,4},{1,5},{22,6},{3,7},{24,8},{13,9},... | collective-permute-start | bytes 1671176 | tf_op jit(solution)/shard_map/ppermute | solution.py:45
  69.5 16.6 %collective-permute-start.25 = (bf16[4,272,256]{2,1,0:T(8,128)(2,1)S(1)}, bf16[4,272,256]{2,1,0:T(8,128)(2,1)S(1)}, u32[]{:S(2)}, u32[]{:S(2)}) collective-permute-start(bf16[4,272,256]{2,1,0:T(8,128)(2,1)S(1)} %join.3.refs_0_), channel_id=1, source_target_pairs={{24,0},{7,1},{26,2},{1,3},{28,4},{3,5},{30,6},{5,7},{0,8},{15,9},{... | collective-permute-start | bytes 1671176 | tf_op jit(solution)/shard_map/ppermute | solution.py:45
  70.6 15.5 %collective-permute-start.26 = (bf16[4,272,256]{2,1,0:T(8,128)(2,1)S(1)}, bf16[4,272,256]{2,1,0:T(8,128)(2,1)S(1)}, u32[]{:S(2)}, u32[]{:S(2)}) collective-permute-start(bf16[4,272,256]{2,1,0:T(8,128)(2,1)S(1)} %join.3.refs_0_), channel_id=1, source_target_pairs={{1,0},{0,1},{3,2},{2,3},{5,4},{4,5},{7,6},{6,7},{9,8},{8,9},{11,10... | collective-permute-start | bytes 1671176 | tf_op jit(solution)/shard_map/ppermute | solution.py:55
  71.8 10.8 %collective-permute-start.11 = (s32[8,128]{1,0:T(8,128)S(1)}, s32[8,128]{1,0:T(8,128)S(1)}, u32[]{:S(2)}, u32[]{:S(2)}) collective-permute-start(s32[8,128]{1,0:T(8,128)S(1)} %get-tuple-element.15), channel_id=1, source_target_pairs={{64,0},{96,32},{0,64},{32,96},{65,1},{97,33},{1,65},{33,97},{66,2}... | collective-permute-start | bytes 12296 | tf_op jit(solution)/shard_map/ppermute | solution.py:59
  82.7 24.0 %collective-permute-start.30 = (bf16[8,256,256]{2,1,0:T(8,128)(2,1)S(1)}, bf16[8,256,256]{2,1,0:T(8,128)(2,1)S(1)}, u32[]{:S(2)}, u32[]{:S(2)}) collective-permute-start(bf16[8,256,256]{2,1,0:T(8,128)(2,1)S(1)} %get-tuple-element.19.refs_8_), channel_id=1, source_target_pairs={{96,0},{0,32},{32,64},{64,96},{97,1},{1,33},{33,65},{65,97},{98,2}... | collective-permute-start | bytes 3145736 | tf_op jit(solution)/shard_map/ppermute | solution.py:59
  82.8 25.3 %collective-permute-start.31 = (bf16[8,256,256]{2,1,0:T(8,128)(2,1)S(1)}, bf16[8,256,256]{2,1,0:T(8,128)(2,1)S(1)}, u32[]{:S(2)}, u32[]{:S(2)}) collective-permute-start(bf16[8,256,256]{2,1,0:T(8,128)(2,1)S(1)} %get-tuple-element.20), channel_id=1, source_target_pairs={{32,0},{64,32},{96,64},{0,96},{33,1},{65,33},{97,65},{1,97},{34,2}... | collective-permute-start | bytes 3145736 | tf_op jit(solution)/shard_map/ppermute | solution.py:59
  84.8 6.3 %collective-permute-start.27 = (bf16[4,272,256]{2,1,0:T(8,128)(2,1)S(1)}, bf16[4,272,256]{2,1,0:T(8,128)(2,1)S(1)}, u32[]{:S(2)}, u32[]{:S(2)}) collective-permute-start(bf16[4,272,256]{2,1,0:T(8,128)(2,1)S(1)} %collective-permute-done.23.refs_1_), channel_id=1, source_target_pairs={{1,0},{0,1},{3,2},{2,3},{5,4},{4,5},{7,6},{6,7},{9,8},{8,9},{11,10... | collective-permute-start | bytes 1671176 | tf_op jit(solution)/shard_map/ppermute | solution.py:55
  86.1 5.0 %collective-permute-start.28 = (bf16[4,272,256]{2,1,0:T(8,128)(2,1)S(1)}, bf16[4,272,256]{2,1,0:T(8,128)(2,1)S(1)}, u32[]{:S(2)}, u32[]{:S(2)}) collective-permute-start(bf16[4,272,256]{2,1,0:T(8,128)(2,1)S(1)} %collective-permute-done.24.refs_2_), channel_id=1, source_target_pairs={{1,0},{0,1},{3,2},{2,3},{5,4},{4,5},{7,6},{6,7},{9,8},{8,9},{11,10... | collective-permute-start | bytes 1671176 | tf_op jit(solution)/shard_map/ppermute | solution.py:55
  86.2 5.0 %collective-permute-start.29 = (bf16[4,272,256]{2,1,0:T(8,128)(2,1)S(1)}, bf16[4,272,256]{2,1,0:T(8,128)(2,1)S(1)}, u32[]{:S(2)}, u32[]{:S(2)}) collective-permute-start(bf16[4,272,256]{2,1,0:T(8,128)(2,1)S(1)} %collective-permute-done.25.refs_3_), channel_id=1, source_target_pairs={{1,0},{0,1},{3,2},{2,3},{5,4},{4,5},{7,6},{6,7},{9,8},{8,9},{11,10... | collective-permute-start | bytes 1671176 | tf_op jit(solution)/shard_map/ppermute | solution.py:55
  (8 other events, 59.8 us)

commit v3 on v2

--- a/solution.py
+++ b/solution.py
@@ -16,14 +16,16 @@
 ROWS = NB_DEV * BLOCK
 MSG = NB_DEV * RANK + 16
 SLOTS = 2
+SKETCH_STEPS = 4
 PER_CHUNK = 8
 ENTRIES = N_CAND * SLOTS
 ZERO = NB_DEV * N_CAND
-LAST_US = 10
+LAST_US = 0
 f32, bf16, i32 = jnp.float32, jnp.bfloat16, jnp.int32
 VMEM = pl.BlockSpec(memory_space=pltpu.VMEM)
 SMEM = pl.BlockSpec(memory_space=pltpu.SMEM)
 ANY = pl.BlockSpec(memory_space=pl.ANY)
+HBM = pl.BlockSpec(memory_space=pltpu.HBM)
 NT = (((1,), (1,)), ((), ()))
 TN = (((0,), (0,)), ((), ()))
 
@@ -59,38 +61,37 @@
     return lax.ppermute(x, "set", [((me + d) % N_SET, me) for me in range(N_SET)])
 
 
-def sketch_kernel(place, rows, sketch, keep, give, total):
-    step = pl.program_id(0)
-
-    @pl.when(step == 0)
-    def _():
-        total[...] = jnp.zeros_like(total)
-
-    sketched = lax.dot_general(sketch[...], rows[...], NT, preferred_element_type=f32)
-    total[...] += jnp.dot(sketched.astype(bf16), rows[...], preferred_element_type=f32)
-
-    @pl.when(step == pl.num_programs(0) - 1)
-    def _():
-        core = place[1] % 2
-        keep[...] = total[pl.ds(pl.multiple_of(core * HALF, HALF), HALF), :]
-        give[...] = total[pl.ds(pl.multiple_of((1 - core) * HALF, HALF), HALF), :]
+def sketch_kernel(place, rows_hbm, sketch, keep, give, rows, total, sems):
+    copies = []
+    for n in range(SKETCH_STEPS):
+        part = pl.ds(n * (ROWS // SKETCH_STEPS), ROWS // SKETCH_STEPS)
+        copies.append(pltpu.make_async_copy(rows_hbm.at[part], rows.at[part], sems.at[n]))
+        copies[n].start()
+    summed = jnp.zeros((RANK, W), f32)
+    for n in range(SKETCH_STEPS):
+        copies[n].wait()
+        part = rows[n * (ROWS // SKETCH_STEPS) : (n + 1) * (ROWS // SKETCH_STEPS), :]
+        sketched = lax.dot_general(sketch[...], part, NT, preferred_element_type=f32)
+        summed += jnp.dot(sketched.astype(bf16), part, preferred_element_type=f32)
+    total[...] = summed
+    core = place[1] % 2
+    keep[...] = total[pl.ds(pl.multiple_of(core * HALF, HALF), HALF), :]
+    give[...] = total[pl.ds(pl.multiple_of((1 - core) * HALF, HALF), HALF), :]
 
 
 def sketch_call(place, rows, sketch):
-    step = 512
     half = jax.ShapeDtypeStruct((HALF, W), f32)
     return pl.pallas_call(
         sketch_kernel,
-        grid=(ROWS // step,),
         out_shape=(half, half),
-        in_specs=[
-            SMEM,
-            pl.BlockSpec((step, W), lambda i: (i, 0)),
-            pl.BlockSpec((RANK, W), lambda i: (0, 0)),
+        in_specs=[SMEM, HBM, VMEM],
+        out_specs=(VMEM, VMEM),
+        scratch_shapes=[
+            pltpu.VMEM((ROWS, W), bf16),
+            pltpu.VMEM((RANK, W), f32),
+            pltpu.SemaphoreType.DMA((SKETCH_STEPS,)),
         ],
-        out_specs=(pl.BlockSpec((HALF, W), lambda i: (0, 0)),) * 2,
-        scratch_shapes=[pltpu.VMEM((RANK, W), f32)],
-        compiler_params=params(62),
+        compiler_params=params(52),
         name="sketch",
     )(place, rows, sketch)
 
@@ -168,10 +169,10 @@
     return pl.pallas_call(
         factor_kernel,
         out_shape=jax.ShapeDtypeStruct((MSG, BLOCK), bf16),
-        in_specs=[SMEM, VMEM, VMEM, ANY],
+        in_specs=[SMEM, VMEM, VMEM, HBM],
         out_specs=VMEM,
         scratch_shapes=[pltpu.VMEM((ROWS, W), bf16), pltpu.SemaphoreType.DMA],
-        compiler_params=params(),
+        compiler_params=params(52),
         name="factor",
     )(place, own, other, rows)
 
@@ -192,24 +193,46 @@
 
 
 def join_kernel(*refs):
-    parts, out, sems = refs[:4], refs[-2], refs[-1]
-    copies = [pltpu.make_async_copy(parts[k], out.at[k], sems.at[k]) for k in range(4)]
-    for copy in copies:
-        copy.start()
-    for copy in copies:
-        copy.wait()
+    for k in range(4):
+        refs[-1][k * MSG : (k + 1) * MSG, :] = refs[k][...]
 
 
 def join_call(parts, *after):
     return pl.pallas_call(
         join_kernel,
-        out_shape=jax.ShapeDtypeStruct((4, MSG, BLOCK), bf16),
-        in_specs=[ANY] * (4 + len(after)),
-        out_specs=ANY,
-        scratch_shapes=[pltpu.SemaphoreType.DMA((4,))],
+        out_shape=jax.ShapeDtypeStruct((4 * MSG, BLOCK), bf16),
+        in_specs=[VMEM] * 4 + [ANY] * len(after),
+        out_specs=VMEM,
         compiler_params=params(),
         name="join",
     )(*parts, *after)
+
+
+def put_call(whole, part, n):
+    def kernel(*refs):
+        out, sem = refs[-2:]
+        copy = pltpu.make_async_copy(refs[-3], out.at[pl.ds(n * 4 * MSG, 4 * MSG)], sem)
+        copy.start()
+        copy.wait()
+
+    first = whole is None
+    return pl.pallas_call(
+        kernel,
+        out_shape=jax.ShapeDtypeStruct((N_CAND * MSG, BLOCK), bf16),
+        in_specs=[ANY] * (1 if first else 2),
+        out_specs=ANY,
+        input_output_aliases={} if first else {0: 0},
+        scratch_shapes=[pltpu.SemaphoreType.DMA],
+        compiler_params=params(),
+        name="put",
+    )(*([part] if first else [whole, part]))
+
+
+def put_all(parts):
+    whole = None
+    for n, part in parts:
+        whole = put_call(whole, part, n)
+    return whole
 
 
 def plan_kernel(place, own, other, *refs):
@@ -247,6 +270,7 @@
     spots = lax.broadcasted_iota(i32, (n, 128), 1).astype(f32)
     spot = lax.broadcasted_iota(i32, (1, 128), 1)
     line = lax.broadcasted_iota(i32, (8, 128), 0)
+    lane = lax.broadcasted_iota(i32, (8, 128), 1)
     row = lax.broadcasted_iota(i32, (16, n), 0)
     for gr in range(N_SET):
         t_down, t_across = target_down[:, gr : gr + 1], target[gr : gr + 1, :]
@@ -257,14 +281,22 @@
         chunks = (count.astype(i32) + (PER_CHUNK - 1)) // PER_CHUNK
         chunks = jnp.where(spot < NT_DEV, chunks, 0).astype(f32)
         start = jnp.sum(jnp.where(spots < t_down, chunks, 0.0), axis=1, keepdims=True)
+        end = jnp.sum(jnp.where(lane <= line, chunks, 0.0), axis=1, keepdims=True)
+        target_of = jnp.sum(jnp.where(end <= lane.astype(f32), 1.0, 0.0), axis=0, keepdims=True)
+        target_of = jnp.minimum(target_of, NT_DEV - 1)
+        pieces = jnp.sum(chunks, axis=1, keepdims=True)
         place_of = jnp.where(t_down < NT_DEV, start * PER_CHUNK + rank, 1000.0)
         chosen = jnp.where(place_of == spots, 1.0, 0.0).astype(bf16)
         both = jnp.where(
             row == 0, left[gr : gr + 1, :], jnp.where(row == 1, right[gr : gr + 1, :], 0.0)
         ).astype(bf16)
         lists = jnp.dot(both, chosen, preferred_element_type=f32)[0:8, :]
-        lists = jnp.where(line == 0, lists + ZERO, jnp.where(line == 2, chunks, lists))
-        outs[gr][...] = lists.astype(i32)
+        lists = jnp.where(line == 0, lists + ZERO, lists)
+        lists = jnp.where(line == 2, target_of, jnp.where(line == 3, pieces, lists))
+        lists = lists.astype(i32)
+        begins = (lists // NB_DEV) % N_CAND * MSG + lists % NB_DEV * RANK
+        outs[gr][0:4, :] = lists[0:4, :]
+        outs[gr][4:6, :] = begins[0:2, :]
 
 
 def plan_call(place, own, other, *after):
@@ -279,135 +311,109 @@
     )(place, own, other, *after)
 
 
-def collect(pieces, factors, scales, sems):
-    copies = [
-        pltpu.make_async_copy(piece, factors.at[pl.ds(4 * n, 4)], sems.at[n])
-        for n, piece in enumerate(pieces)
-    ]
-    for copy in copies:
-        copy.start()
-    for copy in copies:
-        copy.wait()
+def spread(factors, scales):
     for p in range(N_CAND):
-        scales[p * NB_DEV : (p + 1) * NB_DEV, :] = factors[p, NB_DEV * RANK :, 0:128].astype(f32)[
-            0:NB_DEV, :
-        ]
+        rows = factors[p * MSG + NB_DEV * RANK : (p + 1) * MSG, 0:128].astype(f32)
+        scales[p * NB_DEV : (p + 1) * NB_DEV, :] = rows[0:NB_DEV, :]
     scales[ZERO : ZERO + 8, :] = jnp.zeros((8, 128), f32)
 
 
-def block_at(factors, b):
-    at = pl.multiple_of((b % NB_DEV) * RANK, RANK)
-    return factors.at[(b // NB_DEV) % N_CAND, pl.ds(at, RANK), :]
-
-
-def expand(pairs, t, factors, scales, lefts, rights, start, total):
-    def chunk(q, carry):
+def block_at(factors, begin):
+    return factors[pl.ds(pl.multiple_of(begin, 16), RANK), :]
+
+
+def expand(pairs, factors, scales, lefts, rights, totals):
+    def chunk(q, side):
         for k in range(PER_CHUNK):
-            spot = start + q * PER_CHUNK + k
+            spot = q * PER_CHUNK + k
             left, right = pairs[0, spot], pairs[1, spot]
             weight = scales[pl.ds(left, 1), :] * scales[pl.ds(right, 1), :]
-            weight = weight.astype(bf16).astype(f32)
+            weight = jnp.broadcast_to(weight, (RANK, 128)).astype(bf16)
             weight = jnp.concatenate([weight, weight], axis=1)
             here = slice(k * RANK, (k + 1) * RANK)
-            lefts[here, :] = (block_at(factors, left)[...].astype(f32) * weight).astype(bf16)
-            rights[here, :] = block_at(factors, right)[...]
-        total[...] += lax.dot_general(lefts[...], rights[...], TN, preferred_element_type=f32)
+            lefts[side, here, :] = block_at(factors, pairs[4, spot]) * weight
+            rights[side, here, :] = block_at(factors, pairs[5, spot])
+
+    def couple(n, carry):
+        chunk(2 * n, 0)
+        chunk(2 * n + 1, 1)
+        terms = [
+            lax.dot_general(lefts[side], rights[side], TN, preferred_element_type=f32)
+            for side in range(2)
+        ]
+        for side in range(2):
+            t = pairs[2, 2 * n + side]
+            totals[t] += terms[side]
         return carry
 
-    total[...] = jnp.zeros_like(total)
-    chunks = pairs[2, t]
-    lax.fori_loop(0, chunks, chunk, 0)
-    return start + chunks * PER_CHUNK
+    totals[...] = jnp.zeros_like(totals)
+    lax.fori_loop(0, (pairs[3, 0] + 1) // 2, couple, 0)
 
 
 WORK = [
-    pltpu.VMEM((N_CAND, MSG, BLOCK), bf16),
     pltpu.VMEM((ZERO + 8, 128), f32),
-    pltpu.VMEM((RANK * PER_CHUNK, BLOCK), bf16),
-    pltpu.VMEM((RANK * PER_CHUNK, BLOCK), bf16),
-    pltpu.VMEM((BLOCK, BLOCK), f32),
-    pltpu.SemaphoreType.DMA((8,)),
+    pltpu.VMEM((2, RANK * PER_CHUNK, BLOCK), bf16),
+    pltpu.VMEM((2, RANK * PER_CHUNK, BLOCK), bf16),
+    pltpu.VMEM((NT_DEV, BLOCK, BLOCK), f32),
 ]
 
 
-def send_call(next_list, last_list, pieces, cuts):
-    n = len(cuts) - 1
-
-    def kernel(next_list, last_list, *refs):
-        pieces, outs, work = refs[:8], refs[8 : 8 + 2 * n], refs[8 + 2 * n :]
-        factors, scales, lefts, rights, total, sems = work
-        collect(pieces, factors, scales, sems)
-        for side, pairs in enumerate((next_list, last_list)):
-            start = 0
-            for t in range(cuts[0]):
-                start = start + pairs[2, t] * PER_CHUNK
-            for part in range(n):
-                for t in range(cuts[part], cuts[part + 1]):
-                    start = expand(pairs, t, factors, scales, lefts, rights, start, total)
-                    outs[2 * part + side][t - cuts[part]] = total[...].astype(bf16)
-
-    shapes = [
-        jax.ShapeDtypeStruct((cuts[part + 1] - cuts[part], BLOCK, BLOCK), bf16)
-        for part in range(n)
-        for side in range(2)
-    ]
+def send_call(next_list, last_list, factors):
+    def kernel(next_list, last_list, factors, to_next, to_last, scales, lefts, rights, totals):
+        spread(factors, scales)
+        for pairs, out in ((next_list, to_next), (last_list, to_last)):
+            expand(pairs, factors, scales, lefts, rights, totals)
+            out[...] = totals[...].astype(bf16)
+
+    out = jax.ShapeDtypeStruct((NT_DEV, BLOCK, BLOCK), bf16)
     return pl.pallas_call(
         kernel,
-        out_shape=shapes,
-        in_specs=[SMEM, SMEM] + [ANY] * 8,
-        out_specs=[VMEM] * (2 * n),
+        out_shape=(out, out),
+        in_specs=[SMEM, SMEM, VMEM],
+        out_specs=(VMEM, VMEM),
         scratch_shapes=WORK,
         compiler_params=params(),
         name="send_pairs",
-    )(next_list, last_list, *pieces)
-
-
-def keep_call(pairs, base, pieces, *after):
-    def kernel(pairs, base, *refs):
-        pieces, (out, *work) = refs[:8], refs[8 + len(after) :]
-        factors, scales, lefts, rights, total, sems = work
-        collect(pieces, factors, scales, sems)
-        start = 0
-        for t in range(NT_DEV):
-            start = expand(pairs, t, factors, scales, lefts, rights, start, total)
-            out[t] = base[t] - total[...]
+    )(next_list, last_list, factors)
+
+
+def keep_call(pairs, base, factors, *after):
+    def kernel(pairs, base, factors, *refs):
+        out, scales, lefts, rights, totals = refs[len(after) :]
+        spread(factors, scales)
+        expand(pairs, factors, scales, lefts, rights, totals)
+        out[...] = base[...] - totals[...]
 
     return pl.pallas_call(
         kernel,
         out_shape=jax.ShapeDtypeStruct((NT_DEV, BLOCK, BLOCK), f32),
-        in_specs=[SMEM, VMEM] + [ANY] * (8 + len(after)),
+        in_specs=[SMEM, VMEM, VMEM] + [ANY] * len(after),
         out_specs=VMEM,
         scratch_shapes=WORK,
         compiler_params=params(),
         name="keep_pairs",
-    )(pairs, base, *pieces, *after)
-
-
-def final_call(base, parts, cuts):
-    def kernel(base, *refs):
-        parts, out, sems = refs[: len(parts_in)], refs[-2], refs[-1]
+    )(pairs, base, factors, *after)
+
+
+def final_call(base, one, two):
+    def kernel(base, one, two, out, sems):
         copies = []
-        for n in range(len(cuts) - 1):
-            one, two = parts[2 * n], parts[2 * n + 1]
-            for t in range(cuts[n], cuts[n + 1]):
-                k = t - cuts[n]
-                base[t] = base[t] - (one[k].astype(f32) + two[k].astype(f32))
-                copy = pltpu.make_async_copy(base.at[t], out.at[t], sems.at[t])
-                copy.start()
-                copies.append(copy)
+        for t in range(NT_DEV):
+            base[t] = base[t] - (one[t].astype(f32) + two[t].astype(f32))
+            copies.append(pltpu.make_async_copy(base.at[t], out.at[t], sems.at[t]))
+            copies[t].start()
         for copy in copies:
             copy.wait()
 
-    parts_in = parts
     return pl.pallas_call(
         kernel,
         out_shape=jax.ShapeDtypeStruct((NT_DEV, BLOCK, BLOCK), f32),
-        in_specs=[VMEM] * (1 + len(parts)),
+        in_specs=[VMEM] * 3,
         out_specs=ANY,
         scratch_shapes=[pltpu.SemaphoreType.DMA((NT_DEV,))],
         compiler_params=params(),
         name="final",
-    )(base, *parts)
+    )(base, one, two)
 
 
 def per_device(panel_rows, sketch, accumulator, left_block, right_block, target_slot, slot_valid):
@@ -429,23 +435,32 @@
     other = from_core(own)
 
     mine = factor_call(place, own, other, rows)
-    line = join_call([mine] + [from_cand(mine, 0, k) for k in (1, 2, 3)])
-    here = [line] + [from_cand(line, 1, k) for k in (1, 2, 3)]
-    pieces = here + [from_core(x) for x in here]
-
-    far_line = join_call([from_cand(mine, 0, k, far=True) for k in range(4)])
-    own_list, next_list, far_list, last_list = plan_call(place, own, other, line)
+    far = from_set(mine, 2)
+    parts = [mine] + [from_cand(mine, 0, k) for k in (1, 2, 3)]
+    line = join_call(parts)
+    opposite = from_cand(line, 1, 2)
+    far_line = join_call([far] + [from_cand(far, 0, k) for k in (1, 2, 3)])
+    own_list, next_list, far_list, last_list = plan_call(place, own, other, far_line)
     far_list = from_set(far_list, 2)
-
-    cuts = (0, 8)
-    to_next, to_last = send_call(next_list, last_list, pieces, cuts)
+    line = join_call(parts, far_line)
+    opposite = touch_call(opposite, 0, far_list)
+    here = [line, from_cand(line, 1, 1), opposite, from_cand(line, 1, 3)]
+    there = [from_core(x) for x in here]
+    factors = put_all(
+        [p for k in range(4) for p in ((k, here[k]), (4 + k, there[k]))]
+    )
+
+    to_next, to_last = send_call(next_list, last_list, factors)
     arrived = [touch_call(x, LAST_US) for x in (from_set(to_next, 3), from_set(to_last, 1))]
 
     far_here = [far_line] + [from_cand(far_line, 1, k) for k in (1, 2, 3)]
-    far_pieces = far_here + [from_core(x) for x in far_here]
-    base = keep_call(own_list, accumulator[0], pieces, to_next)
-    base = keep_call(far_list, base, far_pieces)
-    base = final_call(base, arrived, cuts)
+    far_there = [from_core(x) for x in far_here]
+    far_factors = put_all(
+        [p for k in range(4) for p in ((k, far_here[k]), (4 + k, far_there[k]))]
+    )
+    base = keep_call(own_list, accumulator[0], factors, to_next)
+    base = keep_call(far_list, base, far_factors)
+    base = final_call(base, *arrived)
     return base[None]
 
 

time: 111 us -> 95.3 us (0.86)
  Pallas kernels: 29.5 us -> 19.4 us
  starting transfers between devices: 34.8 us -> 27.9 us
  waiting for transfers between devices: 42 us -> 43.7 us
    ppermute x4 -> x0, waiting for transfers between devices: 9.19 us -> none  [from_cand(): return lax.ppermute(x, ('set', 'cand'), pairs)]
    ppermute x15 -> x18, waiting for transfers between devices: 17.7 us -> 26.3 us  [from_cand(): return lax.ppermute(x, 'cand', pairs)]
    ppermute x4 -> x0, starting transfers between devices: 8.27 us -> none  [from_cand(): return lax.ppermute(x, ('set', 'cand'), pairs)]
    pallas_call x4 -> x21, Pallas kernels: 13.4 us -> 7.78 us  [the longest x1 3.18 us: send_call(): pl.pallas_call(kernel, out_shape=(out, out), in_specs=[SMEM, SMEM, VMEM],...]
    pallas_call x2, Pallas kernels: 8.85 us -> 4.54 us  [keep_call(): pl.pallas_call(kernel, out_shape=jax.ShapeDtypeStruct((NT_DEV, BLOCK, BLO...]
    ppermute x3 -> x4, waiting for transfers between devices: 12.5 us -> 15.7 us  [from_set(): lax.ppermute(x, 'set', [((me + d) % N_SET, me) for me in range(N_SET)])]
    ppermute x15 -> x18, starting transfers between devices: 20.3 us -> 22.5 us  [from_cand(): return lax.ppermute(x, 'cand', pairs)]
    ppermute x3 -> x4, starting transfers between devices: 5.01 us -> 4.67 us  [from_set(): lax.ppermute(x, 'set', [((me + d) % N_SET, me) for me in range(N_SET)])]
  transfers between devices with their start and end apart: 32 -> 32, of which waited for: 19 -> 20; matrix products, arithmetic and copies ran while one was open for 0% -> 1% of each run, Pallas kernels for 17% -> 11%
where the time goes in v3:
time: 95.3 us; the launch traced here: 94.5 us
  waiting for transfers between devices  43.7 us (46%)
  starting transfers between devices  27.9 us (29%)
  Pallas kernels  19.4 us (20%)
  local copies, waits for them, and re-layouts  2.25 us (2%)
    ppermute x18, waiting for transfers between devices, from_cand(): return lax.ppermute(x, 'cand', pairs)  26.3 us
    ppermute x18, starting transfers between devices, from_cand(): return lax.ppermute(x, 'cand', pairs)  22.5 us
    ppermute x4, waiting for transfers between devices, from_set(): lax.ppermute(x, 'set', [((me + d) % N_SET, me) for me in range(N_SET)])  15.7 us
    ppermute x4, starting transfers between devices, from_set(): lax.ppermute(x, 'set', [((me + d) % N_SET, me) for me in range(N_SET)])  4.67 us
    pallas_call x2, Pallas kernels, keep_call(): pl.pallas_call(kernel, out_shape=jax.ShapeDtypeStruct((NT_DEV, BLOCK, BLO...  4.54 us
    pallas_call x1, Pallas kernels, factor_call(): pl.pallas_call(factor_kernel, out_shape=jax.ShapeDtypeStruct((MSG, BLOCK)...  4.42 us
    pallas_call x1, Pallas kernels, send_call(): pl.pallas_call(kernel, out_shape=(out, out), in_specs=[SMEM, SMEM, VMEM],...  3.18 us
    pallas_call x1, Pallas kernels, sketch_call(): pl.pallas_call(sketch_kernel, out_shape=(half, half), in_specs=[SMEM, HBM...  3.05 us
  transfers between devices with their start and end apart: 32, of which 20 were waited for; matrix products, arithmetic and copies ran while one was open for 1% of the time, Pallas kernels for 11%

profile of v3, /device:TPU:6, one launch (start us, length us, event | category | flops | bytes accessed | tf_op | source)
XLA Modules:
  0.0 94.5 jit_solution(3832041435276054992)
XLA Ops:
  0.8 3.0 %sketch.1 = (f32[16,512]{1,0:T(8,128)S(1)}, f32[16,512]{1,0:T(8,128)S(1)}) custom-call(s32[2]{0:T(128)S(1)} %pad_add_fusion.place.refs_0_, bf16[2048,512]{1,0:T(8,128)(2,1)} %bitcast.22, bf16[32,512]{1,0:T(8,128)(2,1)S(1)} %bitcast.21), custom_call_target="tpu_custom_call" | custom-call | tf_op jit(solution)/shard_map/sketch/pallas_call | solution.py:84
  5.2 3.0 %collective-permute-start.1 = (f32[24,512]{1,0:T(8,128)S(1)}, f32[24,512]{1,0:T(8,128)S(1)}, u32[]{:S(2)}, u32[]{:S(2)}) collective-permute-start(f32[24,512]{1,0:T(8,128)S(1)} %sum_core.1.r0), channel_id=1, source_target_pairs={{2,0},{9,1},{4,2},{11,3},{6,4},{13,5},{0,6},{15,7},{10,8},{17,9},{... | collective-permute-start | bytes 147464 | tf_op jit(solution)/shard_map/ppermute | solution.py:47
  10.0 3.9 %collective-permute-done.2.r2 = f32[24,512]{1,0:T(8,128)S(1)} collective-permute-done((f32[24,512]{1,0:T(8,128)S(1)}, f32[24,512]{1,0:T(8,128)S(1)}, u32[]{:S(2)}, u32[]{:S(2)}) %collective-permute-start.2) | collective-permute-done | bytes 49184 | tf_op jit(solution)/shard_map/ppermute | solution.py:47
  14.3 4.1 %collective-permute-start.4 = (f32[24,512]{1,0:T(8,128)S(1)}, f32[24,512]{1,0:T(8,128)S(1)}, u32[]{:S(2)}, u32[]{:S(2)}) collective-permute-start(f32[24,512]{1,0:T(8,128)S(1)} %sum_first.1.r0), channel_id=1, source_target_pairs={{8,0},{3,1},{10,2},{5,3},{12,4},{7,5},{14,6},{1,7},{16,8},{11,9},{... | collective-permute-start | bytes 147464 | tf_op jit(solution)/shard_map/ppermute | solution.py:47
  18.4 1.3 %collective-permute-start.6 = (f32[24,512]{1,0:T(8,128)S(1)}, f32[24,512]{1,0:T(8,128)S(1)}, u32[]{:S(2)}, u32[]{:S(2)}) collective-permute-start(f32[24,512]{1,0:T(8,128)S(1)} %sum_first.1.r0), channel_id=1, source_target_pairs={{24,0},{7,1},{26,2},{1,3},{28,4},{3,5},{30,6},{5,7},{0,8},{15,9},{... | collective-permute-start | bytes 147464 | tf_op jit(solution)/shard_map/ppermute | solution.py:47
  20.2 3.9 %collective-permute-done.5.r2 = f32[24,512]{1,0:T(8,128)S(1)} collective-permute-done((f32[24,512]{1,0:T(8,128)S(1)}, f32[24,512]{1,0:T(8,128)S(1)}, u32[]{:S(2)}, u32[]{:S(2)}) %collective-permute-start.5) | collective-permute-done | bytes 49184 | tf_op jit(solution)/shard_map/ppermute | solution.py:47
  24.4 1.3 %collective-permute-done.7.other.refs_2_ = f32[48,512]{1,0:T(8,128)S(1)} collective-permute-done((f32[48,512]{1,0:T(8,128)S(1)}, f32[48,512]{1,0:T(8,128)S(1)}, u32[]{:S(2)}, u32[]{:S(2)}) %collective-permute-start.7) | collective-permute-done | bytes 98336 | tf_op jit(solution)/shard_map/ppermute | solution.py:57
  25.7 4.4 %factor.1.refs_0_ = bf16[272,256]{1,0:T(8,128)(2,1)S(1)} custom-call(s32[2]{0:T(128)S(1)} %pad_add_fusion.place.refs_0_, f32[48,512]{1,0:T(8,128)S(1)} %sum_second.1.own.refs_1_, f32[48,512]{1,0:T(8,128)S(1)} %collective-permute-done.7.other.refs_2_, bf16[2048,512]{1,0:T(8,128)(2,1)} %bitcast.23), custom_call_target="tpu_custom_call" | custom-call | tf_op jit(solution)/shard_map/factor/pallas_call | solution.py:169
  30.1 1.5 %collective-permute-start.8 = (bf16[272,256]{1,0:T(8,128)(2,1)S(1)}, bf16[272,256]{1,0:T(8,128)(2,1)S(1)}, u32[]{:S(2)}, u32[]{:S(2)}) collective-permute-start(bf16[272,256]{1,0:T(8,128)(2,1)S(1)} %factor.1.refs_0_), channel_id=1, source_target_pairs={{64,0},{96,32},{0,64},{32,96},{65,1},{97,33},{1,65},{33,97},{66,2}... | collective-permute-start | bytes 417800 | tf_op jit(solution)/shard_map/ppermute | solution.py:61
  33.2 1.3 %collective-permute-start.15 = (bf16[272,256]{1,0:T(8,128)(2,1)S(1)}, bf16[272,256]{1,0:T(8,128)(2,1)S(1)}, u32[]{:S(2)}, u32[]{:S(2)}) collective-permute-start(bf16[272,256]{1,0:T(8,128)(2,1)S(1)} %factor.1.refs_0_), channel_id=1, source_target_pairs={{6,0},{25,1},{0,2},{27,3},{2,4},{29,5},{4,6},{31,7},{14,8},{1,9},{... | collective-permute-start | bytes 417800 | tf_op jit(solution)/shard_map/ppermute | solution.py:47
  34.5 2.9 %collective-permute-done.8.refs_0_ = bf16[272,256]{1,0:T(8,128)(2,1)S(1)} collective-permute-done((bf16[272,256]{1,0:T(8,128)(2,1)S(1)}, bf16[272,256]{1,0:T(8,128)(2,1)S(1)}, u32[]{:S(2)}, u32[]{:S(2)}) %collective-permute-start.8) | collective-permute-done | bytes 139296 | tf_op jit(solution)/shard_map/ppermute | solution.py:61
  38.0 1.1 %collective-permute-start.10 = (bf16[272,256]{1,0:T(8,128)(2,1)S(1)}, bf16[272,256]{1,0:T(8,128)(2,1)S(1)}, u32[]{:S(2)}, u32[]{:S(2)}) collective-permute-start(bf16[272,256]{1,0:T(8,128)(2,1)S(1)} %collective-permute-done.8.refs_0_), channel_id=1, source_target_pairs={{4,0},{17,1},{6,2},{19,3},{0,4},{21,5},{2,6},{23,7},{12,8},{25,9},... | collective-permute-start | bytes 417800 | tf_op jit(solution)/shard_map/ppermute | solution.py:47
  39.1 1.3 %collective-permute-start.11 = (bf16[272,256]{1,0:T(8,128)(2,1)S(1)}, bf16[272,256]{1,0:T(8,128)(2,1)S(1)}, u32[]{:S(2)}, u32[]{:S(2)}) collective-permute-start(bf16[272,256]{1,0:T(8,128)(2,1)S(1)} %collective-permute-done.8.refs_0_), channel_id=1, source_target_pairs={{6,0},{25,1},{0,2},{27,3},{2,4},{29,5},{4,6},{31,7},{14,8},{1,9},{... | collective-permute-start | bytes 417800 | tf_op jit(solution)/shard_map/ppermute | solution.py:47
  40.4 1.9 %collective-permute-start.19 = (bf16[1088,256]{1,0:T(8,128)(2,1)S(1)}, bf16[1088,256]{1,0:T(8,128)(2,1)S(1)}, u32[]{:S(2)}, u32[]{:S(2)}) collective-permute-start(bf16[1088,256]{1,0:T(8,128)(2,1)S(1)} %join.5), channel_id=1, source_target_pairs={{16,0},{5,1},{18,2},{7,3},{20,4},{1,5},{22,6},{3,7},{24,8},{13,9},... | collective-permute-start | bytes 1671176 | tf_op jit(solution)/shard_map/ppermute | solution.py:47
  42.3 1.4 %collective-permute-done.9.refs_1_ = bf16[272,256]{1,0:T(8,128)(2,1)S(1)} collective-permute-done((bf16[272,256]{1,0:T(8,128)(2,1)S(1)}, bf16[272,256]{1,0:T(8,128)(2,1)S(1)}, u32[]{:S(2)}, u32[]{:S(2)}) %collective-permute-start.9) | collective-permute-done | bytes 139296 | tf_op jit(solution)/shard_map/ppermute | solution.py:47
  43.7 2.1 %collective-permute-done.10.refs_2_ = bf16[272,256]{1,0:T(8,128)(2,1)S(1)} collective-permute-done((bf16[272,256]{1,0:T(8,128)(2,1)S(1)}, bf16[272,256]{1,0:T(8,128)(2,1)S(1)}, u32[]{:S(2)}, u32[]{:S(2)}) %collective-permute-start.10) | collective-permute-done | bytes 139296 | tf_op jit(solution)/shard_map/ppermute | solution.py:47
  45.8 2.8 %collective-permute-done.11.refs_3_ = bf16[272,256]{1,0:T(8,128)(2,1)S(1)} collective-permute-done((bf16[272,256]{1,0:T(8,128)(2,1)S(1)}, bf16[272,256]{1,0:T(8,128)(2,1)S(1)}, u32[]{:S(2)}, u32[]{:S(2)}) %collective-permute-start.11) | collective-permute-done | bytes 139296 | tf_op jit(solution)/shard_map/ppermute | solution.py:47
  49.0 1.9 %collective-permute-start.21 = (bf16[1088,256]{1,0:T(8,128)(2,1)S(1)}, bf16[1088,256]{1,0:T(8,128)(2,1)S(1)}, u32[]{:S(2)}, u32[]{:S(2)}) collective-permute-start(bf16[1088,256]{1,0:T(8,128)(2,1)S(1)} %join.4.refs_0_), channel_id=1, source_target_pairs={{24,0},{7,1},{26,2},{1,3},{28,4},{3,5},{30,6},{5,7},{0,8},{15,9},{... | collective-permute-start | bytes 1671176 | tf_op jit(solution)/shard_map/ppermute | solution.py:47
  50.8 1.2 %plan.1 = (s32[8,128]{1,0:T(8,128)S(1)}, s32[8,128]{1,0:T(8,128)S(1)}, s32[8,128]{1,0:T(8,128)S(1)}, s32[8,128]{1,0:T(8,128)S(1)}) custom-call(s32[2]{0:T(128)S(1)} %pad_add_fusion.place.refs_0_, f32[48,512]{1,0:T(8,128)S(1)} %sum_second.1.own.refs_1_, f32[48,512]{1,0:T(8,128)S(1)} %collective-permute-done.7.other.refs_2_, ...), custom_call_target="tpu_custom_call" | custom-call | tf_op jit(solution)/shard_map/plan/pallas_call | solution.py:303
  53.0 4.3 %collective-permute-done.12.refs_1_.pairs = s32[8,128]{1,0:T(8,128)S(1)} collective-permute-done((s32[8,128]{1,0:T(8,128)S(1)}, s32[8,128]{1,0:T(8,128)S(1)}, u32[]{:S(2)}, u32[]{:S(2)}) %collective-permute-start.12) | collective-permute-done | bytes 4128 | tf_op jit(solution)/shard_map/ppermute | solution.py:61
  58.3 1.4 %collective-permute-done.21.refs_1_ = bf16[1088,256]{1,0:T(8,128)(2,1)S(1)} collective-permute-done((bf16[1088,256]{1,0:T(8,128)(2,1)S(1)}, bf16[1088,256]{1,0:T(8,128)(2,1)S(1)}, u32[]{:S(2)}, u32[]{:S(2)}) %collective-permute-start.21) | collective-permute-done | bytes 557088 | tf_op jit(solution)/shard_map/ppermute | solution.py:47
  60.6 2.3 %collective-permute-start.26 = (bf16[1088,256]{1,0:T(8,128)(2,1)S(1)}, bf16[1088,256]{1,0:T(8,128)(2,1)S(1)}, u32[]{:S(2)}, u32[]{:S(2)}) collective-permute-start(bf16[1088,256]{1,0:T(8,128)(2,1)S(1)} %join.3.refs_3_.refs_4_.refs_0_), channel_id=1, source_target_pairs={{16,0},{5,1},{18,2},{7,3},{20,4},{1,5},{22,6},{3,7},{24,8},{13,9},... | collective-permute-start | bytes 1671176 | tf_op jit(solution)/shard_map/ppermute | solution.py:47
  63.8 3.2 %send_pairs.1 = (bf16[8,256,256]{2,1,0:T(8,128)(2,1)S(1)}, bf16[8,256,256]{2,1,0:T(8,128)(2,1)S(1)}) custom-call(s32[8,128]{1,0:T(8,128)S(1)} %get-tuple-element.17.next_list, s32[8,128]{1,0:T(8,128)S(1)} %get-tuple-element.18.last_list, bf16[8704,256]{1,0:T(8,128)(2,1)S(1)} %put.23.factors), custom_call_target="tpu_custom_call" | custom-call | tf_op jit(solution)/shard_map/send_pairs/pallas_call | solution.py:369
  66.9 1.2 %collective-permute-start.30 = (bf16[8,256,256]{2,1,0:T(8,128)(2,1)S(1)}, bf16[8,256,256]{2,1,0:T(8,128)(2,1)S(1)}, u32[]{:S(2)}, u32[]{:S(2)}) collective-permute-start(bf16[8,256,256]{2,1,0:T(8,128)(2,1)S(1)} %get-tuple-element.19.refs_0_), channel_id=1, source_target_pairs={{96,0},{0,32},{32,64},{64,96},{97,1},{1,33},{33,65},{65,97},{98,2}... | collective-permute-start | bytes 3145736 | tf_op jit(solution)/shard_map/ppermute | solution.py:61
  69.8 2.0 %collective-permute-done.26.refs_1_ = bf16[1088,256]{1,0:T(8,128)(2,1)S(1)} collective-permute-done((bf16[1088,256]{1,0:T(8,128)(2,1)S(1)}, bf16[1088,256]{1,0:T(8,128)(2,1)S(1)}, u32[]{:S(2)}, u32[]{:S(2)}) %collective-permute-start.26) | collective-permute-done | bytes 557088 | tf_op jit(solution)/shard_map/ppermute | solution.py:47
  71.7 5.9 %collective-permute-done.28.refs_1_ = bf16[1088,256]{1,0:T(8,128)(2,1)S(1)} collective-permute-done((bf16[1088,256]{1,0:T(8,128)(2,1)S(1)}, bf16[1088,256]{1,0:T(8,128)(2,1)S(1)}, u32[]{:S(2)}, u32[]{:S(2)}) %collective-permute-start.28) | collective-permute-done | bytes 557088 | tf_op jit(solution)/shard_map/ppermute | solution.py:47
  77.9 1.5 %copy-done = f32[1,8,256,256]{3,2,1,0:T(8,128)S(1)} copy-done((f32[1,8,256,256]{3,2,1,0:T(8,128)S(1)}, f32[1,8,256,256]{3,2,1,0:T(8,128)}, u32[]{:S(2)}) %copy-start) | copy-done | bytes 2097176
  79.4 2.3 %keep_pairs.2.base = f32[8,256,256]{2,1,0:T(8,128)S(1)} custom-call(s32[8,128]{1,0:T(8,128)S(1)} %get-tuple-element.16.pairs, f32[8,256,256]{2,1,0:T(8,128)S(1)} %bitcast.20, bf16[8704,256]{1,0:T(8,128)(2,1)S(1)} %put.23.factors, bf16[8,256,256]{2,1,0:T(8,128)(2,1)S(1)} %get-tuple-element.19.refs_0_), custom_call_target="tpu_custom_call" | custom-call | tf_op jit(solution)/shard_map/keep_pairs/pallas_call | solution.py:387
  82.2 2.3 %keep_pairs.3.base = f32[8,256,256]{2,1,0:T(8,128)S(1)} custom-call(s32[8,128]{1,0:T(8,128)S(1)} %collective-permute-done.12.refs_1_.pairs, f32[8,256,256]{2,1,0:T(8,128)S(1)} %keep_pairs.2.base, bf16[8704,256]{1,0:T(8,128)(2,1)S(1)} %put.31.factors), custom_call_target="tpu_custom_call" | custom-call | tf_op jit(solution)/shard_map/keep_pairs/pallas_call | solution.py:387
  84.5 6.8 %collective-permute-done.30.refs_0_ = bf16[8,256,256]{2,1,0:T(8,128)(2,1)S(1)} collective-permute-done((bf16[8,256,256]{2,1,0:T(8,128)(2,1)S(1)}, bf16[8,256,256]{2,1,0:T(8,128)(2,1)S(1)}, u32[]{:S(2)}, u32[]{:S(2)}) %collective-permute-start.30) | collective-permute-done | bytes 1048608 | tf_op jit(solution)/shard_map/ppermute | solution.py:61
  91.2 1.7 %collective-permute-done.31.refs_0_ = bf16[8,256,256]{2,1,0:T(8,128)(2,1)S(1)} collective-permute-done((bf16[8,256,256]{2,1,0:T(8,128)(2,1)S(1)}, bf16[8,256,256]{2,1,0:T(8,128)(2,1)S(1)}, u32[]{:S(2)}, u32[]{:S(2)}) %collective-permute-start.31) | collective-permute-done | bytes 1048608 | tf_op jit(solution)/shard_map/ppermute | solution.py:61
  93.0 1.4 %final.1 = f32[8,256,256]{2,1,0:T(8,128)} custom-call(f32[8,256,256]{2,1,0:T(8,128)S(1)} %keep_pairs.3.base, bf16[8,256,256]{2,1,0:T(8,128)(2,1)S(1)} %touch.4.one, bf16[8,256,256]{2,1,0:T(8,128)(2,1)S(1)} %touch.5.two), custom_call_target="tpu_custom_call" | custom-call | tf_op jit(solution)/shard_map/final/pallas_call | solution.py:408
  (70 shorter events, 13.6 us)
Async XLA Ops:
  3.9 1.3 %collective-permute-start = (f32[16,512]{1,0:T(8,128)S(1)}, f32[16,512]{1,0:T(8,128)S(1)}, u32[]{:S(2)}, u32[]{:S(2)}) collective-permute-start(f32[16,512]{1,0:T(8,128)S(1)} %get-tuple-element.14), channel_id=1, source_target_pairs={{1,0},{0,1},{3,2},{2,3},{5,4},{4,5},{7,6},{6,7},{9,8},{8,9},{11,10... | collective-permute-start | bytes 98312 | tf_op jit(solution)/shard_map/ppermute | solution.py:57
  5.2 4.8 %collective-permute-start.1 = (f32[24,512]{1,0:T(8,128)S(1)}, f32[24,512]{1,0:T(8,128)S(1)}, u32[]{:S(2)}, u32[]{:S(2)}) collective-permute-start(f32[24,512]{1,0:T(8,128)S(1)} %sum_core.1.r0), channel_id=1, source_target_pairs={{2,0},{9,1},{4,2},{11,3},{6,4},{13,5},{0,6},{15,7},{10,8},{17,9},{... | collective-permute-start | bytes 147464 | tf_op jit(solution)/shard_map/ppermute | solution.py:47
  8.2 5.6 %collective-permute-start.2 = (f32[24,512]{1,0:T(8,128)S(1)}, f32[24,512]{1,0:T(8,128)S(1)}, u32[]{:S(2)}, u32[]{:S(2)}) collective-permute-start(f32[24,512]{1,0:T(8,128)S(1)} %sum_core.1.r0), channel_id=1, source_target_pairs={{4,0},{17,1},{6,2},{19,3},{0,4},{21,5},{2,6},{23,7},{12,8},{25,9},... | collective-permute-start | bytes 147464 | tf_op jit(solution)/shard_map/ppermute | solution.py:47
  8.8 5.5 %collective-permute-start.3 = (f32[24,512]{1,0:T(8,128)S(1)}, f32[24,512]{1,0:T(8,128)S(1)}, u32[]{:S(2)}, u32[]{:S(2)}) collective-permute-start(f32[24,512]{1,0:T(8,128)S(1)} %sum_core.1.r0), channel_id=1, source_target_pairs={{6,0},{25,1},{0,2},{27,3},{2,4},{29,5},{4,6},{31,7},{14,8},{1,9},{... | collective-permute-start | bytes 147464 | tf_op jit(solution)/shard_map/ppermute | solution.py:47
  14.3 5.9 %collective-permute-start.4 = (f32[24,512]{1,0:T(8,128)S(1)}, f32[24,512]{1,0:T(8,128)S(1)}, u32[]{:S(2)}, u32[]{:S(2)}) collective-permute-start(f32[24,512]{1,0:T(8,128)S(1)} %sum_first.1.r0), channel_id=1, source_target_pairs={{8,0},{3,1},{10,2},{5,3},{12,4},{7,5},{14,6},{1,7},{16,8},{11,9},{... | collective-permute-start | bytes 147464 | tf_op jit(solution)/shard_map/ppermute | solution.py:47
  18.4 5.7 %collective-permute-start.5 = (f32[24,512]{1,0:T(8,128)S(1)}, f32[24,512]{1,0:T(8,128)S(1)}, u32[]{:S(2)}, u32[]{:S(2)}) collective-permute-start(f32[24,512]{1,0:T(8,128)S(1)} %sum_first.1.r0), channel_id=1, source_target_pairs={{16,0},{5,1},{18,2},{7,3},{20,4},{1,5},{22,6},{3,7},{24,8},{13,9},... | collective-permute-start | bytes 147464 | tf_op jit(solution)/shard_map/ppermute | solution.py:47
  18.4 5.8 %collective-permute-start.6 = (f32[24,512]{1,0:T(8,128)S(1)}, f32[24,512]{1,0:T(8,128)S(1)}, u32[]{:S(2)}, u32[]{:S(2)}) collective-permute-start(f32[24,512]{1,0:T(8,128)S(1)} %sum_first.1.r0), channel_id=1, source_target_pairs={{24,0},{7,1},{26,2},{1,3},{28,4},{3,5},{30,6},{5,7},{0,8},{15,9},{... | collective-permute-start | bytes 147464 | tf_op jit(solution)/shard_map/ppermute | solution.py:47
  24.3 1.4 %collective-permute-start.7 = (f32[48,512]{1,0:T(8,128)S(1)}, f32[48,512]{1,0:T(8,128)S(1)}, u32[]{:S(2)}, u32[]{:S(2)}) collective-permute-start(f32[48,512]{1,0:T(8,128)S(1)} %sum_second.1.own.refs_1_), channel_id=1, source_target_pairs={{1,0},{0,1},{3,2},{2,3},{5,4},{4,5},{7,6},{6,7},{9,8},{8,9},{11,10... | collective-permute-start | bytes 294920 | tf_op jit(solution)/shard_map/ppermute | solution.py:57
  30.1 7.3 %collective-permute-start.8 = (bf16[272,256]{1,0:T(8,128)(2,1)S(1)}, bf16[272,256]{1,0:T(8,128)(2,1)S(1)}, u32[]{:S(2)}, u32[]{:S(2)}) collective-permute-start(bf16[272,256]{1,0:T(8,128)(2,1)S(1)} %factor.1.refs_0_), channel_id=1, source_target_pairs={{64,0},{96,32},{0,64},{32,96},{65,1},{97,33},{1,65},{33,97},{66,2}... | collective-permute-start | bytes 417800 | tf_op jit(solution)/shard_map/ppermute | solution.py:61
  31.6 7.5 %collective-permute-start.13 = (bf16[272,256]{1,0:T(8,128)(2,1)S(1)}, bf16[272,256]{1,0:T(8,128)(2,1)S(1)}, u32[]{:S(2)}, u32[]{:S(2)}) collective-permute-start(bf16[272,256]{1,0:T(8,128)(2,1)S(1)} %factor.1.refs_0_), channel_id=1, source_target_pairs={{2,0},{9,1},{4,2},{11,3},{6,4},{13,5},{0,6},{15,7},{10,8},{17,9},{... | collective-permute-start | bytes 417800 | tf_op jit(solution)/shard_map/ppermute | solution.py:47
  32.1 8.2 %collective-permute-start.14 = (bf16[272,256]{1,0:T(8,128)(2,1)S(1)}, bf16[272,256]{1,0:T(8,128)(2,1)S(1)}, u32[]{:S(2)}, u32[]{:S(2)}) collective-permute-start(bf16[272,256]{1,0:T(8,128)(2,1)S(1)} %factor.1.refs_0_), channel_id=1, source_target_pairs={{4,0},{17,1},{6,2},{19,3},{0,4},{21,5},{2,6},{23,7},{12,8},{25,9},... | collective-permute-start | bytes 417800 | tf_op jit(solution)/shard_map/ppermute | solution.py:47
  33.2 7.1 %collective-permute-start.15 = (bf16[272,256]{1,0:T(8,128)(2,1)S(1)}, bf16[272,256]{1,0:T(8,128)(2,1)S(1)}, u32[]{:S(2)}, u32[]{:S(2)}) collective-permute-start(bf16[272,256]{1,0:T(8,128)(2,1)S(1)} %factor.1.refs_0_), channel_id=1, source_target_pairs={{6,0},{25,1},{0,2},{27,3},{2,4},{29,5},{4,6},{31,7},{14,8},{1,9},{... | collective-permute-start | bytes 417800 | tf_op jit(solution)/shard_map/ppermute | solution.py:47
  37.4 6.3 %collective-permute-start.9 = (bf16[272,256]{1,0:T(8,128)(2,1)S(1)}, bf16[272,256]{1,0:T(8,128)(2,1)S(1)}, u32[]{:S(2)}, u32[]{:S(2)}) collective-permute-start(bf16[272,256]{1,0:T(8,128)(2,1)S(1)} %collective-permute-done.8.refs_0_), channel_id=1, source_target_pairs={{2,0},{9,1},{4,2},{11,3},{6,4},{13,5},{0,6},{15,7},{10,8},{17,9},{... | collective-permute-start | bytes 417800 | tf_op jit(solution)/shard_map/ppermute | solution.py:47
  38.0 7.8 %collective-permute-start.10 = (bf16[272,256]{1,0:T(8,128)(2,1)S(1)}, bf16[272,256]{1,0:T(8,128)(2,1)S(1)}, u32[]{:S(2)}, u32[]{:S(2)}) collective-permute-start(bf16[272,256]{1,0:T(8,128)(2,1)S(1)} %collective-permute-done.8.refs_0_), channel_id=1, source_target_pairs={{4,0},{17,1},{6,2},{19,3},{0,4},{21,5},{2,6},{23,7},{12,8},{25,9},... | collective-permute-start | bytes 417800 | tf_op jit(solution)/shard_map/ppermute | solution.py:47
  39.1 9.6 %collective-permute-start.11 = (bf16[272,256]{1,0:T(8,128)(2,1)S(1)}, bf16[272,256]{1,0:T(8,128)(2,1)S(1)}, u32[]{:S(2)}, u32[]{:S(2)}) collective-permute-start(bf16[272,256]{1,0:T(8,128)(2,1)S(1)} %collective-permute-done.8.refs_0_), channel_id=1, source_target_pairs={{6,0},{25,1},{0,2},{27,3},{2,4},{29,5},{4,6},{31,7},{14,8},{1,9},{... | collective-permute-start | bytes 417800 | tf_op jit(solution)/shard_map/ppermute | solution.py:47
  40.4 16.9 %collective-permute-start.19 = (bf16[1088,256]{1,0:T(8,128)(2,1)S(1)}, bf16[1088,256]{1,0:T(8,128)(2,1)S(1)}, u32[]{:S(2)}, u32[]{:S(2)}) collective-permute-start(bf16[1088,256]{1,0:T(8,128)(2,1)S(1)} %join.5), channel_id=1, source_target_pairs={{16,0},{5,1},{18,2},{7,3},{20,4},{1,5},{22,6},{3,7},{24,8},{13,9},... | collective-permute-start | bytes 1671176 | tf_op jit(solution)/shard_map/ppermute | solution.py:47
  48.7 9.6 %collective-permute-start.17 = (bf16[1088,256]{1,0:T(8,128)(2,1)S(1)}, bf16[1088,256]{1,0:T(8,128)(2,1)S(1)}, u32[]{:S(2)}, u32[]{:S(2)}) collective-permute-start(bf16[1088,256]{1,0:T(8,128)(2,1)S(1)} %join.4.refs_0_), channel_id=1, source_target_pairs={{8,0},{3,1},{10,2},{5,3},{12,4},{7,5},{14,6},{1,7},{16,8},{11,9},{... | collective-permute-start | bytes 1671176 | tf_op jit(solution)/shard_map/ppermute | solution.py:47
  49.0 10.7 %collective-permute-start.21 = (bf16[1088,256]{1,0:T(8,128)(2,1)S(1)}, bf16[1088,256]{1,0:T(8,128)(2,1)S(1)}, u32[]{:S(2)}, u32[]{:S(2)}) collective-permute-start(bf16[1088,256]{1,0:T(8,128)(2,1)S(1)} %join.4.refs_0_), channel_id=1, source_target_pairs={{24,0},{7,1},{26,2},{1,3},{28,4},{3,5},{30,6},{5,7},{0,8},{15,9},{... | collective-permute-start | bytes 1671176 | tf_op jit(solution)/shard_map/ppermute | solution.py:47
  52.1 5.2 %collective-permute-start.12 = (s32[8,128]{1,0:T(8,128)S(1)}, s32[8,128]{1,0:T(8,128)S(1)}, u32[]{:S(2)}, u32[]{:S(2)}) collective-permute-start(s32[8,128]{1,0:T(8,128)S(1)} %get-tuple-element.15), channel_id=1, source_target_pairs={{64,0},{96,32},{0,64},{32,96},{65,1},{97,33},{1,65},{33,97},{66,2}... | collective-permute-start | bytes 12296 | tf_op jit(solution)/shard_map/ppermute | solution.py:61
  53.0 7.2 %collective-permute-start.16 = (bf16[1088,256]{1,0:T(8,128)(2,1)S(1)}, bf16[1088,256]{1,0:T(8,128)(2,1)S(1)}, u32[]{:S(2)}, u32[]{:S(2)}) collective-permute-start(bf16[1088,256]{1,0:T(8,128)(2,1)S(1)} %join.4.refs_0_), channel_id=1, source_target_pairs={{1,0},{0,1},{3,2},{2,3},{5,4},{4,5},{7,6},{6,7},{9,8},{8,9},{11,10... | collective-permute-start | bytes 1671176 | tf_op jit(solution)/shard_map/ppermute | solution.py:57
  57.3 3.3 %collective-permute-start.20 = (bf16[1088,256]{1,0:T(8,128)(2,1)S(1)}, bf16[1088,256]{1,0:T(8,128)(2,1)S(1)}, u32[]{:S(2)}, u32[]{:S(2)}) collective-permute-start(bf16[1088,256]{1,0:T(8,128)(2,1)S(1)} %touch.3.refs_1_), channel_id=1, source_target_pairs={{1,0},{0,1},{3,2},{2,3},{5,4},{4,5},{7,6},{6,7},{9,8},{8,9},{11,10... | collective-permute-start | bytes 1671176 | tf_op jit(solution)/shard_map/ppermute | solution.py:57
  58.3 4.6 %collective-permute-start.18 = (bf16[1088,256]{1,0:T(8,128)(2,1)S(1)}, bf16[1088,256]{1,0:T(8,128)(2,1)S(1)}, u32[]{:S(2)}, u32[]{:S(2)}) collective-permute-start(bf16[1088,256]{1,0:T(8,128)(2,1)S(1)} %collective-permute-done.17.refs_1_), channel_id=1, source_target_pairs={{1,0},{0,1},{3,2},{2,3},{5,4},{4,5},{7,6},{6,7},{9,8},{8,9},{11,10... | collective-permute-start | bytes 1671176 | tf_op jit(solution)/shard_map/ppermute | solution.py:57
  59.7 3.9 %collective-permute-start.22 = (bf16[1088,256]{1,0:T(8,128)(2,1)S(1)}, bf16[1088,256]{1,0:T(8,128)(2,1)S(1)}, u32[]{:S(2)}, u32[]{:S(2)}) collective-permute-start(bf16[1088,256]{1,0:T(8,128)(2,1)S(1)} %collective-permute-done.21.refs_1_), channel_id=1, source_target_pairs={{1,0},{0,1},{3,2},{2,3},{5,4},{4,5},{7,6},{6,7},{9,8},{8,9},{11,10... | collective-permute-start | bytes 1671176 | tf_op jit(solution)/shard_map/ppermute | solution.py:57
  59.7 8.4 %collective-permute-start.23 = (bf16[1088,256]{1,0:T(8,128)(2,1)S(1)}, bf16[1088,256]{1,0:T(8,128)(2,1)S(1)}, u32[]{:S(2)}, u32[]{:S(2)}) collective-permute-start(bf16[1088,256]{1,0:T(8,128)(2,1)S(1)} %join.3.refs_3_.refs_4_.refs_0_), channel_id=1, source_target_pairs={{1,0},{0,1},{3,2},{2,3},{5,4},{4,5},{7,6},{6,7},{9,8},{8,9},{11,10... | collective-permute-start | bytes 1671176 | tf_op jit(solution)/shard_map/ppermute | solution.py:57
  60.2 9.5 %collective-permute-start.24 = (bf16[1088,256]{1,0:T(8,128)(2,1)S(1)}, bf16[1088,256]{1,0:T(8,128)(2,1)S(1)}, u32[]{:S(2)}, u32[]{:S(2)}) collective-permute-start(bf16[1088,256]{1,0:T(8,128)(2,1)S(1)} %join.3.refs_3_.refs_4_.refs_0_), channel_id=1, source_target_pairs={{8,0},{3,1},{10,2},{5,3},{12,4},{7,5},{14,6},{1,7},{16,8},{11,9},{... | collective-permute-start | bytes 1671176 | tf_op jit(solution)/shard_map/ppermute | solution.py:47
  60.6 11.1 %collective-permute-start.26 = (bf16[1088,256]{1,0:T(8,128)(2,1)S(1)}, bf16[1088,256]{1,0:T(8,128)(2,1)S(1)}, u32[]{:S(2)}, u32[]{:S(2)}) collective-permute-start(bf16[1088,256]{1,0:T(8,128)(2,1)S(1)} %join.3.refs_3_.refs_4_.refs_0_), channel_id=1, source_target_pairs={{16,0},{5,1},{18,2},{7,3},{20,4},{1,5},{22,6},{3,7},{24,8},{13,9},... | collective-permute-start | bytes 1671176 | tf_op jit(solution)/shard_map/ppermute | solution.py:47
  63.0 14.7 %collective-permute-start.28 = (bf16[1088,256]{1,0:T(8,128)(2,1)S(1)}, bf16[1088,256]{1,0:T(8,128)(2,1)S(1)}, u32[]{:S(2)}, u32[]{:S(2)}) collective-permute-start(bf16[1088,256]{1,0:T(8,128)(2,1)S(1)} %join.3.refs_3_.refs_4_.refs_0_), channel_id=1, source_target_pairs={{24,0},{7,1},{26,2},{1,3},{28,4},{3,5},{30,6},{5,7},{0,8},{15,9},{... | collective-permute-start | bytes 1671176 | tf_op jit(solution)/shard_map/ppermute | solution.py:47
  66.9 24.3 %collective-permute-start.30 = (bf16[8,256,256]{2,1,0:T(8,128)(2,1)S(1)}, bf16[8,256,256]{2,1,0:T(8,128)(2,1)S(1)}, u32[]{:S(2)}, u32[]{:S(2)}) collective-permute-start(bf16[8,256,256]{2,1,0:T(8,128)(2,1)S(1)} %get-tuple-element.19.refs_0_), channel_id=1, source_target_pairs={{96,0},{0,32},{32,64},{64,96},{97,1},{1,33},{33,65},{65,97},{98,2}... | collective-permute-start | bytes 3145736 | tf_op jit(solution)/shard_map/ppermute | solution.py:61
  68.1 24.8 %collective-permute-start.31 = (bf16[8,256,256]{2,1,0:T(8,128)(2,1)S(1)}, bf16[8,256,256]{2,1,0:T(8,128)(2,1)S(1)}, u32[]{:S(2)}, u32[]{:S(2)}) collective-permute-start(bf16[8,256,256]{2,1,0:T(8,128)(2,1)S(1)} %get-tuple-element.20), channel_id=1, source_target_pairs={{32,0},{64,32},{96,64},{0,96},{33,1},{65,33},{97,65},{1,97},{34,2}... | collective-permute-start | bytes 3145736 | tf_op jit(solution)/shard_map/ppermute | solution.py:61
  69.7 11.9 %collective-permute-start.25 = (bf16[1088,256]{1,0:T(8,128)(2,1)S(1)}, bf16[1088,256]{1,0:T(8,128)(2,1)S(1)}, u32[]{:S(2)}, u32[]{:S(2)}) collective-permute-start(bf16[1088,256]{1,0:T(8,128)(2,1)S(1)} %collective-permute-done.24.refs_1_), channel_id=1, source_target_pairs={{1,0},{0,1},{3,2},{2,3},{5,4},{4,5},{7,6},{6,7},{9,8},{8,9},{11,10... | collective-permute-start | bytes 1671176 | tf_op jit(solution)/shard_map/ppermute | solution.py:57
  71.7 10.1 %collective-permute-start.27 = (bf16[1088,256]{1,0:T(8,128)(2,1)S(1)}, bf16[1088,256]{1,0:T(8,128)(2,1)S(1)}, u32[]{:S(2)}, u32[]{:S(2)}) collective-permute-start(bf16[1088,256]{1,0:T(8,128)(2,1)S(1)} %collective-permute-done.26.refs_1_), channel_id=1, source_target_pairs={{1,0},{0,1},{3,2},{2,3},{5,4},{4,5},{7,6},{6,7},{9,8},{8,9},{11,10... | collective-permute-start | bytes 1671176 | tf_op jit(solution)/shard_map/ppermute | solution.py:57
  77.6 4.5 %collective-permute-start.29 = (bf16[1088,256]{1,0:T(8,128)(2,1)S(1)}, bf16[1088,256]{1,0:T(8,128)(2,1)S(1)}, u32[]{:S(2)}, u32[]{:S(2)}) collective-permute-start(bf16[1088,256]{1,0:T(8,128)(2,1)S(1)} %collective-permute-done.28.refs_1_), channel_id=1, source_target_pairs={{1,0},{0,1},{3,2},{2,3},{5,4},{4,5},{7,6},{6,7},{9,8},{8,9},{11,10... | collective-permute-start | bytes 1671176 | tf_op jit(solution)/shard_map/ppermute | solution.py:57
  (2 other events, 2.4 us)

commit v4 on v3

--- a/solution.py
+++ b/solution.py
@@ -34,7 +34,7 @@
     return pltpu.CompilerParams(vmem_limit_bytes=mib * 1024 * 1024)
 
 
-def from_cand(x, leg, k, far=False):
+def from_cand(x, leg, k):
     pairs = []
     for me in range(N_CAND):
         z, y, core = me // 8, (me // 2) % 4, me % 2
@@ -43,14 +43,7 @@
         else:
             z = (z + k) % 4
         pairs.append((z * 8 + y * 2 + core, me))
-    if not far:
-        return lax.ppermute(x, "cand", pairs)
-    pairs = [
-        ((me_set + 2) % N_SET * N_CAND + source, me_set * N_CAND + me)
-        for me_set in range(N_SET)
-        for source, me in pairs
-    ]
-    return lax.ppermute(x, ("set", "cand"), pairs)
+    return lax.ppermute(x, "cand", pairs)
 
 
 def from_core(x):
@@ -140,10 +133,18 @@
     lane = lax.broadcasted_iota(i32, (RANK, 128), 1)
     line = lax.broadcasted_iota(i32, (RANK, 128), 0)
     work = gram + jnp.where(lane == line + RANK, 1.0, 0.0)
-    for k in range(RANK - 1):
-        column = jnp.broadcast_to(work[:, k : k + 1], (RANK, 128))
-        pivot_row = work[k : k + 1, :] / column[k : k + 1, :]
-        work = work - jnp.where(line > k, column, 0.0) * pivot_row
+    for k in range(0, RANK, 2):
+        first_column = jnp.broadcast_to(work[:, k : k + 1], (RANK, 128))
+        second_column = jnp.broadcast_to(work[:, k + 1 : k + 2], (RANK, 128))
+        inverse = 1.0 / first_column[k : k + 1, :]
+        first_row = work[k : k + 1, :] * inverse
+        second_column = second_column - first_column * (second_column[k : k + 1, :] * inverse)
+        second_row = work[k + 1 : k + 2, :] - first_column[k + 1 : k + 2, :] * first_row
+        second_row = second_row / second_column[k + 1 : k + 2, :]
+        work = work - (
+            jnp.where(line > k, first_column, 0.0) * first_row
+            + jnp.where(line > k + 1, second_column, 0.0) * second_row
+        )
     pivots = jnp.sum(jnp.where(lane == line, work, 0.0), axis=1, keepdims=True)
     inverse = work * lax.rsqrt(pivots)
     shifted = jnp.concatenate([jnp.zeros((32, W), f32), summed, jnp.zeros((64, W), f32)], axis=0)
@@ -192,26 +193,31 @@
     )(x, *after)
 
 
-def join_kernel(*refs):
-    for k in range(4):
-        refs[-1][k * MSG : (k + 1) * MSG, :] = refs[k][...]
-
-
-def join_call(parts, *after):
-    return pl.pallas_call(
-        join_kernel,
-        out_shape=jax.ShapeDtypeStruct((4 * MSG, BLOCK), bf16),
-        in_specs=[VMEM] * 4 + [ANY] * len(after),
+def join_call(parts, name, *after):
+    heights = [part.shape[0] for part in parts]
+
+    def kernel(*refs):
+        at = 0
+        for ref, height in zip(refs, heights):
+            refs[-1][at : at + height, :] = ref[...]
+            at += height
+
+    return pl.pallas_call(
+        kernel,
+        out_shape=jax.ShapeDtypeStruct((sum(heights), BLOCK), bf16),
+        in_specs=[VMEM] * len(parts) + [ANY] * len(after),
         out_specs=VMEM,
         compiler_params=params(),
-        name="join",
+        name=name,
     )(*parts, *after)
 
 
 def put_call(whole, part, n):
     def kernel(*refs):
         out, sem = refs[-2:]
-        copy = pltpu.make_async_copy(refs[-3], out.at[pl.ds(n * 4 * MSG, 4 * MSG)], sem)
+        copy = pltpu.make_async_copy(
+            refs[-3].at[pl.ds(0, 4 * MSG)], out.at[pl.ds(n * 4 * MSG, 4 * MSG)], sem
+        )
         copy.start()
         copy.wait()
 
@@ -233,6 +239,13 @@
     for n, part in parts:
         whole = put_call(whole, part, n)
     return whole
+
+
+def with_begins(lists, out):
+    begins = (lists // NB_DEV) % N_CAND * MSG + lists % NB_DEV * RANK
+    out[0:4, :] = lists[0:4, :]
+    out[4:6, :] = begins[0:2, :]
+    out[6:8, :] = lists[6:8, :]
 
 
 def plan_kernel(place, own, other, *refs):
@@ -293,22 +306,41 @@
         lists = jnp.dot(both, chosen, preferred_element_type=f32)[0:8, :]
         lists = jnp.where(line == 0, lists + ZERO, lists)
         lists = jnp.where(line == 2, target_of, jnp.where(line == 3, pieces, lists))
-        lists = lists.astype(i32)
-        begins = (lists // NB_DEV) % N_CAND * MSG + lists % NB_DEV * RANK
-        outs[gr][0:4, :] = lists[0:4, :]
-        outs[gr][4:6, :] = begins[0:2, :]
+        lists = jnp.where(line == 6, chunks, lists)
+        if gr == 2:
+            lists = jnp.concatenate([lists, jnp.zeros((8, 128), f32)], axis=0).astype(bf16)
+            outs[gr][...] = jnp.concatenate([lists, jnp.zeros((16, 128), bf16)], axis=1)
+        else:
+            with_begins(lists.astype(i32), outs[gr])
 
 
 def plan_call(place, own, other, *after):
+    shapes = [jax.ShapeDtypeStruct((8, 128), i32)] * N_SET
+    shapes[2] = jax.ShapeDtypeStruct((16, BLOCK), bf16)
     return pl.pallas_call(
         lambda *refs: plan_kernel(*refs[:3], *refs[3 + len(after) :]),
-        out_shape=(jax.ShapeDtypeStruct((8, 128), i32),) * N_SET,
+        out_shape=shapes,
         in_specs=[SMEM, VMEM, VMEM] + [ANY] * len(after),
-        out_specs=(VMEM,) * N_SET,
+        out_specs=[VMEM] * N_SET,
         scratch_shapes=[pltpu.VMEM((N_CAND * 8, 128), f32)],
         compiler_params=params(),
         name="plan",
     )(place, own, other, *after)
+
+
+def unpack_call(message):
+    def kernel(message, out):
+        lists = message[4 * MSG :, 0:128].astype(f32)[0:8, :]
+        with_begins(lists.astype(i32), out)
+
+    return pl.pallas_call(
+        kernel,
+        out_shape=jax.ShapeDtypeStruct((8, 128), i32),
+        in_specs=[VMEM],
+        out_specs=VMEM,
+        compiler_params=params(),
+        name="unpack",
+    )(message)
 
 
 def spread(factors, scales):
@@ -334,7 +366,7 @@
             lefts[side, here, :] = block_at(factors, pairs[4, spot]) * weight
             rights[side, here, :] = block_at(factors, pairs[5, spot])
 
-    def couple(n, carry):
+    def couple(n, last):
         chunk(2 * n, 0)
         chunk(2 * n + 1, 1)
         terms = [
@@ -343,11 +375,15 @@
         ]
         for side in range(2):
             t = pairs[2, 2 * n + side]
-            totals[t] += terms[side]
-        return carry
-
-    totals[...] = jnp.zeros_like(totals)
-    lax.fori_loop(0, (pairs[3, 0] + 1) // 2, couple, 0)
+            totals[t] = jnp.where(t == last, totals[t], 0.0) + terms[side]
+            last = t
+        return last
+
+    lax.fori_loop(0, (pairs[3, 0] + 1) // 2, couple, -1)
+
+
+def total_of(pairs, t, totals):
+    return jnp.where(pairs[6, t] > 0, totals[t], 0.0)
 
 
 WORK = [
@@ -358,23 +394,25 @@
 ]
 
 
-def send_call(next_list, last_list, factors):
-    def kernel(next_list, last_list, factors, to_next, to_last, scales, lefts, rights, totals):
+def send_call(next_list, last_list, factors, *after):
+    def kernel(next_list, last_list, factors, *refs):
+        to_next, to_last, scales, lefts, rights, totals = refs[len(after) :]
         spread(factors, scales)
         for pairs, out in ((next_list, to_next), (last_list, to_last)):
             expand(pairs, factors, scales, lefts, rights, totals)
-            out[...] = totals[...].astype(bf16)
+            for t in range(NT_DEV):
+                out[t] = total_of(pairs, t, totals).astype(bf16)
 
     out = jax.ShapeDtypeStruct((NT_DEV, BLOCK, BLOCK), bf16)
     return pl.pallas_call(
         kernel,
         out_shape=(out, out),
-        in_specs=[SMEM, SMEM, VMEM],
+        in_specs=[SMEM, SMEM, VMEM] + [ANY] * len(after),
         out_specs=(VMEM, VMEM),
         scratch_shapes=WORK,
         compiler_params=params(),
         name="send_pairs",
-    )(next_list, last_list, factors)
+    )(next_list, last_list, factors, *after)
 
 
 def keep_call(pairs, base, factors, *after):
@@ -382,7 +420,8 @@
         out, scales, lefts, rights, totals = refs[len(after) :]
         spread(factors, scales)
         expand(pairs, factors, scales, lefts, rights, totals)
-        out[...] = base[...] - totals[...]
+        for t in range(NT_DEV):
+            out[t] = base[t] - total_of(pairs, t, totals)
 
     return pl.pallas_call(
         kernel,
@@ -435,16 +474,10 @@
     other = from_core(own)
 
     mine = factor_call(place, own, other, rows)
-    far = from_set(mine, 2)
-    parts = [mine] + [from_cand(mine, 0, k) for k in (1, 2, 3)]
-    line = join_call(parts)
-    opposite = from_cand(line, 1, 2)
-    far_line = join_call([far] + [from_cand(far, 0, k) for k in (1, 2, 3)])
-    own_list, next_list, far_list, last_list = plan_call(place, own, other, far_line)
-    far_list = from_set(far_list, 2)
-    line = join_call(parts, far_line)
-    opposite = touch_call(opposite, 0, far_list)
-    here = [line, from_cand(line, 1, 1), opposite, from_cand(line, 1, 3)]
+    own_list, next_list, far_list, last_list = plan_call(place, own, other, mine)
+    line = join_call([mine] + [from_cand(mine, 0, k) for k in (1, 2, 3)], "join_line", next_list)
+    far_line = from_set(join_call([line, far_list], "join_far"), 2)
+    here = [line] + [from_cand(line, 1, k) for k in (1, 2, 3)]
     there = [from_core(x) for x in here]
     factors = put_all(
         [p for k in range(4) for p in ((k, here[k]), (4 + k, there[k]))]
@@ -459,7 +492,7 @@
         [p for k in range(4) for p in ((k, far_here[k]), (4 + k, far_there[k]))]
     )
     base = keep_call(own_list, accumulator[0], factors, to_next)
-    base = keep_call(far_list, base, far_factors)
+    base = keep_call(unpack_call(far_line), base, far_factors)
     base = final_call(base, *arrived)
     return base[None]
 

time: 95.3 us -> 91.5 us (0.960)
  Pallas kernels: 19.4 us -> 17.4 us
  local copies, waits for them, and re-layouts: 2.25 us -> 0.76 us
    ppermute x10, starting transfers between devices: 0.7 us -> 5.52 us  [from_core(): return lax.ppermute(x, 'cand', [(me ^ 1, me) for me in range(N_CAND)])]
    ppermute x18 -> x15, starting transfers between devices: 22.5 us -> 18.7 us  [from_cand(): return lax.ppermute(x, 'cand', pairs)]
    pallas_call x2, Pallas kernels: 4.54 us -> 2.32 us  [keep_call(): pl.pallas_call(kernel, out_shape=jax.ShapeDtypeStruct((NT_DEV, BLOCK, BLO...]
    unnamed x4, local copies, waits for them, and re-layouts: 2.25 us -> 0.76 us
    pallas_call x4, Pallas kernels: 3.29 us -> 4.51 us  [the longest x1 4.42 us: send_call(): pl.pallas_call(kernel, out_shape=(out, out), in_specs=[SMEM, SMEM, VMEM]...]
    ppermute x4 -> x3, starting transfers between devices: 4.67 us -> 3.56 us  [from_set(): lax.ppermute(x, 'set', [((me + d) % N_SET, me) for me in range(N_SET)])]
    ppermute x18 -> x15, waiting for transfers between devices: 26.3 us -> 25.2 us  [from_cand(): return lax.ppermute(x, 'cand', pairs)]
    ppermute x4 -> x3, waiting for transfers between devices: 15.7 us -> 16.8 us  [from_set(): lax.ppermute(x, 'set', [((me + d) % N_SET, me) for me in range(N_SET)])]
  transfers between devices with their start and end apart: 32 -> 28, of which waited for: 20 -> 18; matrix products, arithmetic and copies ran while one was open for 1% -> 1% of each run, Pallas kernels for 11% -> 10%
where the time goes in v4:
time: 91.5 us; the launch traced here: 90.8 us
  waiting for transfers between devices  43.7 us (48%)
  starting transfers between devices  27.8 us (30%)
  Pallas kernels  17.4 us (19%)
    ppermute x15, waiting for transfers between devices, from_cand(): return lax.ppermute(x, 'cand', pairs)  25.2 us
    ppermute x15, starting transfers between devices, from_cand(): return lax.ppermute(x, 'cand', pairs)  18.7 us
    ppermute x3, waiting for transfers between devices, from_set(): lax.ppermute(x, 'set', [((me + d) % N_SET, me) for me in range(N_SET)])  16.8 us
    ppermute x10, starting transfers between devices, from_core(): return lax.ppermute(x, 'cand', [(me ^ 1, me) for me in range(N_CAND)])  5.52 us
    pallas_call x1, Pallas kernels, send_call(): pl.pallas_call(kernel, out_shape=(out, out), in_specs=[SMEM, SMEM, VMEM]...  4.42 us
    ppermute x3, starting transfers between devices, from_set(): lax.ppermute(x, 'set', [((me + d) % N_SET, me) for me in range(N_SET)])  3.56 us
    pallas_call x1, Pallas kernels, factor_call(): pl.pallas_call(factor_kernel, out_shape=jax.ShapeDtypeStruct((MSG, BLOCK)...  3.45 us
    pallas_call x1, Pallas kernels, sketch_call(): pl.pallas_call(sketch_kernel, out_shape=(half, half), in_specs=[SMEM, HBM...  3.05 us
  transfers between devices with their start and end apart: 28, of which 18 were waited for; matrix products, arithmetic and copies ran while one was open for 1% of the time, Pallas kernels for 10%

profile of v4, /device:TPU:6, one launch (start us, length us, event | category | flops | bytes accessed | tf_op | source)
XLA Modules:
  0.0 90.8 jit_solution(17829958994913734490)
XLA Ops:
  0.8 3.1 %sketch.1 = (f32[16,512]{1,0:T(8,128)S(1)}, f32[16,512]{1,0:T(8,128)S(1)}) custom-call(s32[2]{0:T(128)S(1)} %pad_add_fusion.place.refs_0_, bf16[2048,512]{1,0:T(8,128)(2,1)} %bitcast.22, bf16[32,512]{1,0:T(8,128)(2,1)S(1)} %bitcast.21), custom_call_target="tpu_custom_call" | custom-call | tf_op jit(solution)/shard_map/sketch/pallas_call | solution.py:77
  5.2 3.0 %collective-permute-start.1 = (f32[24,512]{1,0:T(8,128)S(1)}, f32[24,512]{1,0:T(8,128)S(1)}, u32[]{:S(2)}, u32[]{:S(2)}) collective-permute-start(f32[24,512]{1,0:T(8,128)S(1)} %sum_core.1.r0), channel_id=1, source_target_pairs={{2,0},{9,1},{4,2},{11,3},{6,4},{13,5},{0,6},{15,7},{10,8},{17,9},{... | collective-permute-start | bytes 147464 | tf_op jit(solution)/shard_map/ppermute | solution.py:46
  8.8 1.0 %collective-permute-start.3 = (f32[24,512]{1,0:T(8,128)S(1)}, f32[24,512]{1,0:T(8,128)S(1)}, u32[]{:S(2)}, u32[]{:S(2)}) collective-permute-start(f32[24,512]{1,0:T(8,128)S(1)} %sum_core.1.r0), channel_id=1, source_target_pairs={{6,0},{25,1},{0,2},{27,3},{2,4},{29,5},{4,6},{31,7},{14,8},{1,9},{... | collective-permute-start | bytes 147464 | tf_op jit(solution)/shard_map/ppermute | solution.py:46
  10.0 3.9 %collective-permute-done.2.r2 = f32[24,512]{1,0:T(8,128)S(1)} collective-permute-done((f32[24,512]{1,0:T(8,128)S(1)}, f32[24,512]{1,0:T(8,128)S(1)}, u32[]{:S(2)}, u32[]{:S(2)}) %collective-permute-start.2) | collective-permute-done | bytes 49184 | tf_op jit(solution)/shard_map/ppermute | solution.py:46
  14.3 4.1 %collective-permute-start.4 = (f32[24,512]{1,0:T(8,128)S(1)}, f32[24,512]{1,0:T(8,128)S(1)}, u32[]{:S(2)}, u32[]{:S(2)}) collective-permute-start(f32[24,512]{1,0:T(8,128)S(1)} %sum_first.1.r0), channel_id=1, source_target_pairs={{8,0},{3,1},{10,2},{5,3},{12,4},{7,5},{14,6},{1,7},{16,8},{11,9},{... | collective-permute-start | bytes 147464 | tf_op jit(solution)/shard_map/ppermute | solution.py:46
  18.4 1.3 %collective-permute-start.6 = (f32[24,512]{1,0:T(8,128)S(1)}, f32[24,512]{1,0:T(8,128)S(1)}, u32[]{:S(2)}, u32[]{:S(2)}) collective-permute-start(f32[24,512]{1,0:T(8,128)S(1)} %sum_first.1.r0), channel_id=1, source_target_pairs={{24,0},{7,1},{26,2},{1,3},{28,4},{3,5},{30,6},{5,7},{0,8},{15,9},{... | collective-permute-start | bytes 147464 | tf_op jit(solution)/shard_map/ppermute | solution.py:46
  20.2 3.9 %collective-permute-done.5.r2 = f32[24,512]{1,0:T(8,128)S(1)} collective-permute-done((f32[24,512]{1,0:T(8,128)S(1)}, f32[24,512]{1,0:T(8,128)S(1)}, u32[]{:S(2)}, u32[]{:S(2)}) %collective-permute-start.5) | collective-permute-done | bytes 49184 | tf_op jit(solution)/shard_map/ppermute | solution.py:46
  24.4 1.3 %collective-permute-done.7.other.refs_2_ = f32[48,512]{1,0:T(8,128)S(1)} collective-permute-done((f32[48,512]{1,0:T(8,128)S(1)}, f32[48,512]{1,0:T(8,128)S(1)}, u32[]{:S(2)}, u32[]{:S(2)}) %collective-permute-start.7) | collective-permute-done | bytes 98336 | tf_op jit(solution)/shard_map/ppermute | solution.py:50
  25.7 3.5 %factor.1.refs_3_.refs_0_ = bf16[272,256]{1,0:T(8,128)(2,1)S(1)} custom-call(s32[2]{0:T(128)S(1)} %pad_add_fusion.place.refs_0_, f32[48,512]{1,0:T(8,128)S(1)} %sum_second.1.own.refs_1_, f32[48,512]{1,0:T(8,128)S(1)} %collective-permute-done.7.other.refs_2_, bf16[2048,512]{1,0:T(8,128)(2,1)} %bitcast.23), custom_call_target="tpu_custom_call" | custom-call | tf_op jit(solution)/shard_map/factor/pallas_call | solution.py:170
  29.8 1.1 %collective-permute-start.9 = (bf16[272,256]{1,0:T(8,128)(2,1)S(1)}, bf16[272,256]{1,0:T(8,128)(2,1)S(1)}, u32[]{:S(2)}, u32[]{:S(2)}) collective-permute-start(bf16[272,256]{1,0:T(8,128)(2,1)S(1)} %factor.1.refs_3_.refs_0_), channel_id=1, source_target_pairs={{4,0},{17,1},{6,2},{19,3},{0,4},{21,5},{2,6},{23,7},{12,8},{25,9},... | collective-permute-start | bytes 417800 | tf_op jit(solution)/shard_map/ppermute | solution.py:46
  30.8 1.3 %collective-permute-start.10 = (bf16[272,256]{1,0:T(8,128)(2,1)S(1)}, bf16[272,256]{1,0:T(8,128)(2,1)S(1)}, u32[]{:S(2)}, u32[]{:S(2)}) collective-permute-start(bf16[272,256]{1,0:T(8,128)(2,1)S(1)} %factor.1.refs_3_.refs_0_), channel_id=1, source_target_pairs={{6,0},{25,1},{0,2},{27,3},{2,4},{29,5},{4,6},{31,7},{14,8},{1,9},{... | collective-permute-start | bytes 417800 | tf_op jit(solution)/shard_map/ppermute | solution.py:46
  32.1 1.2 %plan.1 = (s32[8,128]{1,0:T(8,128)S(1)}, s32[8,128]{1,0:T(8,128)S(1)}, bf16[16,256]{1,0:T(8,128)(2,1)S(1)}, s32[8,128]{1,0:T(8,128)S(1)}) custom-call(s32[2]{0:T(128)S(1)} %pad_add_fusion.place.refs_0_, f32[48,512]{1,0:T(8,128)S(1)} %sum_second.1.own.refs_1_, f32[48,512]{1,0:T(8,128)S(1)} %collective-permute-done.7.other.refs_2_, ...), custom_call_target="tpu_custom_call" | custom-call | tf_op jit(solution)/shard_map/plan/pallas_call | solution.py:320
  34.3 2.1 %collective-permute-done.9.refs_2_ = bf16[272,256]{1,0:T(8,128)(2,1)S(1)} collective-permute-done((bf16[272,256]{1,0:T(8,128)(2,1)S(1)}, bf16[272,256]{1,0:T(8,128)(2,1)S(1)}, u32[]{:S(2)}, u32[]{:S(2)}) %collective-permute-start.9) | collective-permute-done | bytes 139296 | tf_op jit(solution)/shard_map/ppermute | solution.py:46
  36.4 1.4 %collective-permute-done.10.refs_3_ = bf16[272,256]{1,0:T(8,128)(2,1)S(1)} collective-permute-done((bf16[272,256]{1,0:T(8,128)(2,1)S(1)}, bf16[272,256]{1,0:T(8,128)(2,1)S(1)}, u32[]{:S(2)}, u32[]{:S(2)}) %collective-permute-start.10) | collective-permute-done | bytes 139296 | tf_op jit(solution)/shard_map/ppermute | solution.py:46
  37.9 0.9 %collective-permute-start.13 = (bf16[1088,256]{1,0:T(8,128)(2,1)S(1)}, bf16[1088,256]{1,0:T(8,128)(2,1)S(1)}, u32[]{:S(2)}, u32[]{:S(2)}) collective-permute-start(bf16[1088,256]{1,0:T(8,128)(2,1)S(1)} %join_line.1.refs_0_), channel_id=1, source_target_pairs={{8,0},{3,1},{10,2},{5,3},{12,4},{7,5},{14,6},{1,7},{16,8},{11,9},{... | collective-permute-start | bytes 1671176 | tf_op jit(solution)/shard_map/ppermute | solution.py:46
  38.8 1.0 %collective-permute-start.15 = (bf16[1088,256]{1,0:T(8,128)(2,1)S(1)}, bf16[1088,256]{1,0:T(8,128)(2,1)S(1)}, u32[]{:S(2)}, u32[]{:S(2)}) collective-permute-start(bf16[1088,256]{1,0:T(8,128)(2,1)S(1)} %join_line.1.refs_0_), channel_id=1, source_target_pairs={{16,0},{5,1},{18,2},{7,3},{20,4},{1,5},{22,6},{3,7},{24,8},{13,9},... | collective-permute-start | bytes 1671176 | tf_op jit(solution)/shard_map/ppermute | solution.py:46
  39.9 1.5 %collective-permute-start.11 = (bf16[1104,256]{1,0:T(8,128)(2,1)S(1)}, bf16[1104,256]{1,0:T(8,128)(2,1)S(1)}, u32[]{:S(2)}, u32[]{:S(2)}) collective-permute-start(bf16[1104,256]{1,0:T(8,128)(2,1)S(1)} %join_far.1), channel_id=1, source_target_pairs={{64,0},{96,32},{0,64},{32,96},{65,1},{97,33},{1,65},{33,97},{66,2}... | collective-permute-start | bytes 1695752 | tf_op jit(solution)/shard_map/ppermute | solution.py:54
  41.3 1.3 %collective-permute-start.17 = (bf16[1088,256]{1,0:T(8,128)(2,1)S(1)}, bf16[1088,256]{1,0:T(8,128)(2,1)S(1)}, u32[]{:S(2)}, u32[]{:S(2)}) collective-permute-start(bf16[1088,256]{1,0:T(8,128)(2,1)S(1)} %join_line.1.refs_0_), channel_id=1, source_target_pairs={{24,0},{7,1},{26,2},{1,3},{28,4},{3,5},{30,6},{5,7},{0,8},{15,9},{... | collective-permute-start | bytes 1671176 | tf_op jit(solution)/shard_map/ppermute | solution.py:46
  42.7 4.8 %collective-permute-done.13.refs_1_ = bf16[1088,256]{1,0:T(8,128)(2,1)S(1)} collective-permute-done((bf16[1088,256]{1,0:T(8,128)(2,1)S(1)}, bf16[1088,256]{1,0:T(8,128)(2,1)S(1)}, u32[]{:S(2)}, u32[]{:S(2)}) %collective-permute-start.13) | collective-permute-done | bytes 557088 | tf_op jit(solution)/shard_map/ppermute | solution.py:46
  47.5 2.5 %collective-permute-done.15.refs_1_ = bf16[1088,256]{1,0:T(8,128)(2,1)S(1)} collective-permute-done((bf16[1088,256]{1,0:T(8,128)(2,1)S(1)}, bf16[1088,256]{1,0:T(8,128)(2,1)S(1)}, u32[]{:S(2)}, u32[]{:S(2)}) %collective-permute-start.15) | collective-permute-done | bytes 557088 | tf_op jit(solution)/shard_map/ppermute | solution.py:46
  49.9 4.7 %collective-permute-done.11.message.refs_0_ = bf16[1104,256]{1,0:T(8,128)(2,1)S(1)} collective-permute-done((bf16[1104,256]{1,0:T(8,128)(2,1)S(1)}, bf16[1104,256]{1,0:T(8,128)(2,1)S(1)}, u32[]{:S(2)}, u32[]{:S(2)}) %collective-permute-start.11) | collective-permute-done | bytes 565280 | tf_op jit(solution)/shard_map/ppermute | solution.py:54
  54.6 1.2 %collective-permute-done.17.refs_1_ = bf16[1088,256]{1,0:T(8,128)(2,1)S(1)} collective-permute-done((bf16[1088,256]{1,0:T(8,128)(2,1)S(1)}, bf16[1088,256]{1,0:T(8,128)(2,1)S(1)}, u32[]{:S(2)}, u32[]{:S(2)}) %collective-permute-start.17) | collective-permute-done | bytes 557088 | tf_op jit(solution)/shard_map/ppermute | solution.py:46
  55.8 0.9 %collective-permute-start.20 = (bf16[1104,256]{1,0:T(8,128)(2,1)S(1)}, bf16[1104,256]{1,0:T(8,128)(2,1)S(1)}, u32[]{:S(2)}, u32[]{:S(2)}) collective-permute-start(bf16[1104,256]{1,0:T(8,128)(2,1)S(1)} %collective-permute-done.11.message.refs_0_), channel_id=1, source_target_pairs={{8,0},{3,1},{10,2},{5,3},{12,4},{7,5},{14,6},{1,7},{16,8},{11,9},{... | collective-permute-start | bytes 1695752 | tf_op jit(solution)/shard_map/ppermute | solution.py:46
  59.1 4.4 %send_pairs.1 = (bf16[8,256,256]{2,1,0:T(8,128)(2,1)S(1)}, bf16[8,256,256]{2,1,0:T(8,128)(2,1)S(1)}) custom-call(s32[8,128]{1,0:T(8,128)S(1)} %get-tuple-element.15.refs_4_.next_list, s32[8,128]{1,0:T(8,128)S(1)} %get-tuple-element.18.last_list, bf16[8704,256]{1,0:T(8,128)(2,1)S(1)} %put.23.factors), custom_call_target="tpu_custom_call" | custom-call | tf_op jit(solution)/shard_map/send_pairs/pallas_call | solution.py:407
  63.6 2.0 %collective-permute-start.27 = (bf16[8,256,256]{2,1,0:T(8,128)(2,1)S(1)}, bf16[8,256,256]{2,1,0:T(8,128)(2,1)S(1)}, u32[]{:S(2)}, u32[]{:S(2)}) collective-permute-start(bf16[8,256,256]{2,1,0:T(8,128)(2,1)S(1)} %get-tuple-element.20), channel_id=1, source_target_pairs={{32,0},{64,32},{96,64},{0,96},{33,1},{65,33},{97,65},{1,97},{34,2}... | collective-permute-start | bytes 3145736 | tf_op jit(solution)/shard_map/ppermute | solution.py:54
  65.6 5.1 %collective-permute-start.21 = (bf16[1104,256]{1,0:T(8,128)(2,1)S(1)}, bf16[1104,256]{1,0:T(8,128)(2,1)S(1)}, u32[]{:S(2)}, u32[]{:S(2)}) collective-permute-start(bf16[1104,256]{1,0:T(8,128)(2,1)S(1)} %collective-permute-done.20.refs_1_), channel_id=1, source_target_pairs={{1,0},{0,1},{3,2},{2,3},{5,4},{4,5},{7,6},{6,7},{9,8},{8,9},{11,10... | collective-permute-start | bytes 1695752 | tf_op jit(solution)/shard_map/ppermute | solution.py:50
  70.7 3.2 %collective-permute-done.24.refs_1_ = bf16[1104,256]{1,0:T(8,128)(2,1)S(1)} collective-permute-done((bf16[1104,256]{1,0:T(8,128)(2,1)S(1)}, bf16[1104,256]{1,0:T(8,128)(2,1)S(1)}, u32[]{:S(2)}, u32[]{:S(2)}) %collective-permute-start.24) | collective-permute-done | bytes 565280 | tf_op jit(solution)/shard_map/ppermute | solution.py:46
  74.3 1.2 %keep_pairs.2.base = f32[8,256,256]{2,1,0:T(8,128)S(1)} custom-call(s32[8,128]{1,0:T(8,128)S(1)} %get-tuple-element.17.pairs, f32[8,256,256]{2,1,0:T(8,128)S(1)} %bitcast.20, bf16[8704,256]{1,0:T(8,128)(2,1)S(1)} %put.23.factors, bf16[8,256,256]{2,1,0:T(8,128)(2,1)S(1)} %get-tuple-element.19.refs_0_), custom_call_target="tpu_custom_call" | custom-call | tf_op jit(solution)/shard_map/keep_pairs/pallas_call | solution.py:426
  76.2 1.2 %keep_pairs.3.base = f32[8,256,256]{2,1,0:T(8,128)S(1)} custom-call(s32[8,128]{1,0:T(8,128)S(1)} %unpack.1.pairs, f32[8,256,256]{2,1,0:T(8,128)S(1)} %keep_pairs.2.base, bf16[8704,256]{1,0:T(8,128)(2,1)S(1)} %put.31.factors), custom_call_target="tpu_custom_call" | custom-call | tf_op jit(solution)/shard_map/keep_pairs/pallas_call | solution.py:426
  77.3 10.8 %collective-permute-done.26.refs_0_ = bf16[8,256,256]{2,1,0:T(8,128)(2,1)S(1)} collective-permute-done((bf16[8,256,256]{2,1,0:T(8,128)(2,1)S(1)}, bf16[8,256,256]{2,1,0:T(8,128)(2,1)S(1)}, u32[]{:S(2)}, u32[]{:S(2)}) %collective-permute-start.26) | collective-permute-done | bytes 1048608 | tf_op jit(solution)/shard_map/ppermute | solution.py:54
  88.1 1.3 %collective-permute-done.27.refs_0_ = bf16[8,256,256]{2,1,0:T(8,128)(2,1)S(1)} collective-permute-done((bf16[8,256,256]{2,1,0:T(8,128)(2,1)S(1)}, bf16[8,256,256]{2,1,0:T(8,128)(2,1)S(1)}, u32[]{:S(2)}, u32[]{:S(2)}) %collective-permute-start.27) | collective-permute-done | bytes 1048608 | tf_op jit(solution)/shard_map/ppermute | solution.py:54
  89.4 1.4 %final.1 = f32[8,256,256]{2,1,0:T(8,128)} custom-call(f32[8,256,256]{2,1,0:T(8,128)S(1)} %keep_pairs.3.base, bf16[8,256,256]{2,1,0:T(8,128)(2,1)S(1)} %touch.2.one, bf16[8,256,256]{2,1,0:T(8,128)(2,1)S(1)} %touch.3.two), custom_call_target="tpu_custom_call" | custom-call | tf_op jit(solution)/shard_map/final/pallas_call | solution.py:447
  (61 shorter events, 9.1 us)
Async XLA Ops:
  0.1 0.8 copy-start.1
  3.9 1.3 %collective-permute-start = (f32[16,512]{1,0:T(8,128)S(1)}, f32[16,512]{1,0:T(8,128)S(1)}, u32[]{:S(2)}, u32[]{:S(2)}) collective-permute-start(f32[16,512]{1,0:T(8,128)S(1)} %get-tuple-element.14), channel_id=1, source_target_pairs={{1,0},{0,1},{3,2},{2,3},{5,4},{4,5},{7,6},{6,7},{9,8},{8,9},{11,10... | collective-permute-start | bytes 98312 | tf_op jit(solution)/shard_map/ppermute | solution.py:50
  5.2 4.8 %collective-permute-start.1 = (f32[24,512]{1,0:T(8,128)S(1)}, f32[24,512]{1,0:T(8,128)S(1)}, u32[]{:S(2)}, u32[]{:S(2)}) collective-permute-start(f32[24,512]{1,0:T(8,128)S(1)} %sum_core.1.r0), channel_id=1, source_target_pairs={{2,0},{9,1},{4,2},{11,3},{6,4},{13,5},{0,6},{15,7},{10,8},{17,9},{... | collective-permute-start | bytes 147464 | tf_op jit(solution)/shard_map/ppermute | solution.py:46
  8.2 5.6 %collective-permute-start.2 = (f32[24,512]{1,0:T(8,128)S(1)}, f32[24,512]{1,0:T(8,128)S(1)}, u32[]{:S(2)}, u32[]{:S(2)}) collective-permute-start(f32[24,512]{1,0:T(8,128)S(1)} %sum_core.1.r0), channel_id=1, source_target_pairs={{4,0},{17,1},{6,2},{19,3},{0,4},{21,5},{2,6},{23,7},{12,8},{25,9},... | collective-permute-start | bytes 147464 | tf_op jit(solution)/shard_map/ppermute | solution.py:46
  8.8 5.5 %collective-permute-start.3 = (f32[24,512]{1,0:T(8,128)S(1)}, f32[24,512]{1,0:T(8,128)S(1)}, u32[]{:S(2)}, u32[]{:S(2)}) collective-permute-start(f32[24,512]{1,0:T(8,128)S(1)} %sum_core.1.r0), channel_id=1, source_target_pairs={{6,0},{25,1},{0,2},{27,3},{2,4},{29,5},{4,6},{31,7},{14,8},{1,9},{... | collective-permute-start | bytes 147464 | tf_op jit(solution)/shard_map/ppermute | solution.py:46
  14.3 5.9 %collective-permute-start.4 = (f32[24,512]{1,0:T(8,128)S(1)}, f32[24,512]{1,0:T(8,128)S(1)}, u32[]{:S(2)}, u32[]{:S(2)}) collective-permute-start(f32[24,512]{1,0:T(8,128)S(1)} %sum_first.1.r0), channel_id=1, source_target_pairs={{8,0},{3,1},{10,2},{5,3},{12,4},{7,5},{14,6},{1,7},{16,8},{11,9},{... | collective-permute-start | bytes 147464 | tf_op jit(solution)/shard_map/ppermute | solution.py:46
  18.4 5.7 %collective-permute-start.5 = (f32[24,512]{1,0:T(8,128)S(1)}, f32[24,512]{1,0:T(8,128)S(1)}, u32[]{:S(2)}, u32[]{:S(2)}) collective-permute-start(f32[24,512]{1,0:T(8,128)S(1)} %sum_first.1.r0), channel_id=1, source_target_pairs={{16,0},{5,1},{18,2},{7,3},{20,4},{1,5},{22,6},{3,7},{24,8},{13,9},... | collective-permute-start | bytes 147464 | tf_op jit(solution)/shard_map/ppermute | solution.py:46
  18.4 5.8 %collective-permute-start.6 = (f32[24,512]{1,0:T(8,128)S(1)}, f32[24,512]{1,0:T(8,128)S(1)}, u32[]{:S(2)}, u32[]{:S(2)}) collective-permute-start(f32[24,512]{1,0:T(8,128)S(1)} %sum_first.1.r0), channel_id=1, source_target_pairs={{24,0},{7,1},{26,2},{1,3},{28,4},{3,5},{30,6},{5,7},{0,8},{15,9},{... | collective-permute-start | bytes 147464 | tf_op jit(solution)/shard_map/ppermute | solution.py:46
  24.3 1.4 %collective-permute-start.7 = (f32[48,512]{1,0:T(8,128)S(1)}, f32[48,512]{1,0:T(8,128)S(1)}, u32[]{:S(2)}, u32[]{:S(2)}) collective-permute-start(f32[48,512]{1,0:T(8,128)S(1)} %sum_second.1.own.refs_1_), channel_id=1, source_target_pairs={{1,0},{0,1},{3,2},{2,3},{5,4},{4,5},{7,6},{6,7},{9,8},{8,9},{11,10... | collective-permute-start | bytes 294920 | tf_op jit(solution)/shard_map/ppermute | solution.py:50
  29.1 5.1 %collective-permute-start.8 = (bf16[272,256]{1,0:T(8,128)(2,1)S(1)}, bf16[272,256]{1,0:T(8,128)(2,1)S(1)}, u32[]{:S(2)}, u32[]{:S(2)}) collective-permute-start(bf16[272,256]{1,0:T(8,128)(2,1)S(1)} %factor.1.refs_3_.refs_0_), channel_id=1, source_target_pairs={{2,0},{9,1},{4,2},{11,3},{6,4},{13,5},{0,6},{15,7},{10,8},{17,9},{... | collective-permute-start | bytes 417800 | tf_op jit(solution)/shard_map/ppermute | solution.py:46
  29.8 6.6 %collective-permute-start.9 = (bf16[272,256]{1,0:T(8,128)(2,1)S(1)}, bf16[272,256]{1,0:T(8,128)(2,1)S(1)}, u32[]{:S(2)}, u32[]{:S(2)}) collective-permute-start(bf16[272,256]{1,0:T(8,128)(2,1)S(1)} %factor.1.refs_3_.refs_0_), channel_id=1, source_target_pairs={{4,0},{17,1},{6,2},{19,3},{0,4},{21,5},{2,6},{23,7},{12,8},{25,9},... | collective-permute-start | bytes 417800 | tf_op jit(solution)/shard_map/ppermute | solution.py:46
  30.8 7.0 %collective-permute-start.10 = (bf16[272,256]{1,0:T(8,128)(2,1)S(1)}, bf16[272,256]{1,0:T(8,128)(2,1)S(1)}, u32[]{:S(2)}, u32[]{:S(2)}) collective-permute-start(bf16[272,256]{1,0:T(8,128)(2,1)S(1)} %factor.1.refs_3_.refs_0_), channel_id=1, source_target_pairs={{6,0},{25,1},{0,2},{27,3},{2,4},{29,5},{4,6},{31,7},{14,8},{1,9},{... | collective-permute-start | bytes 417800 | tf_op jit(solution)/shard_map/ppermute | solution.py:46
  37.9 9.6 %collective-permute-start.13 = (bf16[1088,256]{1,0:T(8,128)(2,1)S(1)}, bf16[1088,256]{1,0:T(8,128)(2,1)S(1)}, u32[]{:S(2)}, u32[]{:S(2)}) collective-permute-start(bf16[1088,256]{1,0:T(8,128)(2,1)S(1)} %join_line.1.refs_0_), channel_id=1, source_target_pairs={{8,0},{3,1},{10,2},{5,3},{12,4},{7,5},{14,6},{1,7},{16,8},{11,9},{... | collective-permute-start | bytes 1671176 | tf_op jit(solution)/shard_map/ppermute | solution.py:46
  38.8 11.1 %collective-permute-start.15 = (bf16[1088,256]{1,0:T(8,128)(2,1)S(1)}, bf16[1088,256]{1,0:T(8,128)(2,1)S(1)}, u32[]{:S(2)}, u32[]{:S(2)}) collective-permute-start(bf16[1088,256]{1,0:T(8,128)(2,1)S(1)} %join_line.1.refs_0_), channel_id=1, source_target_pairs={{16,0},{5,1},{18,2},{7,3},{20,4},{1,5},{22,6},{3,7},{24,8},{13,9},... | collective-permute-start | bytes 1671176 | tf_op jit(solution)/shard_map/ppermute | solution.py:46
  39.9 14.7 %collective-permute-start.11 = (bf16[1104,256]{1,0:T(8,128)(2,1)S(1)}, bf16[1104,256]{1,0:T(8,128)(2,1)S(1)}, u32[]{:S(2)}, u32[]{:S(2)}) collective-permute-start(bf16[1104,256]{1,0:T(8,128)(2,1)S(1)} %join_far.1), channel_id=1, source_target_pairs={{64,0},{96,32},{0,64},{32,96},{65,1},{97,33},{1,65},{33,97},{66,2}... | collective-permute-start | bytes 1695752 | tf_op jit(solution)/shard_map/ppermute | solution.py:54
  41.3 14.4 %collective-permute-start.17 = (bf16[1088,256]{1,0:T(8,128)(2,1)S(1)}, bf16[1088,256]{1,0:T(8,128)(2,1)S(1)}, u32[]{:S(2)}, u32[]{:S(2)}) collective-permute-start(bf16[1088,256]{1,0:T(8,128)(2,1)S(1)} %join_line.1.refs_0_), channel_id=1, source_target_pairs={{24,0},{7,1},{26,2},{1,3},{28,4},{3,5},{30,6},{5,7},{0,8},{15,9},{... | collective-permute-start | bytes 1671176 | tf_op jit(solution)/shard_map/ppermute | solution.py:46
  42.7 13.1 %collective-permute-start.12 = (bf16[1088,256]{1,0:T(8,128)(2,1)S(1)}, bf16[1088,256]{1,0:T(8,128)(2,1)S(1)}, u32[]{:S(2)}, u32[]{:S(2)}) collective-permute-start(bf16[1088,256]{1,0:T(8,128)(2,1)S(1)} %join_line.1.refs_0_), channel_id=1, source_target_pairs={{1,0},{0,1},{3,2},{2,3},{5,4},{4,5},{7,6},{6,7},{9,8},{8,9},{11,10... | collective-permute-start | bytes 1671176 | tf_op jit(solution)/shard_map/ppermute | solution.py:50
  47.5 9.3 %collective-permute-start.14 = (bf16[1088,256]{1,0:T(8,128)(2,1)S(1)}, bf16[1088,256]{1,0:T(8,128)(2,1)S(1)}, u32[]{:S(2)}, u32[]{:S(2)}) collective-permute-start(bf16[1088,256]{1,0:T(8,128)(2,1)S(1)} %collective-permute-done.13.refs_1_), channel_id=1, source_target_pairs={{1,0},{0,1},{3,2},{2,3},{5,4},{4,5},{7,6},{6,7},{9,8},{8,9},{11,10... | collective-permute-start | bytes 1671176 | tf_op jit(solution)/shard_map/ppermute | solution.py:50
  49.9 7.5 %collective-permute-start.16 = (bf16[1088,256]{1,0:T(8,128)(2,1)S(1)}, bf16[1088,256]{1,0:T(8,128)(2,1)S(1)}, u32[]{:S(2)}, u32[]{:S(2)}) collective-permute-start(bf16[1088,256]{1,0:T(8,128)(2,1)S(1)} %collective-permute-done.15.refs_1_), channel_id=1, source_target_pairs={{1,0},{0,1},{3,2},{2,3},{5,4},{4,5},{7,6},{6,7},{9,8},{8,9},{11,10... | collective-permute-start | bytes 1671176 | tf_op jit(solution)/shard_map/ppermute | solution.py:50
  54.6 9.0 %collective-permute-start.19 = (bf16[1104,256]{1,0:T(8,128)(2,1)S(1)}, bf16[1104,256]{1,0:T(8,128)(2,1)S(1)}, u32[]{:S(2)}, u32[]{:S(2)}) collective-permute-start(bf16[1104,256]{1,0:T(8,128)(2,1)S(1)} %collective-permute-done.11.message.refs_0_), channel_id=1, source_target_pairs={{1,0},{0,1},{3,2},{2,3},{5,4},{4,5},{7,6},{6,7},{9,8},{8,9},{11,10... | collective-permute-start | bytes 1695752 | tf_op jit(solution)/shard_map/ppermute | solution.py:50
  55.8 3.2 %collective-permute-start.18 = (bf16[1088,256]{1,0:T(8,128)(2,1)S(1)}, bf16[1088,256]{1,0:T(8,128)(2,1)S(1)}, u32[]{:S(2)}, u32[]{:S(2)}) collective-permute-start(bf16[1088,256]{1,0:T(8,128)(2,1)S(1)} %collective-permute-done.17.refs_1_), channel_id=1, source_target_pairs={{1,0},{0,1},{3,2},{2,3},{5,4},{4,5},{7,6},{6,7},{9,8},{8,9},{11,10... | collective-permute-start | bytes 1671176 | tf_op jit(solution)/shard_map/ppermute | solution.py:50
  55.8 9.8 %collective-permute-start.20 = (bf16[1104,256]{1,0:T(8,128)(2,1)S(1)}, bf16[1104,256]{1,0:T(8,128)(2,1)S(1)}, u32[]{:S(2)}, u32[]{:S(2)}) collective-permute-start(bf16[1104,256]{1,0:T(8,128)(2,1)S(1)} %collective-permute-done.11.message.refs_0_), channel_id=1, source_target_pairs={{8,0},{3,1},{10,2},{5,3},{12,4},{7,5},{14,6},{1,7},{16,8},{11,9},{... | collective-permute-start | bytes 1695752 | tf_op jit(solution)/shard_map/ppermute | solution.py:46
  56.7 13.9 %collective-permute-start.22 = (bf16[1104,256]{1,0:T(8,128)(2,1)S(1)}, bf16[1104,256]{1,0:T(8,128)(2,1)S(1)}, u32[]{:S(2)}, u32[]{:S(2)}) collective-permute-start(bf16[1104,256]{1,0:T(8,128)(2,1)S(1)} %collective-permute-done.11.message.refs_0_), channel_id=1, source_target_pairs={{16,0},{5,1},{18,2},{7,3},{20,4},{1,5},{22,6},{3,7},{24,8},{13,9},... | collective-permute-start | bytes 1695752 | tf_op jit(solution)/shard_map/ppermute | solution.py:46
  57.4 16.5 %collective-permute-start.24 = (bf16[1104,256]{1,0:T(8,128)(2,1)S(1)}, bf16[1104,256]{1,0:T(8,128)(2,1)S(1)}, u32[]{:S(2)}, u32[]{:S(2)}) collective-permute-start(bf16[1104,256]{1,0:T(8,128)(2,1)S(1)} %collective-permute-done.11.message.refs_0_), channel_id=1, source_target_pairs={{24,0},{7,1},{26,2},{1,3},{28,4},{3,5},{30,6},{5,7},{0,8},{15,9},{... | collective-permute-start | bytes 1695752 | tf_op jit(solution)/shard_map/ppermute | solution.py:46
  59.0 15.2 %copy-start = (f32[1,8,256,256]{3,2,1,0:T(8,128)S(1)}, f32[1,8,256,256]{3,2,1,0:T(8,128)}, u32[]{:S(2)}) copy-start(f32[1,8,256,256]{3,2,1,0:T(8,128)} %param.9) | copy-start | bytes 6291460
  63.5 24.6 %collective-permute-start.26 = (bf16[8,256,256]{2,1,0:T(8,128)(2,1)S(1)}, bf16[8,256,256]{2,1,0:T(8,128)(2,1)S(1)}, u32[]{:S(2)}, u32[]{:S(2)}) collective-permute-start(bf16[8,256,256]{2,1,0:T(8,128)(2,1)S(1)} %get-tuple-element.19.refs_0_), channel_id=1, source_target_pairs={{96,0},{0,32},{32,64},{64,96},{97,1},{1,33},{33,65},{65,97},{98,2}... | collective-permute-start | bytes 3145736 | tf_op jit(solution)/shard_map/ppermute | solution.py:54
  63.6 25.8 %collective-permute-start.27 = (bf16[8,256,256]{2,1,0:T(8,128)(2,1)S(1)}, bf16[8,256,256]{2,1,0:T(8,128)(2,1)S(1)}, u32[]{:S(2)}, u32[]{:S(2)}) collective-permute-start(bf16[8,256,256]{2,1,0:T(8,128)(2,1)S(1)} %get-tuple-element.20), channel_id=1, source_target_pairs={{32,0},{64,32},{96,64},{0,96},{33,1},{65,33},{97,65},{1,97},{34,2}... | collective-permute-start | bytes 3145736 | tf_op jit(solution)/shard_map/ppermute | solution.py:54
  65.6 10.1 %collective-permute-start.21 = (bf16[1104,256]{1,0:T(8,128)(2,1)S(1)}, bf16[1104,256]{1,0:T(8,128)(2,1)S(1)}, u32[]{:S(2)}, u32[]{:S(2)}) collective-permute-start(bf16[1104,256]{1,0:T(8,128)(2,1)S(1)} %collective-permute-done.20.refs_1_), channel_id=1, source_target_pairs={{1,0},{0,1},{3,2},{2,3},{5,4},{4,5},{7,6},{6,7},{9,8},{8,9},{11,10... | collective-permute-start | bytes 1695752 | tf_op jit(solution)/shard_map/ppermute | solution.py:50
  70.7 5.2 %collective-permute-start.23 = (bf16[1104,256]{1,0:T(8,128)(2,1)S(1)}, bf16[1104,256]{1,0:T(8,128)(2,1)S(1)}, u32[]{:S(2)}, u32[]{:S(2)}) collective-permute-start(bf16[1104,256]{1,0:T(8,128)(2,1)S(1)} %collective-permute-done.22.refs_1_), channel_id=1, source_target_pairs={{1,0},{0,1},{3,2},{2,3},{5,4},{4,5},{7,6},{6,7},{9,8},{8,9},{11,10... | collective-permute-start | bytes 1695752 | tf_op jit(solution)/shard_map/ppermute | solution.py:50
  73.9 2.2 %collective-permute-start.25 = (bf16[1104,256]{1,0:T(8,128)(2,1)S(1)}, bf16[1104,256]{1,0:T(8,128)(2,1)S(1)}, u32[]{:S(2)}, u32[]{:S(2)}) collective-permute-start(bf16[1104,256]{1,0:T(8,128)(2,1)S(1)} %collective-permute-done.24.refs_1_), channel_id=1, source_target_pairs={{1,0},{0,1},{3,2},{2,3},{5,4},{4,5},{7,6},{6,7},{9,8},{8,9},{11,10... | collective-permute-start | bytes 1695752 | tf_op jit(solution)/shard_map/ppermute | solution.py:50

commit v5 on v4

--- a/solution.py
+++ b/solution.py
@@ -18,6 +18,7 @@
 SLOTS = 2
 SKETCH_STEPS = 4
 PER_CHUNK = 8
+TURN = 4
 ENTRIES = N_CAND * SLOTS
 ZERO = NB_DEV * N_CAND
 LAST_US = 0
@@ -366,20 +367,20 @@
             lefts[side, here, :] = block_at(factors, pairs[4, spot]) * weight
             rights[side, here, :] = block_at(factors, pairs[5, spot])
 
-    def couple(n, last):
-        chunk(2 * n, 0)
-        chunk(2 * n + 1, 1)
+    def several(n, last):
+        for side in range(TURN):
+            chunk(TURN * n + side, side)
         terms = [
             lax.dot_general(lefts[side], rights[side], TN, preferred_element_type=f32)
-            for side in range(2)
+            for side in range(TURN)
         ]
-        for side in range(2):
-            t = pairs[2, 2 * n + side]
+        for side in range(TURN):
+            t = pairs[2, TURN * n + side]
             totals[t] = jnp.where(t == last, totals[t], 0.0) + terms[side]
             last = t
         return last
 
-    lax.fori_loop(0, (pairs[3, 0] + 1) // 2, couple, -1)
+    lax.fori_loop(0, (pairs[3, 0] + (TURN - 1)) // TURN, several, -1)
 
 
 def total_of(pairs, t, totals):
@@ -388,8 +389,8 @@
 
 WORK = [
     pltpu.VMEM((ZERO + 8, 128), f32),
-    pltpu.VMEM((2, RANK * PER_CHUNK, BLOCK), bf16),
-    pltpu.VMEM((2, RANK * PER_CHUNK, BLOCK), bf16),
+    pltpu.VMEM((TURN, RANK * PER_CHUNK, BLOCK), bf16),
+    pltpu.VMEM((TURN, RANK * PER_CHUNK, BLOCK), bf16),
     pltpu.VMEM((NT_DEV, BLOCK, BLOCK), f32),
 ]
 

time: 91.5 us -> 91.8 us (level)
  waiting for transfers between devices: 43.7 us -> 42.6 us
    ppermute x3, waiting for transfers between devices: 16.8 us -> 14.4 us  [from_set(): lax.ppermute(x, 'set', [((me + d) % N_SET, me) for me in range(N_SET)])]
    pallas_call x2, Pallas kernels: 2.32 us -> 4.37 us  [keep_call(): pl.pallas_call(kernel, out_shape=jax.ShapeDtypeStruct((NT_DEV, BLOCK, BLO...]
    pallas_call x1, Pallas kernels: 4.42 us -> 3.07 us  [send_call(): pl.pallas_call(kernel, out_shape=(out, out), in_specs=[SMEM, SMEM, VMEM]...]
    ppermute x15, waiting for transfers between devices: 25.2 us -> 26.4 us  [from_cand(): return lax.ppermute(x, 'cand', pairs)]
  transfers between devices with their start and end apart: 28 -> 28, of which waited for: 18 -> 19; matrix products, arithmetic and copies ran while one was open for 1% -> 1% of each run, Pallas kernels for 10% -> 11%
where the time goes in v5:
time: 91.8 us; the launch traced here: 90.6 us
  waiting for transfers between devices  42.6 us (46%)
  starting transfers between devices  28 us (31%)
  Pallas kernels  18.1 us (20%)
    ppermute x15, waiting for transfers between devices, from_cand(): return lax.ppermute(x, 'cand', pairs)  26.4 us
    ppermute x15, starting transfers between devices, from_cand(): return lax.ppermute(x, 'cand', pairs)  18.7 us
    ppermute x3, waiting for transfers between devices, from_set(): lax.ppermute(x, 'set', [((me + d) % N_SET, me) for me in range(N_SET)])  14.4 us
    ppermute x10, starting transfers between devices, from_core(): return lax.ppermute(x, 'cand', [(me ^ 1, me) for me in range(N_CAND)])  5.69 us
    pallas_call x2, Pallas kernels, keep_call(): pl.pallas_call(kernel, out_shape=jax.ShapeDtypeStruct((NT_DEV, BLOCK, BLO...  4.37 us
    ppermute x3, starting transfers between devices, from_set(): lax.ppermute(x, 'set', [((me + d) % N_SET, me) for me in range(N_SET)])  3.58 us
    pallas_call x1, Pallas kernels, factor_call(): pl.pallas_call(factor_kernel, out_shape=jax.ShapeDtypeStruct((MSG, BLOCK)...  3.45 us
    pallas_call x1, Pallas kernels, send_call(): pl.pallas_call(kernel, out_shape=(out, out), in_specs=[SMEM, SMEM, VMEM]...  3.07 us
  transfers between devices with their start and end apart: 28, of which 19 were waited for; matrix products, arithmetic and copies ran while one was open for 1% of the time, Pallas kernels for 11%

profile of v5, /device:TPU:6, one launch (start us, length us, event | category | flops | bytes accessed | tf_op | source)
XLA Modules:
  0.0 90.6 jit_solution(10711751651038498472)
XLA Ops:
  0.8 3.1 %sketch.1 = (f32[16,512]{1,0:T(8,128)S(1)}, f32[16,512]{1,0:T(8,128)S(1)}) custom-call(s32[2]{0:T(128)S(1)} %pad_add_fusion.place.refs_0_, bf16[2048,512]{1,0:T(8,128)(2,1)} %bitcast.22, bf16[32,512]{1,0:T(8,128)(2,1)S(1)} %bitcast.21), custom_call_target="tpu_custom_call" | custom-call | tf_op jit(solution)/shard_map/sketch/pallas_call | solution.py:78
  5.2 3.0 %collective-permute-start.1 = (f32[24,512]{1,0:T(8,128)S(1)}, f32[24,512]{1,0:T(8,128)S(1)}, u32[]{:S(2)}, u32[]{:S(2)}) collective-permute-start(f32[24,512]{1,0:T(8,128)S(1)} %sum_core.1.r0), channel_id=1, source_target_pairs={{2,0},{9,1},{4,2},{11,3},{6,4},{13,5},{0,6},{15,7},{10,8},{17,9},{... | collective-permute-start | bytes 147464 | tf_op jit(solution)/shard_map/ppermute | solution.py:47
  8.8 1.0 %collective-permute-start.3 = (f32[24,512]{1,0:T(8,128)S(1)}, f32[24,512]{1,0:T(8,128)S(1)}, u32[]{:S(2)}, u32[]{:S(2)}) collective-permute-start(f32[24,512]{1,0:T(8,128)S(1)} %sum_core.1.r0), channel_id=1, source_target_pairs={{6,0},{25,1},{0,2},{27,3},{2,4},{29,5},{4,6},{31,7},{14,8},{1,9},{... | collective-permute-start | bytes 147464 | tf_op jit(solution)/shard_map/ppermute | solution.py:47
  10.0 3.9 %collective-permute-done.2.r2 = f32[24,512]{1,0:T(8,128)S(1)} collective-permute-done((f32[24,512]{1,0:T(8,128)S(1)}, f32[24,512]{1,0:T(8,128)S(1)}, u32[]{:S(2)}, u32[]{:S(2)}) %collective-permute-start.2) | collective-permute-done | bytes 49184 | tf_op jit(solution)/shard_map/ppermute | solution.py:47
  14.3 4.1 %collective-permute-start.4 = (f32[24,512]{1,0:T(8,128)S(1)}, f32[24,512]{1,0:T(8,128)S(1)}, u32[]{:S(2)}, u32[]{:S(2)}) collective-permute-start(f32[24,512]{1,0:T(8,128)S(1)} %sum_first.1.r0), channel_id=1, source_target_pairs={{8,0},{3,1},{10,2},{5,3},{12,4},{7,5},{14,6},{1,7},{16,8},{11,9},{... | collective-permute-start | bytes 147464 | tf_op jit(solution)/shard_map/ppermute | solution.py:47
  18.4 1.3 %collective-permute-start.6 = (f32[24,512]{1,0:T(8,128)S(1)}, f32[24,512]{1,0:T(8,128)S(1)}, u32[]{:S(2)}, u32[]{:S(2)}) collective-permute-start(f32[24,512]{1,0:T(8,128)S(1)} %sum_first.1.r0), channel_id=1, source_target_pairs={{24,0},{7,1},{26,2},{1,3},{28,4},{3,5},{30,6},{5,7},{0,8},{15,9},{... | collective-permute-start | bytes 147464 | tf_op jit(solution)/shard_map/ppermute | solution.py:47
  20.2 3.9 %collective-permute-done.5.r2 = f32[24,512]{1,0:T(8,128)S(1)} collective-permute-done((f32[24,512]{1,0:T(8,128)S(1)}, f32[24,512]{1,0:T(8,128)S(1)}, u32[]{:S(2)}, u32[]{:S(2)}) %collective-permute-start.5) | collective-permute-done | bytes 49184 | tf_op jit(solution)/shard_map/ppermute | solution.py:47
  24.4 1.3 %collective-permute-done.7.other.refs_2_ = f32[48,512]{1,0:T(8,128)S(1)} collective-permute-done((f32[48,512]{1,0:T(8,128)S(1)}, f32[48,512]{1,0:T(8,128)S(1)}, u32[]{:S(2)}, u32[]{:S(2)}) %collective-permute-start.7) | collective-permute-done | bytes 98336 | tf_op jit(solution)/shard_map/ppermute | solution.py:51
  25.7 3.5 %factor.1.refs_3_.refs_0_ = bf16[272,256]{1,0:T(8,128)(2,1)S(1)} custom-call(s32[2]{0:T(128)S(1)} %pad_add_fusion.place.refs_0_, f32[48,512]{1,0:T(8,128)S(1)} %sum_second.1.own.refs_1_, f32[48,512]{1,0:T(8,128)S(1)} %collective-permute-done.7.other.refs_2_, bf16[2048,512]{1,0:T(8,128)(2,1)} %bitcast.23), custom_call_target="tpu_custom_call" | custom-call | tf_op jit(solution)/shard_map/factor/pallas_call | solution.py:171
  29.8 1.1 %collective-permute-start.9 = (bf16[272,256]{1,0:T(8,128)(2,1)S(1)}, bf16[272,256]{1,0:T(8,128)(2,1)S(1)}, u32[]{:S(2)}, u32[]{:S(2)}) collective-permute-start(bf16[272,256]{1,0:T(8,128)(2,1)S(1)} %factor.1.refs_3_.refs_0_), channel_id=1, source_target_pairs={{4,0},{17,1},{6,2},{19,3},{0,4},{21,5},{2,6},{23,7},{12,8},{25,9},... | collective-permute-start | bytes 417800 | tf_op jit(solution)/shard_map/ppermute | solution.py:47
  30.8 1.3 %collective-permute-start.10 = (bf16[272,256]{1,0:T(8,128)(2,1)S(1)}, bf16[272,256]{1,0:T(8,128)(2,1)S(1)}, u32[]{:S(2)}, u32[]{:S(2)}) collective-permute-start(bf16[272,256]{1,0:T(8,128)(2,1)S(1)} %factor.1.refs_3_.refs_0_), channel_id=1, source_target_pairs={{6,0},{25,1},{0,2},{27,3},{2,4},{29,5},{4,6},{31,7},{14,8},{1,9},{... | collective-permute-start | bytes 417800 | tf_op jit(solution)/shard_map/ppermute | solution.py:47
  32.1 1.2 %plan.1 = (s32[8,128]{1,0:T(8,128)S(1)}, s32[8,128]{1,0:T(8,128)S(1)}, bf16[16,256]{1,0:T(8,128)(2,1)S(1)}, s32[8,128]{1,0:T(8,128)S(1)}) custom-call(s32[2]{0:T(128)S(1)} %pad_add_fusion.place.refs_0_, f32[48,512]{1,0:T(8,128)S(1)} %sum_second.1.own.refs_1_, f32[48,512]{1,0:T(8,128)S(1)} %collective-permute-done.7.other.refs_2_, ...), custom_call_target="tpu_custom_call" | custom-call | tf_op jit(solution)/shard_map/plan/pallas_call | solution.py:321
  34.3 2.1 %collective-permute-done.9.refs_2_ = bf16[272,256]{1,0:T(8,128)(2,1)S(1)} collective-permute-done((bf16[272,256]{1,0:T(8,128)(2,1)S(1)}, bf16[272,256]{1,0:T(8,128)(2,1)S(1)}, u32[]{:S(2)}, u32[]{:S(2)}) %collective-permute-start.9) | collective-permute-done | bytes 139296 | tf_op jit(solution)/shard_map/ppermute | solution.py:47
  36.4 1.4 %collective-permute-done.10.refs_3_ = bf16[272,256]{1,0:T(8,128)(2,1)S(1)} collective-permute-done((bf16[272,256]{1,0:T(8,128)(2,1)S(1)}, bf16[272,256]{1,0:T(8,128)(2,1)S(1)}, u32[]{:S(2)}, u32[]{:S(2)}) %collective-permute-start.10) | collective-permute-done | bytes 139296 | tf_op jit(solution)/shard_map/ppermute | solution.py:47
  37.9 0.9 %collective-permute-start.13 = (bf16[1088,256]{1,0:T(8,128)(2,1)S(1)}, bf16[1088,256]{1,0:T(8,128)(2,1)S(1)}, u32[]{:S(2)}, u32[]{:S(2)}) collective-permute-start(bf16[1088,256]{1,0:T(8,128)(2,1)S(1)} %join_line.1.refs_0_), channel_id=1, source_target_pairs={{8,0},{3,1},{10,2},{5,3},{12,4},{7,5},{14,6},{1,7},{16,8},{11,9},{... | collective-permute-start | bytes 1671176 | tf_op jit(solution)/shard_map/ppermute | solution.py:47
  38.8 1.0 %collective-permute-start.15 = (bf16[1088,256]{1,0:T(8,128)(2,1)S(1)}, bf16[1088,256]{1,0:T(8,128)(2,1)S(1)}, u32[]{:S(2)}, u32[]{:S(2)}) collective-permute-start(bf16[1088,256]{1,0:T(8,128)(2,1)S(1)} %join_line.1.refs_0_), channel_id=1, source_target_pairs={{16,0},{5,1},{18,2},{7,3},{20,4},{1,5},{22,6},{3,7},{24,8},{13,9},... | collective-permute-start | bytes 1671176 | tf_op jit(solution)/shard_map/ppermute | solution.py:47
  39.9 1.5 %collective-permute-start.11 = (bf16[1104,256]{1,0:T(8,128)(2,1)S(1)}, bf16[1104,256]{1,0:T(8,128)(2,1)S(1)}, u32[]{:S(2)}, u32[]{:S(2)}) collective-permute-start(bf16[1104,256]{1,0:T(8,128)(2,1)S(1)} %join_far.1), channel_id=1, source_target_pairs={{64,0},{96,32},{0,64},{32,96},{65,1},{97,33},{1,65},{33,97},{66,2}... | collective-permute-start | bytes 1695752 | tf_op jit(solution)/shard_map/ppermute | solution.py:55
  41.3 1.3 %collective-permute-start.17 = (bf16[1088,256]{1,0:T(8,128)(2,1)S(1)}, bf16[1088,256]{1,0:T(8,128)(2,1)S(1)}, u32[]{:S(2)}, u32[]{:S(2)}) collective-permute-start(bf16[1088,256]{1,0:T(8,128)(2,1)S(1)} %join_line.1.refs_0_), channel_id=1, source_target_pairs={{24,0},{7,1},{26,2},{1,3},{28,4},{3,5},{30,6},{5,7},{0,8},{15,9},{... | collective-permute-start | bytes 1671176 | tf_op jit(solution)/shard_map/ppermute | solution.py:47
  42.7 4.8 %collective-permute-done.13.refs_1_ = bf16[1088,256]{1,0:T(8,128)(2,1)S(1)} collective-permute-done((bf16[1088,256]{1,0:T(8,128)(2,1)S(1)}, bf16[1088,256]{1,0:T(8,128)(2,1)S(1)}, u32[]{:S(2)}, u32[]{:S(2)}) %collective-permute-start.13) | collective-permute-done | bytes 557088 | tf_op jit(solution)/shard_map/ppermute | solution.py:47
  47.5 2.5 %collective-permute-done.15.refs_1_ = bf16[1088,256]{1,0:T(8,128)(2,1)S(1)} collective-permute-done((bf16[1088,256]{1,0:T(8,128)(2,1)S(1)}, bf16[1088,256]{1,0:T(8,128)(2,1)S(1)}, u32[]{:S(2)}, u32[]{:S(2)}) %collective-permute-start.15) | collective-permute-done | bytes 557088 | tf_op jit(solution)/shard_map/ppermute | solution.py:47
  49.9 4.7 %collective-permute-done.11.message.refs_0_ = bf16[1104,256]{1,0:T(8,128)(2,1)S(1)} collective-permute-done((bf16[1104,256]{1,0:T(8,128)(2,1)S(1)}, bf16[1104,256]{1,0:T(8,128)(2,1)S(1)}, u32[]{:S(2)}, u32[]{:S(2)}) %collective-permute-start.11) | collective-permute-done | bytes 565280 | tf_op jit(solution)/shard_map/ppermute | solution.py:55
  54.6 1.2 %collective-permute-done.17.refs_1_ = bf16[1088,256]{1,0:T(8,128)(2,1)S(1)} collective-permute-done((bf16[1088,256]{1,0:T(8,128)(2,1)S(1)}, bf16[1088,256]{1,0:T(8,128)(2,1)S(1)}, u32[]{:S(2)}, u32[]{:S(2)}) %collective-permute-start.17) | collective-permute-done | bytes 557088 | tf_op jit(solution)/shard_map/ppermute | solution.py:47
  59.1 3.1 %send_pairs.1 = (bf16[8,256,256]{2,1,0:T(8,128)(2,1)S(1)}, bf16[8,256,256]{2,1,0:T(8,128)(2,1)S(1)}) custom-call(s32[8,128]{1,0:T(8,128)S(1)} %get-tuple-element.15.refs_4_.next_list, s32[8,128]{1,0:T(8,128)S(1)} %get-tuple-element.18.last_list, bf16[8704,256]{1,0:T(8,128)(2,1)S(1)} %put.23.factors), custom_call_target="tpu_custom_call" | custom-call | tf_op jit(solution)/shard_map/send_pairs/pallas_call | solution.py:408
  62.2 2.0 %collective-permute-start.27 = (bf16[8,256,256]{2,1,0:T(8,128)(2,1)S(1)}, bf16[8,256,256]{2,1,0:T(8,128)(2,1)S(1)}, u32[]{:S(2)}, u32[]{:S(2)}) collective-permute-start(bf16[8,256,256]{2,1,0:T(8,128)(2,1)S(1)} %get-tuple-element.20), channel_id=1, source_target_pairs={{32,0},{64,32},{96,64},{0,96},{33,1},{65,33},{97,65},{1,97},{34,2}... | collective-permute-start | bytes 3145736 | tf_op jit(solution)/shard_map/ppermute | solution.py:55
  64.2 1.2 %collective-permute-done.20.refs_1_ = bf16[1104,256]{1,0:T(8,128)(2,1)S(1)} collective-permute-done((bf16[1104,256]{1,0:T(8,128)(2,1)S(1)}, bf16[1104,256]{1,0:T(8,128)(2,1)S(1)}, u32[]{:S(2)}, u32[]{:S(2)}) %collective-permute-start.20) | collective-permute-done | bytes 565280 | tf_op jit(solution)/shard_map/ppermute | solution.py:47
  65.4 5.2 %collective-permute-start.21 = (bf16[1104,256]{1,0:T(8,128)(2,1)S(1)}, bf16[1104,256]{1,0:T(8,128)(2,1)S(1)}, u32[]{:S(2)}, u32[]{:S(2)}) collective-permute-start(bf16[1104,256]{1,0:T(8,128)(2,1)S(1)} %collective-permute-done.20.refs_1_), channel_id=1, source_target_pairs={{1,0},{0,1},{3,2},{2,3},{5,4},{4,5},{7,6},{6,7},{9,8},{8,9},{11,10... | collective-permute-start | bytes 1695752 | tf_op jit(solution)/shard_map/ppermute | solution.py:51
  70.7 3.2 %collective-permute-done.24.refs_1_ = bf16[1104,256]{1,0:T(8,128)(2,1)S(1)} collective-permute-done((bf16[1104,256]{1,0:T(8,128)(2,1)S(1)}, bf16[1104,256]{1,0:T(8,128)(2,1)S(1)}, u32[]{:S(2)}, u32[]{:S(2)}) %collective-permute-start.24) | collective-permute-done | bytes 565280 | tf_op jit(solution)/shard_map/ppermute | solution.py:47
  74.3 2.2 %keep_pairs.2.base = f32[8,256,256]{2,1,0:T(8,128)S(1)} custom-call(s32[8,128]{1,0:T(8,128)S(1)} %get-tuple-element.17.pairs, f32[8,256,256]{2,1,0:T(8,128)S(1)} %bitcast.20, bf16[8704,256]{1,0:T(8,128)(2,1)S(1)} %put.23.factors, bf16[8,256,256]{2,1,0:T(8,128)(2,1)S(1)} %get-tuple-element.19.refs_0_), custom_call_target="tpu_custom_call" | custom-call | tf_op jit(solution)/shard_map/keep_pairs/pallas_call | solution.py:427
  77.2 2.2 %keep_pairs.3.base = f32[8,256,256]{2,1,0:T(8,128)S(1)} custom-call(s32[8,128]{1,0:T(8,128)S(1)} %unpack.1.pairs, f32[8,256,256]{2,1,0:T(8,128)S(1)} %keep_pairs.2.base, bf16[8704,256]{1,0:T(8,128)(2,1)S(1)} %put.31.factors), custom_call_target="tpu_custom_call" | custom-call | tf_op jit(solution)/shard_map/keep_pairs/pallas_call | solution.py:427
  79.4 8.4 %collective-permute-done.26.refs_0_ = bf16[8,256,256]{2,1,0:T(8,128)(2,1)S(1)} collective-permute-done((bf16[8,256,256]{2,1,0:T(8,128)(2,1)S(1)}, bf16[8,256,256]{2,1,0:T(8,128)(2,1)S(1)}, u32[]{:S(2)}, u32[]{:S(2)}) %collective-permute-start.26) | collective-permute-done | bytes 1048608 | tf_op jit(solution)/shard_map/ppermute | solution.py:55
  87.7 1.4 %collective-permute-done.27.refs_0_ = bf16[8,256,256]{2,1,0:T(8,128)(2,1)S(1)} collective-permute-done((bf16[8,256,256]{2,1,0:T(8,128)(2,1)S(1)}, bf16[8,256,256]{2,1,0:T(8,128)(2,1)S(1)}, u32[]{:S(2)}, u32[]{:S(2)}) %collective-permute-start.27) | collective-permute-done | bytes 1048608 | tf_op jit(solution)/shard_map/ppermute | solution.py:55
  89.1 1.4 %final.1 = f32[8,256,256]{2,1,0:T(8,128)} custom-call(f32[8,256,256]{2,1,0:T(8,128)S(1)} %keep_pairs.3.base, bf16[8,256,256]{2,1,0:T(8,128)(2,1)S(1)} %touch.2.one, bf16[8,256,256]{2,1,0:T(8,128)(2,1)S(1)} %touch.3.two), custom_call_target="tpu_custom_call" | custom-call | tf_op jit(solution)/shard_map/final/pallas_call | solution.py:448
  (61 shorter events, 10.1 us)
Async XLA Ops:
  0.1 0.8 copy-start.1
  3.9 1.3 %collective-permute-start = (f32[16,512]{1,0:T(8,128)S(1)}, f32[16,512]{1,0:T(8,128)S(1)}, u32[]{:S(2)}, u32[]{:S(2)}) collective-permute-start(f32[16,512]{1,0:T(8,128)S(1)} %get-tuple-element.14), channel_id=1, source_target_pairs={{1,0},{0,1},{3,2},{2,3},{5,4},{4,5},{7,6},{6,7},{9,8},{8,9},{11,10... | collective-permute-start | bytes 98312 | tf_op jit(solution)/shard_map/ppermute | solution.py:51
  5.2 4.8 %collective-permute-start.1 = (f32[24,512]{1,0:T(8,128)S(1)}, f32[24,512]{1,0:T(8,128)S(1)}, u32[]{:S(2)}, u32[]{:S(2)}) collective-permute-start(f32[24,512]{1,0:T(8,128)S(1)} %sum_core.1.r0), channel_id=1, source_target_pairs={{2,0},{9,1},{4,2},{11,3},{6,4},{13,5},{0,6},{15,7},{10,8},{17,9},{... | collective-permute-start | bytes 147464 | tf_op jit(solution)/shard_map/ppermute | solution.py:47
  8.2 5.6 %collective-permute-start.2 = (f32[24,512]{1,0:T(8,128)S(1)}, f32[24,512]{1,0:T(8,128)S(1)}, u32[]{:S(2)}, u32[]{:S(2)}) collective-permute-start(f32[24,512]{1,0:T(8,128)S(1)} %sum_core.1.r0), channel_id=1, source_target_pairs={{4,0},{17,1},{6,2},{19,3},{0,4},{21,5},{2,6},{23,7},{12,8},{25,9},... | collective-permute-start | bytes 147464 | tf_op jit(solution)/shard_map/ppermute | solution.py:47
  8.8 5.5 %collective-permute-start.3 = (f32[24,512]{1,0:T(8,128)S(1)}, f32[24,512]{1,0:T(8,128)S(1)}, u32[]{:S(2)}, u32[]{:S(2)}) collective-permute-start(f32[24,512]{1,0:T(8,128)S(1)} %sum_core.1.r0), channel_id=1, source_target_pairs={{6,0},{25,1},{0,2},{27,3},{2,4},{29,5},{4,6},{31,7},{14,8},{1,9},{... | collective-permute-start | bytes 147464 | tf_op jit(solution)/shard_map/ppermute | solution.py:47
  14.3 5.9 %collective-permute-start.4 = (f32[24,512]{1,0:T(8,128)S(1)}, f32[24,512]{1,0:T(8,128)S(1)}, u32[]{:S(2)}, u32[]{:S(2)}) collective-permute-start(f32[24,512]{1,0:T(8,128)S(1)} %sum_first.1.r0), channel_id=1, source_target_pairs={{8,0},{3,1},{10,2},{5,3},{12,4},{7,5},{14,6},{1,7},{16,8},{11,9},{... | collective-permute-start | bytes 147464 | tf_op jit(solution)/shard_map/ppermute | solution.py:47
  18.4 5.7 %collective-permute-start.5 = (f32[24,512]{1,0:T(8,128)S(1)}, f32[24,512]{1,0:T(8,128)S(1)}, u32[]{:S(2)}, u32[]{:S(2)}) collective-permute-start(f32[24,512]{1,0:T(8,128)S(1)} %sum_first.1.r0), channel_id=1, source_target_pairs={{16,0},{5,1},{18,2},{7,3},{20,4},{1,5},{22,6},{3,7},{24,8},{13,9},... | collective-permute-start | bytes 147464 | tf_op jit(solution)/shard_map/ppermute | solution.py:47
  18.4 5.8 %collective-permute-start.6 = (f32[24,512]{1,0:T(8,128)S(1)}, f32[24,512]{1,0:T(8,128)S(1)}, u32[]{:S(2)}, u32[]{:S(2)}) collective-permute-start(f32[24,512]{1,0:T(8,128)S(1)} %sum_first.1.r0), channel_id=1, source_target_pairs={{24,0},{7,1},{26,2},{1,3},{28,4},{3,5},{30,6},{5,7},{0,8},{15,9},{... | collective-permute-start | bytes 147464 | tf_op jit(solution)/shard_map/ppermute | solution.py:47
  24.3 1.4 %collective-permute-start.7 = (f32[48,512]{1,0:T(8,128)S(1)}, f32[48,512]{1,0:T(8,128)S(1)}, u32[]{:S(2)}, u32[]{:S(2)}) collective-permute-start(f32[48,512]{1,0:T(8,128)S(1)} %sum_second.1.own.refs_1_), channel_id=1, source_target_pairs={{1,0},{0,1},{3,2},{2,3},{5,4},{4,5},{7,6},{6,7},{9,8},{8,9},{11,10... | collective-permute-start | bytes 294920 | tf_op jit(solution)/shard_map/ppermute | solution.py:51
  29.1 5.1 %collective-permute-start.8 = (bf16[272,256]{1,0:T(8,128)(2,1)S(1)}, bf16[272,256]{1,0:T(8,128)(2,1)S(1)}, u32[]{:S(2)}, u32[]{:S(2)}) collective-permute-start(bf16[272,256]{1,0:T(8,128)(2,1)S(1)} %factor.1.refs_3_.refs_0_), channel_id=1, source_target_pairs={{2,0},{9,1},{4,2},{11,3},{6,4},{13,5},{0,6},{15,7},{10,8},{17,9},{... | collective-permute-start | bytes 417800 | tf_op jit(solution)/shard_map/ppermute | solution.py:47
  29.8 6.6 %collective-permute-start.9 = (bf16[272,256]{1,0:T(8,128)(2,1)S(1)}, bf16[272,256]{1,0:T(8,128)(2,1)S(1)}, u32[]{:S(2)}, u32[]{:S(2)}) collective-permute-start(bf16[272,256]{1,0:T(8,128)(2,1)S(1)} %factor.1.refs_3_.refs_0_), channel_id=1, source_target_pairs={{4,0},{17,1},{6,2},{19,3},{0,4},{21,5},{2,6},{23,7},{12,8},{25,9},... | collective-permute-start | bytes 417800 | tf_op jit(solution)/shard_map/ppermute | solution.py:47
  30.8 7.0 %collective-permute-start.10 = (bf16[272,256]{1,0:T(8,128)(2,1)S(1)}, bf16[272,256]{1,0:T(8,128)(2,1)S(1)}, u32[]{:S(2)}, u32[]{:S(2)}) collective-permute-start(bf16[272,256]{1,0:T(8,128)(2,1)S(1)} %factor.1.refs_3_.refs_0_), channel_id=1, source_target_pairs={{6,0},{25,1},{0,2},{27,3},{2,4},{29,5},{4,6},{31,7},{14,8},{1,9},{... | collective-permute-start | bytes 417800 | tf_op jit(solution)/shard_map/ppermute | solution.py:47
  37.9 9.6 %collective-permute-start.13 = (bf16[1088,256]{1,0:T(8,128)(2,1)S(1)}, bf16[1088,256]{1,0:T(8,128)(2,1)S(1)}, u32[]{:S(2)}, u32[]{:S(2)}) collective-permute-start(bf16[1088,256]{1,0:T(8,128)(2,1)S(1)} %join_line.1.refs_0_), channel_id=1, source_target_pairs={{8,0},{3,1},{10,2},{5,3},{12,4},{7,5},{14,6},{1,7},{16,8},{11,9},{... | collective-permute-start | bytes 1671176 | tf_op jit(solution)/shard_map/ppermute | solution.py:47
  38.8 11.1 %collective-permute-start.15 = (bf16[1088,256]{1,0:T(8,128)(2,1)S(1)}, bf16[1088,256]{1,0:T(8,128)(2,1)S(1)}, u32[]{:S(2)}, u32[]{:S(2)}) collective-permute-start(bf16[1088,256]{1,0:T(8,128)(2,1)S(1)} %join_line.1.refs_0_), channel_id=1, source_target_pairs={{16,0},{5,1},{18,2},{7,3},{20,4},{1,5},{22,6},{3,7},{24,8},{13,9},... | collective-permute-start | bytes 1671176 | tf_op jit(solution)/shard_map/ppermute | solution.py:47
  39.9 14.7 %collective-permute-start.11 = (bf16[1104,256]{1,0:T(8,128)(2,1)S(1)}, bf16[1104,256]{1,0:T(8,128)(2,1)S(1)}, u32[]{:S(2)}, u32[]{:S(2)}) collective-permute-start(bf16[1104,256]{1,0:T(8,128)(2,1)S(1)} %join_far.1), channel_id=1, source_target_pairs={{64,0},{96,32},{0,64},{32,96},{65,1},{97,33},{1,65},{33,97},{66,2}... | collective-permute-start | bytes 1695752 | tf_op jit(solution)/shard_map/ppermute | solution.py:55
  41.3 14.4 %collective-permute-start.17 = (bf16[1088,256]{1,0:T(8,128)(2,1)S(1)}, bf16[1088,256]{1,0:T(8,128)(2,1)S(1)}, u32[]{:S(2)}, u32[]{:S(2)}) collective-permute-start(bf16[1088,256]{1,0:T(8,128)(2,1)S(1)} %join_line.1.refs_0_), channel_id=1, source_target_pairs={{24,0},{7,1},{26,2},{1,3},{28,4},{3,5},{30,6},{5,7},{0,8},{15,9},{... | collective-permute-start | bytes 1671176 | tf_op jit(solution)/shard_map/ppermute | solution.py:47
  42.7 13.1 %collective-permute-start.12 = (bf16[1088,256]{1,0:T(8,128)(2,1)S(1)}, bf16[1088,256]{1,0:T(8,128)(2,1)S(1)}, u32[]{:S(2)}, u32[]{:S(2)}) collective-permute-start(bf16[1088,256]{1,0:T(8,128)(2,1)S(1)} %join_line.1.refs_0_), channel_id=1, source_target_pairs={{1,0},{0,1},{3,2},{2,3},{5,4},{4,5},{7,6},{6,7},{9,8},{8,9},{11,10... | collective-permute-start | bytes 1671176 | tf_op jit(solution)/shard_map/ppermute | solution.py:51
  47.5 9.3 %collective-permute-start.14 = (bf16[1088,256]{1,0:T(8,128)(2,1)S(1)}, bf16[1088,256]{1,0:T(8,128)(2,1)S(1)}, u32[]{:S(2)}, u32[]{:S(2)}) collective-permute-start(bf16[1088,256]{1,0:T(8,128)(2,1)S(1)} %collective-permute-done.13.refs_1_), channel_id=1, source_target_pairs={{1,0},{0,1},{3,2},{2,3},{5,4},{4,5},{7,6},{6,7},{9,8},{8,9},{11,10... | collective-permute-start | bytes 1671176 | tf_op jit(solution)/shard_map/ppermute | solution.py:51
  49.9 7.5 %collective-permute-start.16 = (bf16[1088,256]{1,0:T(8,128)(2,1)S(1)}, bf16[1088,256]{1,0:T(8,128)(2,1)S(1)}, u32[]{:S(2)}, u32[]{:S(2)}) collective-permute-start(bf16[1088,256]{1,0:T(8,128)(2,1)S(1)} %collective-permute-done.15.refs_1_), channel_id=1, source_target_pairs={{1,0},{0,1},{3,2},{2,3},{5,4},{4,5},{7,6},{6,7},{9,8},{8,9},{11,10... | collective-permute-start | bytes 1671176 | tf_op jit(solution)/shard_map/ppermute | solution.py:51
  54.6 7.7 %collective-permute-start.19 = (bf16[1104,256]{1,0:T(8,128)(2,1)S(1)}, bf16[1104,256]{1,0:T(8,128)(2,1)S(1)}, u32[]{:S(2)}, u32[]{:S(2)}) collective-permute-start(bf16[1104,256]{1,0:T(8,128)(2,1)S(1)} %collective-permute-done.11.message.refs_0_), channel_id=1, source_target_pairs={{1,0},{0,1},{3,2},{2,3},{5,4},{4,5},{7,6},{6,7},{9,8},{8,9},{11,10... | collective-permute-start | bytes 1695752 | tf_op jit(solution)/shard_map/ppermute | solution.py:51
  55.8 3.2 %collective-permute-start.18 = (bf16[1088,256]{1,0:T(8,128)(2,1)S(1)}, bf16[1088,256]{1,0:T(8,128)(2,1)S(1)}, u32[]{:S(2)}, u32[]{:S(2)}) collective-permute-start(bf16[1088,256]{1,0:T(8,128)(2,1)S(1)} %collective-permute-done.17.refs_1_), channel_id=1, source_target_pairs={{1,0},{0,1},{3,2},{2,3},{5,4},{4,5},{7,6},{6,7},{9,8},{8,9},{11,10... | collective-permute-start | bytes 1671176 | tf_op jit(solution)/shard_map/ppermute | solution.py:51
  55.8 9.6 %collective-permute-start.20 = (bf16[1104,256]{1,0:T(8,128)(2,1)S(1)}, bf16[1104,256]{1,0:T(8,128)(2,1)S(1)}, u32[]{:S(2)}, u32[]{:S(2)}) collective-permute-start(bf16[1104,256]{1,0:T(8,128)(2,1)S(1)} %collective-permute-done.11.message.refs_0_), channel_id=1, source_target_pairs={{8,0},{3,1},{10,2},{5,3},{12,4},{7,5},{14,6},{1,7},{16,8},{11,9},{... | collective-permute-start | bytes 1695752 | tf_op jit(solution)/shard_map/ppermute | solution.py:47
  56.7 13.9 %collective-permute-start.22 = (bf16[1104,256]{1,0:T(8,128)(2,1)S(1)}, bf16[1104,256]{1,0:T(8,128)(2,1)S(1)}, u32[]{:S(2)}, u32[]{:S(2)}) collective-permute-start(bf16[1104,256]{1,0:T(8,128)(2,1)S(1)} %collective-permute-done.11.message.refs_0_), channel_id=1, source_target_pairs={{16,0},{5,1},{18,2},{7,3},{20,4},{1,5},{22,6},{3,7},{24,8},{13,9},... | collective-permute-start | bytes 1695752 | tf_op jit(solution)/shard_map/ppermute | solution.py:47
  57.4 16.5 %collective-permute-start.24 = (bf16[1104,256]{1,0:T(8,128)(2,1)S(1)}, bf16[1104,256]{1,0:T(8,128)(2,1)S(1)}, u32[]{:S(2)}, u32[]{:S(2)}) collective-permute-start(bf16[1104,256]{1,0:T(8,128)(2,1)S(1)} %collective-permute-done.11.message.refs_0_), channel_id=1, source_target_pairs={{24,0},{7,1},{26,2},{1,3},{28,4},{3,5},{30,6},{5,7},{0,8},{15,9},{... | collective-permute-start | bytes 1695752 | tf_op jit(solution)/shard_map/ppermute | solution.py:47
  59.0 15.2 %copy-start = (f32[1,8,256,256]{3,2,1,0:T(8,128)S(1)}, f32[1,8,256,256]{3,2,1,0:T(8,128)}, u32[]{:S(2)}) copy-start(f32[1,8,256,256]{3,2,1,0:T(8,128)} %param.9) | copy-start | bytes 6291460
  62.1 25.6 %collective-permute-start.26 = (bf16[8,256,256]{2,1,0:T(8,128)(2,1)S(1)}, bf16[8,256,256]{2,1,0:T(8,128)(2,1)S(1)}, u32[]{:S(2)}, u32[]{:S(2)}) collective-permute-start(bf16[8,256,256]{2,1,0:T(8,128)(2,1)S(1)} %get-tuple-element.19.refs_0_), channel_id=1, source_target_pairs={{96,0},{0,32},{32,64},{64,96},{97,1},{1,33},{33,65},{65,97},{98,2}... | collective-permute-start | bytes 3145736 | tf_op jit(solution)/shard_map/ppermute | solution.py:55
  62.2 26.9 %collective-permute-start.27 = (bf16[8,256,256]{2,1,0:T(8,128)(2,1)S(1)}, bf16[8,256,256]{2,1,0:T(8,128)(2,1)S(1)}, u32[]{:S(2)}, u32[]{:S(2)}) collective-permute-start(bf16[8,256,256]{2,1,0:T(8,128)(2,1)S(1)} %get-tuple-element.20), channel_id=1, source_target_pairs={{32,0},{64,32},{96,64},{0,96},{33,1},{65,33},{97,65},{1,97},{34,2}... | collective-permute-start | bytes 3145736 | tf_op jit(solution)/shard_map/ppermute | solution.py:55
  65.4 11.2 %collective-permute-start.21 = (bf16[1104,256]{1,0:T(8,128)(2,1)S(1)}, bf16[1104,256]{1,0:T(8,128)(2,1)S(1)}, u32[]{:S(2)}, u32[]{:S(2)}) collective-permute-start(bf16[1104,256]{1,0:T(8,128)(2,1)S(1)} %collective-permute-done.20.refs_1_), channel_id=1, source_target_pairs={{1,0},{0,1},{3,2},{2,3},{5,4},{4,5},{7,6},{6,7},{9,8},{8,9},{11,10... | collective-permute-start | bytes 1695752 | tf_op jit(solution)/shard_map/ppermute | solution.py:51
  70.7 6.2 %collective-permute-start.23 = (bf16[1104,256]{1,0:T(8,128)(2,1)S(1)}, bf16[1104,256]{1,0:T(8,128)(2,1)S(1)}, u32[]{:S(2)}, u32[]{:S(2)}) collective-permute-start(bf16[1104,256]{1,0:T(8,128)(2,1)S(1)} %collective-permute-done.22.refs_1_), channel_id=1, source_target_pairs={{1,0},{0,1},{3,2},{2,3},{5,4},{4,5},{7,6},{6,7},{9,8},{8,9},{11,10... | collective-permute-start | bytes 1695752 | tf_op jit(solution)/shard_map/ppermute | solution.py:51
  73.9 3.2 %collective-permute-start.25 = (bf16[1104,256]{1,0:T(8,128)(2,1)S(1)}, bf16[1104,256]{1,0:T(8,128)(2,1)S(1)}, u32[]{:S(2)}, u32[]{:S(2)}) collective-permute-start(bf16[1104,256]{1,0:T(8,128)(2,1)S(1)} %collective-permute-done.24.refs_1_), channel_id=1, source_target_pairs={{1,0},{0,1},{3,2},{2,3},{5,4},{4,5},{7,6},{6,7},{9,8},{8,9},{11,10... | collective-permute-start | bytes 1695752 | tf_op jit(solution)/shard_map/ppermute | solution.py:51

commit v6 on v5

--- a/solution.py
+++ b/solution.py
@@ -47,12 +47,22 @@
     return lax.ppermute(x, "cand", pairs)
 
 
+def from_three(x, leg):
+    opposite = from_cand(x, leg, 2)
+    return [from_cand(x, leg, 1), opposite, from_cand(x, leg, 3)]
+
+
 def from_core(x):
     return lax.ppermute(x, "cand", [(me ^ 1, me) for me in range(N_CAND)])
 
 
-def from_set(x, d):
-    return lax.ppermute(x, "set", [((me + d) % N_SET, me) for me in range(N_SET)])
+def from_set(x, d, d_core_1=None):
+    pairs = []
+    for me_set in range(N_SET):
+        for me in range(N_CAND):
+            ahead = d if d_core_1 is None or me % 2 == 0 else d_core_1
+            pairs.append(((me_set + ahead) % N_SET * N_CAND + me, me_set * N_CAND + me))
+    return lax.ppermute(x, ("set", "cand"), pairs)
 
 
 def sketch_kernel(place, rows_hbm, sketch, keep, give, rows, total, sems):
@@ -265,7 +275,8 @@
     ).astype(bf16)
     line = lax.broadcasted_iota(i32, (16, 128), 0)
     lane = lax.broadcasted_iota(i32, (16, 128), 1)
-    wanted = ((me_set + line) % N_SET) * N_CAND + me
+    ahead = line + jnp.where(line % 2 == 1, 2 * me_core, 0)
+    wanted = ((me_set + ahead) % N_SET) * N_CAND + me
     hot = jnp.where((lane == wanted) & (line < N_SET), 1.0, 0.0).astype(bf16)
     across = lax.dot_general(hot, fields, NT, preferred_element_type=f32)
     down = lax.dot_general(fields, hot, NT, preferred_element_type=f32)
@@ -395,11 +406,11 @@
 ]
 
 
-def send_call(next_list, last_list, factors, *after):
-    def kernel(next_list, last_list, factors, *refs):
-        to_next, to_last, scales, lefts, rights, totals = refs[len(after) :]
+def send_call(one_list, two_list, factors, *after):
+    def kernel(one_list, two_list, factors, *refs):
+        to_one, to_two, scales, lefts, rights, totals = refs[len(after) :]
         spread(factors, scales)
-        for pairs, out in ((next_list, to_next), (last_list, to_last)):
+        for pairs, out in ((one_list, to_one), (two_list, to_two)):
             expand(pairs, factors, scales, lefts, rights, totals)
             for t in range(NT_DEV):
                 out[t] = total_of(pairs, t, totals).astype(bf16)
@@ -413,7 +424,7 @@
         scratch_shapes=WORK,
         compiler_params=params(),
         name="send_pairs",
-    )(next_list, last_list, factors, *after)
+    )(one_list, two_list, factors, *after)
 
 
 def keep_call(pairs, base, factors, *after):
@@ -467,32 +478,33 @@
     ).astype(f32)
     part = small_call(sum_core_kernel, HALF + 8, "sum_core", keep, got, slots)
     part = small_call(
-        sum_first_kernel, HALF + 8, "sum_first", part, *[from_cand(part, 0, k) for k in (1, 2, 3)]
+        sum_first_kernel, HALF + 8, "sum_first", part, *from_three(part, 0)
     )
     own = small_call(
-        sum_second_kernel, HALF + 32, "sum_second", part, *[from_cand(part, 1, k) for k in (1, 2, 3)]
+        sum_second_kernel, HALF + 32, "sum_second", part, *from_three(part, 1)
     )
     other = from_core(own)
 
     mine = factor_call(place, own, other, rows)
-    own_list, next_list, far_list, last_list = plan_call(place, own, other, mine)
-    line = join_call([mine] + [from_cand(mine, 0, k) for k in (1, 2, 3)], "join_line", next_list)
+    own_list, one_list, far_list, two_list = plan_call(place, own, other, mine)
+    line = join_call([mine] + from_three(mine, 0), "join_line", one_list)
     far_line = from_set(join_call([line, far_list], "join_far"), 2)
-    here = [line] + [from_cand(line, 1, k) for k in (1, 2, 3)]
-    there = [from_core(x) for x in here]
-    factors = put_all(
-        [p for k in range(4) for p in ((k, here[k]), (4 + k, there[k]))]
-    )
-
-    to_next, to_last = send_call(next_list, last_list, factors)
-    arrived = [touch_call(x, LAST_US) for x in (from_set(to_next, 3), from_set(to_last, 1))]
-
-    far_here = [far_line] + [from_cand(far_line, 1, k) for k in (1, 2, 3)]
+    here = [line] + from_three(line, 1)
+    factors = put_all([(k, here[k]) for k in range(3)])
+    here[3] = touch_call(here[3], 0, factors)
+    factors = put_call(factors, here[3], 3)
+    for k in range(4):
+        factors = put_call(factors, from_core(here[k]), 4 + k)
+
+    to_one, to_two = send_call(one_list, two_list, factors)
+    arrived = [touch_call(x, LAST_US) for x in (from_set(to_one, 3, 1), from_set(to_two, 1, 3))]
+
+    far_here = [far_line] + from_three(far_line, 1)
     far_there = [from_core(x) for x in far_here]
     far_factors = put_all(
         [p for k in range(4) for p in ((k, far_here[k]), (4 + k, far_there[k]))]
     )
-    base = keep_call(own_list, accumulator[0], factors, to_next)
+    base = keep_call(own_list, accumulator[0], factors, to_one)
     base = keep_call(unpack_call(far_line), base, far_factors)
     base = final_call(base, *arrived)
     return base[None]

time: 91.8 us -> 91.4 us (level)
    ppermute x3, waiting for transfers between devices: 14.4 us -> 13.1 us  [from_set(): return lax.ppermute(x, ('set', 'cand'), pairs)]
  transfers between devices with their start and end apart: 28 -> 28, of which waited for: 19 -> 19; matrix products, arithmetic and copies ran while one was open for 1% -> 1% of each run, Pallas kernels for 11% -> 10%
where the time goes in v6:
time: 91.4 us; the launch traced here: 89.6 us
  waiting for transfers between devices  41.9 us (46%)
  starting transfers between devices  28.6 us (31%)
  Pallas kernels  17.3 us (19%)
    ppermute x15, waiting for transfers between devices, from_cand(): return lax.ppermute(x, 'cand', pairs)  27.1 us
    ppermute x15, starting transfers between devices, from_cand(): return lax.ppermute(x, 'cand', pairs)  19 us
    ppermute x3, waiting for transfers between devices, from_set(): return lax.ppermute(x, ('set', 'cand'), pairs)  13.1 us
    ppermute x10, starting transfers between devices, from_core(): return lax.ppermute(x, 'cand', [(me ^ 1, me) for me in range(N_CAND)])  6.03 us
    pallas_call x2, Pallas kernels, keep_call(): pl.pallas_call(kernel, out_shape=jax.ShapeDtypeStruct((NT_DEV, BLOCK, BLO...  4.37 us
    ppermute x3, starting transfers between devices, from_set(): return lax.ppermute(x, ('set', 'cand'), pairs)  3.58 us
    pallas_call x1, Pallas kernels, factor_call(): pl.pallas_call(factor_kernel, out_shape=jax.ShapeDtypeStruct((MSG, BLOCK)...  3.45 us
    pallas_call x1, Pallas kernels, sketch_call(): pl.pallas_call(sketch_kernel, out_shape=(half, half), in_specs=[SMEM, HBM...  3.05 us
  transfers between devices with their start and end apart: 28, of which 19 were waited for; matrix products, arithmetic and copies ran while one was open for 1% of the time, Pallas kernels for 10%

profile of v6, /device:TPU:6, one launch (start us, length us, event | category | flops | bytes accessed | tf_op | source)
XLA Modules:
  0.0 89.6 jit_solution(14306263578800535607)
XLA Ops:
  0.8 3.1 %sketch.1 = (f32[16,512]{1,0:T(8,128)S(1)}, f32[16,512]{1,0:T(8,128)S(1)}) custom-call(s32[2]{0:T(128)S(1)} %pad_add_fusion.place.refs_0_, bf16[2048,512]{1,0:T(8,128)(2,1)} %bitcast.22, bf16[32,512]{1,0:T(8,128)(2,1)S(1)} %bitcast.21), custom_call_target="tpu_custom_call" | custom-call | tf_op jit(solution)/shard_map/sketch/pallas_call | solution.py:88
  5.2 3.0 %collective-permute-start.1 = (f32[24,512]{1,0:T(8,128)S(1)}, f32[24,512]{1,0:T(8,128)S(1)}, u32[]{:S(2)}, u32[]{:S(2)}) collective-permute-start(f32[24,512]{1,0:T(8,128)S(1)} %sum_core.1.r0), channel_id=1, source_target_pairs={{2,0},{9,1},{4,2},{11,3},{6,4},{13,5},{0,6},{15,7},{10,8},{17,9},{... | collective-permute-start | bytes 147464 | tf_op jit(solution)/shard_map/ppermute | solution.py:47
  8.8 1.0 %collective-permute-start.3 = (f32[24,512]{1,0:T(8,128)S(1)}, f32[24,512]{1,0:T(8,128)S(1)}, u32[]{:S(2)}, u32[]{:S(2)}) collective-permute-start(f32[24,512]{1,0:T(8,128)S(1)} %sum_core.1.r0), channel_id=1, source_target_pairs={{6,0},{25,1},{0,2},{27,3},{2,4},{29,5},{4,6},{31,7},{14,8},{1,9},{... | collective-permute-start | bytes 147464 | tf_op jit(solution)/shard_map/ppermute | solution.py:47
  10.0 3.9 %collective-permute-done.2.r2 = f32[24,512]{1,0:T(8,128)S(1)} collective-permute-done((f32[24,512]{1,0:T(8,128)S(1)}, f32[24,512]{1,0:T(8,128)S(1)}, u32[]{:S(2)}, u32[]{:S(2)}) %collective-permute-start.2) | collective-permute-done | bytes 49184 | tf_op jit(solution)/shard_map/ppermute | solution.py:47
  14.3 4.1 %collective-permute-start.4 = (f32[24,512]{1,0:T(8,128)S(1)}, f32[24,512]{1,0:T(8,128)S(1)}, u32[]{:S(2)}, u32[]{:S(2)}) collective-permute-start(f32[24,512]{1,0:T(8,128)S(1)} %sum_first.1.r0), channel_id=1, source_target_pairs={{8,0},{3,1},{10,2},{5,3},{12,4},{7,5},{14,6},{1,7},{16,8},{11,9},{... | collective-permute-start | bytes 147464 | tf_op jit(solution)/shard_map/ppermute | solution.py:47
  18.4 1.3 %collective-permute-start.6 = (f32[24,512]{1,0:T(8,128)S(1)}, f32[24,512]{1,0:T(8,128)S(1)}, u32[]{:S(2)}, u32[]{:S(2)}) collective-permute-start(f32[24,512]{1,0:T(8,128)S(1)} %sum_first.1.r0), channel_id=1, source_target_pairs={{24,0},{7,1},{26,2},{1,3},{28,4},{3,5},{30,6},{5,7},{0,8},{15,9},{... | collective-permute-start | bytes 147464 | tf_op jit(solution)/shard_map/ppermute | solution.py:47
  20.2 3.9 %collective-permute-done.5.r2 = f32[24,512]{1,0:T(8,128)S(1)} collective-permute-done((f32[24,512]{1,0:T(8,128)S(1)}, f32[24,512]{1,0:T(8,128)S(1)}, u32[]{:S(2)}, u32[]{:S(2)}) %collective-permute-start.5) | collective-permute-done | bytes 49184 | tf_op jit(solution)/shard_map/ppermute | solution.py:47
  24.4 1.3 %collective-permute-done.7.other.refs_2_ = f32[48,512]{1,0:T(8,128)S(1)} collective-permute-done((f32[48,512]{1,0:T(8,128)S(1)}, f32[48,512]{1,0:T(8,128)S(1)}, u32[]{:S(2)}, u32[]{:S(2)}) %collective-permute-start.7) | collective-permute-done | bytes 98336 | tf_op jit(solution)/shard_map/ppermute | solution.py:56
  25.7 3.5 %factor.1.refs_3_.refs_0_ = bf16[272,256]{1,0:T(8,128)(2,1)S(1)} custom-call(s32[2]{0:T(128)S(1)} %pad_add_fusion.place.refs_0_, f32[48,512]{1,0:T(8,128)S(1)} %sum_second.1.own.refs_1_, f32[48,512]{1,0:T(8,128)S(1)} %collective-permute-done.7.other.refs_2_, bf16[2048,512]{1,0:T(8,128)(2,1)} %bitcast.23), custom_call_target="tpu_custom_call" | custom-call | tf_op jit(solution)/shard_map/factor/pallas_call | solution.py:181
  29.8 1.1 %collective-permute-start.9 = (bf16[272,256]{1,0:T(8,128)(2,1)S(1)}, bf16[272,256]{1,0:T(8,128)(2,1)S(1)}, u32[]{:S(2)}, u32[]{:S(2)}) collective-permute-start(bf16[272,256]{1,0:T(8,128)(2,1)S(1)} %factor.1.refs_3_.refs_0_), channel_id=1, source_target_pairs={{4,0},{17,1},{6,2},{19,3},{0,4},{21,5},{2,6},{23,7},{12,8},{25,9},... | collective-permute-start | bytes 417800 | tf_op jit(solution)/shard_map/ppermute | solution.py:47
  30.8 1.3 %collective-permute-start.10 = (bf16[272,256]{1,0:T(8,128)(2,1)S(1)}, bf16[272,256]{1,0:T(8,128)(2,1)S(1)}, u32[]{:S(2)}, u32[]{:S(2)}) collective-permute-start(bf16[272,256]{1,0:T(8,128)(2,1)S(1)} %factor.1.refs_3_.refs_0_), channel_id=1, source_target_pairs={{6,0},{25,1},{0,2},{27,3},{2,4},{29,5},{4,6},{31,7},{14,8},{1,9},{... | collective-permute-start | bytes 417800 | tf_op jit(solution)/shard_map/ppermute | solution.py:47
  32.1 1.2 %plan.1 = (s32[8,128]{1,0:T(8,128)S(1)}, s32[8,128]{1,0:T(8,128)S(1)}, bf16[16,256]{1,0:T(8,128)(2,1)S(1)}, s32[8,128]{1,0:T(8,128)S(1)}) custom-call(s32[2]{0:T(128)S(1)} %pad_add_fusion.place.refs_0_, f32[48,512]{1,0:T(8,128)S(1)} %sum_second.1.own.refs_1_, f32[48,512]{1,0:T(8,128)S(1)} %collective-permute-done.7.other.refs_2_, ...), custom_call_target="tpu_custom_call" | custom-call | tf_op jit(solution)/shard_map/plan/pallas_call | solution.py:332
  34.3 2.1 %collective-permute-done.9.refs_2_ = bf16[272,256]{1,0:T(8,128)(2,1)S(1)} collective-permute-done((bf16[272,256]{1,0:T(8,128)(2,1)S(1)}, bf16[272,256]{1,0:T(8,128)(2,1)S(1)}, u32[]{:S(2)}, u32[]{:S(2)}) %collective-permute-start.9) | collective-permute-done | bytes 139296 | tf_op jit(solution)/shard_map/ppermute | solution.py:47
  36.4 1.4 %collective-permute-done.10.refs_3_ = bf16[272,256]{1,0:T(8,128)(2,1)S(1)} collective-permute-done((bf16[272,256]{1,0:T(8,128)(2,1)S(1)}, bf16[272,256]{1,0:T(8,128)(2,1)S(1)}, u32[]{:S(2)}, u32[]{:S(2)}) %collective-permute-start.10) | collective-permute-done | bytes 139296 | tf_op jit(solution)/shard_map/ppermute | solution.py:47
  38.8 1.0 %collective-permute-start.13 = (bf16[1088,256]{1,0:T(8,128)(2,1)S(1)}, bf16[1088,256]{1,0:T(8,128)(2,1)S(1)}, u32[]{:S(2)}, u32[]{:S(2)}) collective-permute-start(bf16[1088,256]{1,0:T(8,128)(2,1)S(1)} %join_line.1.refs_0_), channel_id=1, source_target_pairs={{16,0},{5,1},{18,2},{7,3},{20,4},{1,5},{22,6},{3,7},{24,8},{13,9},... | collective-permute-start | bytes 1671176 | tf_op jit(solution)/shard_map/ppermute | solution.py:47
  39.9 1.5 %collective-permute-start.11 = (bf16[1104,256]{1,0:T(8,128)(2,1)S(1)}, bf16[1104,256]{1,0:T(8,128)(2,1)S(1)}, u32[]{:S(2)}, u32[]{:S(2)}) collective-permute-start(bf16[1104,256]{1,0:T(8,128)(2,1)S(1)} %join_far.1), channel_id=1, source_target_pairs={{64,0},{65,1},{66,2},{67,3},{68,4},{69,5},{70,6},{71,7},{72,8},{73... | collective-permute-start | bytes 1695752 | tf_op jit(solution)/shard_map/ppermute | solution.py:65
  41.3 1.3 %collective-permute-start.14 = (bf16[1088,256]{1,0:T(8,128)(2,1)S(1)}, bf16[1088,256]{1,0:T(8,128)(2,1)S(1)}, u32[]{:S(2)}, u32[]{:S(2)}) collective-permute-start(bf16[1088,256]{1,0:T(8,128)(2,1)S(1)} %join_line.1.refs_0_), channel_id=1, source_target_pairs={{24,0},{7,1},{26,2},{1,3},{28,4},{3,5},{30,6},{5,7},{0,8},{15,9},{... | collective-permute-start | bytes 1671176 | tf_op jit(solution)/shard_map/ppermute | solution.py:47
  42.7 4.8 %collective-permute-done.12.refs_1_ = bf16[1088,256]{1,0:T(8,128)(2,1)S(1)} collective-permute-done((bf16[1088,256]{1,0:T(8,128)(2,1)S(1)}, bf16[1088,256]{1,0:T(8,128)(2,1)S(1)}, u32[]{:S(2)}, u32[]{:S(2)}) %collective-permute-start.12) | collective-permute-done | bytes 557088 | tf_op jit(solution)/shard_map/ppermute | solution.py:47
  47.5 2.5 %collective-permute-done.13.refs_1_ = bf16[1088,256]{1,0:T(8,128)(2,1)S(1)} collective-permute-done((bf16[1088,256]{1,0:T(8,128)(2,1)S(1)}, bf16[1088,256]{1,0:T(8,128)(2,1)S(1)}, u32[]{:S(2)}, u32[]{:S(2)}) %collective-permute-start.13) | collective-permute-done | bytes 557088 | tf_op jit(solution)/shard_map/ppermute | solution.py:47
  49.9 4.7 %collective-permute-done.11.message.refs_0_ = bf16[1104,256]{1,0:T(8,128)(2,1)S(1)} collective-permute-done((bf16[1104,256]{1,0:T(8,128)(2,1)S(1)}, bf16[1104,256]{1,0:T(8,128)(2,1)S(1)}, u32[]{:S(2)}, u32[]{:S(2)}) %collective-permute-start.11) | collective-permute-done | bytes 565280 | tf_op jit(solution)/shard_map/ppermute | solution.py:65
  55.8 1.3 %collective-permute-start.20 = (bf16[1104,256]{1,0:T(8,128)(2,1)S(1)}, bf16[1104,256]{1,0:T(8,128)(2,1)S(1)}, u32[]{:S(2)}, u32[]{:S(2)}) collective-permute-start(bf16[1104,256]{1,0:T(8,128)(2,1)S(1)} %collective-permute-done.11.message.refs_0_), channel_id=1, source_target_pairs={{8,0},{3,1},{10,2},{5,3},{12,4},{7,5},{14,6},{1,7},{16,8},{11,9},{... | collective-permute-start | bytes 1695752 | tf_op jit(solution)/shard_map/ppermute | solution.py:47
  59.0 2.2 %send_pairs.1 = (bf16[8,256,256]{2,1,0:T(8,128)(2,1)S(1)}, bf16[8,256,256]{2,1,0:T(8,128)(2,1)S(1)}) custom-call(s32[8,128]{1,0:T(8,128)S(1)} %get-tuple-element.15.refs_4_.one_list, s32[8,128]{1,0:T(8,128)S(1)} %get-tuple-element.18.two_list, bf16[8704,256]{1,0:T(8,128)(2,1)S(1)} %put.23.factors), custom_call_target="tpu_custom_call" | custom-call | tf_op jit(solution)/shard_map/send_pairs/pallas_call | solution.py:419
  61.2 1.0 %collective-permute-start.26 = (bf16[8,256,256]{2,1,0:T(8,128)(2,1)S(1)}, bf16[8,256,256]{2,1,0:T(8,128)(2,1)S(1)}, u32[]{:S(2)}, u32[]{:S(2)}) collective-permute-start(bf16[8,256,256]{2,1,0:T(8,128)(2,1)S(1)} %get-tuple-element.19.refs_0_), channel_id=1, source_target_pairs={{96,0},{33,1},{98,2},{35,3},{100,4},{37,5},{102,6},{39,7},{104,8},... | collective-permute-start | bytes 3145736 | tf_op jit(solution)/shard_map/ppermute | solution.py:65
  62.2 1.1 %collective-permute-start.27 = (bf16[8,256,256]{2,1,0:T(8,128)(2,1)S(1)}, bf16[8,256,256]{2,1,0:T(8,128)(2,1)S(1)}, u32[]{:S(2)}, u32[]{:S(2)}) collective-permute-start(bf16[8,256,256]{2,1,0:T(8,128)(2,1)S(1)} %get-tuple-element.20), channel_id=1, source_target_pairs={{32,0},{97,1},{34,2},{99,3},{36,4},{101,5},{38,6},{103,7},{40,8},{... | collective-permute-start | bytes 3145736 | tf_op jit(solution)/shard_map/ppermute | solution.py:65
  63.3 2.1 %collective-permute-done.20.refs_1_ = bf16[1104,256]{1,0:T(8,128)(2,1)S(1)} collective-permute-done((bf16[1104,256]{1,0:T(8,128)(2,1)S(1)}, bf16[1104,256]{1,0:T(8,128)(2,1)S(1)}, u32[]{:S(2)}, u32[]{:S(2)}) %collective-permute-start.20) | collective-permute-done | bytes 565280 | tf_op jit(solution)/shard_map/ppermute | solution.py:47
  65.5 5.6 %collective-permute-start.21 = (bf16[1104,256]{1,0:T(8,128)(2,1)S(1)}, bf16[1104,256]{1,0:T(8,128)(2,1)S(1)}, u32[]{:S(2)}, u32[]{:S(2)}) collective-permute-start(bf16[1104,256]{1,0:T(8,128)(2,1)S(1)} %collective-permute-done.20.refs_1_), channel_id=1, source_target_pairs={{1,0},{0,1},{3,2},{2,3},{5,4},{4,5},{7,6},{6,7},{9,8},{8,9},{11,10... | collective-permute-start | bytes 1695752 | tf_op jit(solution)/shard_map/ppermute | solution.py:56
  71.1 3.2 %collective-permute-done.24.refs_1_ = bf16[1104,256]{1,0:T(8,128)(2,1)S(1)} collective-permute-done((bf16[1104,256]{1,0:T(8,128)(2,1)S(1)}, bf16[1104,256]{1,0:T(8,128)(2,1)S(1)}, u32[]{:S(2)}, u32[]{:S(2)}) %collective-permute-start.24) | collective-permute-done | bytes 565280 | tf_op jit(solution)/shard_map/ppermute | solution.py:47
  74.7 2.2 %keep_pairs.2.base = f32[8,256,256]{2,1,0:T(8,128)S(1)} custom-call(s32[8,128]{1,0:T(8,128)S(1)} %get-tuple-element.17.pairs, f32[8,256,256]{2,1,0:T(8,128)S(1)} %bitcast.20, bf16[8704,256]{1,0:T(8,128)(2,1)S(1)} %put.23.factors, bf16[8,256,256]{2,1,0:T(8,128)(2,1)S(1)} %get-tuple-element.19.refs_0_), custom_call_target="tpu_custom_call" | custom-call | tf_op jit(solution)/shard_map/keep_pairs/pallas_call | solution.py:438
  77.6 2.2 %keep_pairs.3.base = f32[8,256,256]{2,1,0:T(8,128)S(1)} custom-call(s32[8,128]{1,0:T(8,128)S(1)} %unpack.1.pairs, f32[8,256,256]{2,1,0:T(8,128)S(1)} %keep_pairs.2.base, bf16[8704,256]{1,0:T(8,128)(2,1)S(1)} %put.31.factors), custom_call_target="tpu_custom_call" | custom-call | tf_op jit(solution)/shard_map/keep_pairs/pallas_call | solution.py:438
  79.8 7.0 %collective-permute-done.26.refs_0_ = bf16[8,256,256]{2,1,0:T(8,128)(2,1)S(1)} collective-permute-done((bf16[8,256,256]{2,1,0:T(8,128)(2,1)S(1)}, bf16[8,256,256]{2,1,0:T(8,128)(2,1)S(1)}, u32[]{:S(2)}, u32[]{:S(2)}) %collective-permute-start.26) | collective-permute-done | bytes 1048608 | tf_op jit(solution)/shard_map/ppermute | solution.py:65
  86.8 1.4 %collective-permute-done.27.refs_0_ = bf16[8,256,256]{2,1,0:T(8,128)(2,1)S(1)} collective-permute-done((bf16[8,256,256]{2,1,0:T(8,128)(2,1)S(1)}, bf16[8,256,256]{2,1,0:T(8,128)(2,1)S(1)}, u32[]{:S(2)}, u32[]{:S(2)}) %collective-permute-start.27) | collective-permute-done | bytes 1048608 | tf_op jit(solution)/shard_map/ppermute | solution.py:65
  88.2 1.4 %final.1 = f32[8,256,256]{2,1,0:T(8,128)} custom-call(f32[8,256,256]{2,1,0:T(8,128)S(1)} %keep_pairs.3.base, bf16[8,256,256]{2,1,0:T(8,128)(2,1)S(1)} %touch.4.one, bf16[8,256,256]{2,1,0:T(8,128)(2,1)S(1)} %touch.5.two), custom_call_target="tpu_custom_call" | custom-call | tf_op jit(solution)/shard_map/final/pallas_call | solution.py:459
  (62 shorter events, 10.8 us)
Async XLA Ops:
  0.1 0.8 copy-start.1
  3.9 1.3 %collective-permute-start = (f32[16,512]{1,0:T(8,128)S(1)}, f32[16,512]{1,0:T(8,128)S(1)}, u32[]{:S(2)}, u32[]{:S(2)}) collective-permute-start(f32[16,512]{1,0:T(8,128)S(1)} %get-tuple-element.14), channel_id=1, source_target_pairs={{1,0},{0,1},{3,2},{2,3},{5,4},{4,5},{7,6},{6,7},{9,8},{8,9},{11,10... | collective-permute-start | bytes 98312 | tf_op jit(solution)/shard_map/ppermute | solution.py:56
  5.2 4.8 %collective-permute-start.1 = (f32[24,512]{1,0:T(8,128)S(1)}, f32[24,512]{1,0:T(8,128)S(1)}, u32[]{:S(2)}, u32[]{:S(2)}) collective-permute-start(f32[24,512]{1,0:T(8,128)S(1)} %sum_core.1.r0), channel_id=1, source_target_pairs={{2,0},{9,1},{4,2},{11,3},{6,4},{13,5},{0,6},{15,7},{10,8},{17,9},{... | collective-permute-start | bytes 147464 | tf_op jit(solution)/shard_map/ppermute | solution.py:47
  8.2 5.6 %collective-permute-start.2 = (f32[24,512]{1,0:T(8,128)S(1)}, f32[24,512]{1,0:T(8,128)S(1)}, u32[]{:S(2)}, u32[]{:S(2)}) collective-permute-start(f32[24,512]{1,0:T(8,128)S(1)} %sum_core.1.r0), channel_id=1, source_target_pairs={{4,0},{17,1},{6,2},{19,3},{0,4},{21,5},{2,6},{23,7},{12,8},{25,9},... | collective-permute-start | bytes 147464 | tf_op jit(solution)/shard_map/ppermute | solution.py:47
  8.8 5.5 %collective-permute-start.3 = (f32[24,512]{1,0:T(8,128)S(1)}, f32[24,512]{1,0:T(8,128)S(1)}, u32[]{:S(2)}, u32[]{:S(2)}) collective-permute-start(f32[24,512]{1,0:T(8,128)S(1)} %sum_core.1.r0), channel_id=1, source_target_pairs={{6,0},{25,1},{0,2},{27,3},{2,4},{29,5},{4,6},{31,7},{14,8},{1,9},{... | collective-permute-start | bytes 147464 | tf_op jit(solution)/shard_map/ppermute | solution.py:47
  14.3 5.9 %collective-permute-start.4 = (f32[24,512]{1,0:T(8,128)S(1)}, f32[24,512]{1,0:T(8,128)S(1)}, u32[]{:S(2)}, u32[]{:S(2)}) collective-permute-start(f32[24,512]{1,0:T(8,128)S(1)} %sum_first.1.r0), channel_id=1, source_target_pairs={{8,0},{3,1},{10,2},{5,3},{12,4},{7,5},{14,6},{1,7},{16,8},{11,9},{... | collective-permute-start | bytes 147464 | tf_op jit(solution)/shard_map/ppermute | solution.py:47
  18.4 5.7 %collective-permute-start.5 = (f32[24,512]{1,0:T(8,128)S(1)}, f32[24,512]{1,0:T(8,128)S(1)}, u32[]{:S(2)}, u32[]{:S(2)}) collective-permute-start(f32[24,512]{1,0:T(8,128)S(1)} %sum_first.1.r0), channel_id=1, source_target_pairs={{16,0},{5,1},{18,2},{7,3},{20,4},{1,5},{22,6},{3,7},{24,8},{13,9},... | collective-permute-start | bytes 147464 | tf_op jit(solution)/shard_map/ppermute | solution.py:47
  18.4 5.8 %collective-permute-start.6 = (f32[24,512]{1,0:T(8,128)S(1)}, f32[24,512]{1,0:T(8,128)S(1)}, u32[]{:S(2)}, u32[]{:S(2)}) collective-permute-start(f32[24,512]{1,0:T(8,128)S(1)} %sum_first.1.r0), channel_id=1, source_target_pairs={{24,0},{7,1},{26,2},{1,3},{28,4},{3,5},{30,6},{5,7},{0,8},{15,9},{... | collective-permute-start | bytes 147464 | tf_op jit(solution)/shard_map/ppermute | solution.py:47
  24.3 1.4 %collective-permute-start.7 = (f32[48,512]{1,0:T(8,128)S(1)}, f32[48,512]{1,0:T(8,128)S(1)}, u32[]{:S(2)}, u32[]{:S(2)}) collective-permute-start(f32[48,512]{1,0:T(8,128)S(1)} %sum_second.1.own.refs_1_), channel_id=1, source_target_pairs={{1,0},{0,1},{3,2},{2,3},{5,4},{4,5},{7,6},{6,7},{9,8},{8,9},{11,10... | collective-permute-start | bytes 294920 | tf_op jit(solution)/shard_map/ppermute | solution.py:56
  29.1 5.1 %collective-permute-start.8 = (bf16[272,256]{1,0:T(8,128)(2,1)S(1)}, bf16[272,256]{1,0:T(8,128)(2,1)S(1)}, u32[]{:S(2)}, u32[]{:S(2)}) collective-permute-start(bf16[272,256]{1,0:T(8,128)(2,1)S(1)} %factor.1.refs_3_.refs_0_), channel_id=1, source_target_pairs={{2,0},{9,1},{4,2},{11,3},{6,4},{13,5},{0,6},{15,7},{10,8},{17,9},{... | collective-permute-start | bytes 417800 | tf_op jit(solution)/shard_map/ppermute | solution.py:47
  29.8 6.6 %collective-permute-start.9 = (bf16[272,256]{1,0:T(8,128)(2,1)S(1)}, bf16[272,256]{1,0:T(8,128)(2,1)S(1)}, u32[]{:S(2)}, u32[]{:S(2)}) collective-permute-start(bf16[272,256]{1,0:T(8,128)(2,1)S(1)} %factor.1.refs_3_.refs_0_), channel_id=1, source_target_pairs={{4,0},{17,1},{6,2},{19,3},{0,4},{21,5},{2,6},{23,7},{12,8},{25,9},... | collective-permute-start | bytes 417800 | tf_op jit(solution)/shard_map/ppermute | solution.py:47
  30.8 7.0 %collective-permute-start.10 = (bf16[272,256]{1,0:T(8,128)(2,1)S(1)}, bf16[272,256]{1,0:T(8,128)(2,1)S(1)}, u32[]{:S(2)}, u32[]{:S(2)}) collective-permute-start(bf16[272,256]{1,0:T(8,128)(2,1)S(1)} %factor.1.refs_3_.refs_0_), channel_id=1, source_target_pairs={{6,0},{25,1},{0,2},{27,3},{2,4},{29,5},{4,6},{31,7},{14,8},{1,9},{... | collective-permute-start | bytes 417800 | tf_op jit(solution)/shard_map/ppermute | solution.py:47
  37.9 9.6 %collective-permute-start.12 = (bf16[1088,256]{1,0:T(8,128)(2,1)S(1)}, bf16[1088,256]{1,0:T(8,128)(2,1)S(1)}, u32[]{:S(2)}, u32[]{:S(2)}) collective-permute-start(bf16[1088,256]{1,0:T(8,128)(2,1)S(1)} %join_line.1.refs_0_), channel_id=1, source_target_pairs={{8,0},{3,1},{10,2},{5,3},{12,4},{7,5},{14,6},{1,7},{16,8},{11,9},{... | collective-permute-start | bytes 1671176 | tf_op jit(solution)/shard_map/ppermute | solution.py:47
  38.8 11.1 %collective-permute-start.13 = (bf16[1088,256]{1,0:T(8,128)(2,1)S(1)}, bf16[1088,256]{1,0:T(8,128)(2,1)S(1)}, u32[]{:S(2)}, u32[]{:S(2)}) collective-permute-start(bf16[1088,256]{1,0:T(8,128)(2,1)S(1)} %join_line.1.refs_0_), channel_id=1, source_target_pairs={{16,0},{5,1},{18,2},{7,3},{20,4},{1,5},{22,6},{3,7},{24,8},{13,9},... | collective-permute-start | bytes 1671176 | tf_op jit(solution)/shard_map/ppermute | solution.py:47
  39.9 14.7 %collective-permute-start.11 = (bf16[1104,256]{1,0:T(8,128)(2,1)S(1)}, bf16[1104,256]{1,0:T(8,128)(2,1)S(1)}, u32[]{:S(2)}, u32[]{:S(2)}) collective-permute-start(bf16[1104,256]{1,0:T(8,128)(2,1)S(1)} %join_far.1), channel_id=1, source_target_pairs={{64,0},{65,1},{66,2},{67,3},{68,4},{69,5},{70,6},{71,7},{72,8},{73... | collective-permute-start | bytes 1695752 | tf_op jit(solution)/shard_map/ppermute | solution.py:65
  41.3 14.4 %collective-permute-start.14 = (bf16[1088,256]{1,0:T(8,128)(2,1)S(1)}, bf16[1088,256]{1,0:T(8,128)(2,1)S(1)}, u32[]{:S(2)}, u32[]{:S(2)}) collective-permute-start(bf16[1088,256]{1,0:T(8,128)(2,1)S(1)} %join_line.1.refs_0_), channel_id=1, source_target_pairs={{24,0},{7,1},{26,2},{1,3},{28,4},{3,5},{30,6},{5,7},{0,8},{15,9},{... | collective-permute-start | bytes 1671176 | tf_op jit(solution)/shard_map/ppermute | solution.py:47
  42.7 13.1 %collective-permute-start.15 = (bf16[1088,256]{1,0:T(8,128)(2,1)S(1)}, bf16[1088,256]{1,0:T(8,128)(2,1)S(1)}, u32[]{:S(2)}, u32[]{:S(2)}) collective-permute-start(bf16[1088,256]{1,0:T(8,128)(2,1)S(1)} %join_line.1.refs_0_), channel_id=1, source_target_pairs={{1,0},{0,1},{3,2},{2,3},{5,4},{4,5},{7,6},{6,7},{9,8},{8,9},{11,10... | collective-permute-start | bytes 1671176 | tf_op jit(solution)/shard_map/ppermute | solution.py:56
  47.5 9.6 %collective-permute-start.16 = (bf16[1088,256]{1,0:T(8,128)(2,1)S(1)}, bf16[1088,256]{1,0:T(8,128)(2,1)S(1)}, u32[]{:S(2)}, u32[]{:S(2)}) collective-permute-start(bf16[1088,256]{1,0:T(8,128)(2,1)S(1)} %collective-permute-done.12.refs_1_), channel_id=1, source_target_pairs={{1,0},{0,1},{3,2},{2,3},{5,4},{4,5},{7,6},{6,7},{9,8},{8,9},{11,10... | collective-permute-start | bytes 1671176 | tf_op jit(solution)/shard_map/ppermute | solution.py:56
  49.9 7.8 %collective-permute-start.17 = (bf16[1088,256]{1,0:T(8,128)(2,1)S(1)}, bf16[1088,256]{1,0:T(8,128)(2,1)S(1)}, u32[]{:S(2)}, u32[]{:S(2)}) collective-permute-start(bf16[1088,256]{1,0:T(8,128)(2,1)S(1)} %collective-permute-done.13.refs_1_), channel_id=1, source_target_pairs={{1,0},{0,1},{3,2},{2,3},{5,4},{4,5},{7,6},{6,7},{9,8},{8,9},{11,10... | collective-permute-start | bytes 1671176 | tf_op jit(solution)/shard_map/ppermute | solution.py:56
  54.6 7.6 %collective-permute-start.19 = (bf16[1104,256]{1,0:T(8,128)(2,1)S(1)}, bf16[1104,256]{1,0:T(8,128)(2,1)S(1)}, u32[]{:S(2)}, u32[]{:S(2)}) collective-permute-start(bf16[1104,256]{1,0:T(8,128)(2,1)S(1)} %collective-permute-done.11.message.refs_0_), channel_id=1, source_target_pairs={{1,0},{0,1},{3,2},{2,3},{5,4},{4,5},{7,6},{6,7},{9,8},{8,9},{11,10... | collective-permute-start | bytes 1695752 | tf_op jit(solution)/shard_map/ppermute | solution.py:56
  55.8 3.1 %collective-permute-start.18 = (bf16[1088,256]{1,0:T(8,128)(2,1)S(1)}, bf16[1088,256]{1,0:T(8,128)(2,1)S(1)}, u32[]{:S(2)}, u32[]{:S(2)}) collective-permute-start(bf16[1088,256]{1,0:T(8,128)(2,1)S(1)} %touch.3.refs_1_), channel_id=1, source_target_pairs={{1,0},{0,1},{3,2},{2,3},{5,4},{4,5},{7,6},{6,7},{9,8},{8,9},{11,10... | collective-permute-start | bytes 1671176 | tf_op jit(solution)/shard_map/ppermute | solution.py:56
  55.8 9.7 %collective-permute-start.20 = (bf16[1104,256]{1,0:T(8,128)(2,1)S(1)}, bf16[1104,256]{1,0:T(8,128)(2,1)S(1)}, u32[]{:S(2)}, u32[]{:S(2)}) collective-permute-start(bf16[1104,256]{1,0:T(8,128)(2,1)S(1)} %collective-permute-done.11.message.refs_0_), channel_id=1, source_target_pairs={{8,0},{3,1},{10,2},{5,3},{12,4},{7,5},{14,6},{1,7},{16,8},{11,9},{... | collective-permute-start | bytes 1695752 | tf_op jit(solution)/shard_map/ppermute | solution.py:47
  57.1 14.0 %collective-permute-start.22 = (bf16[1104,256]{1,0:T(8,128)(2,1)S(1)}, bf16[1104,256]{1,0:T(8,128)(2,1)S(1)}, u32[]{:S(2)}, u32[]{:S(2)}) collective-permute-start(bf16[1104,256]{1,0:T(8,128)(2,1)S(1)} %collective-permute-done.11.message.refs_0_), channel_id=1, source_target_pairs={{16,0},{5,1},{18,2},{7,3},{20,4},{1,5},{22,6},{3,7},{24,8},{13,9},... | collective-permute-start | bytes 1695752 | tf_op jit(solution)/shard_map/ppermute | solution.py:47
  57.7 16.6 %collective-permute-start.24 = (bf16[1104,256]{1,0:T(8,128)(2,1)S(1)}, bf16[1104,256]{1,0:T(8,128)(2,1)S(1)}, u32[]{:S(2)}, u32[]{:S(2)}) collective-permute-start(bf16[1104,256]{1,0:T(8,128)(2,1)S(1)} %collective-permute-done.11.message.refs_0_), channel_id=1, source_target_pairs={{24,0},{7,1},{26,2},{1,3},{28,4},{3,5},{30,6},{5,7},{0,8},{15,9},{... | collective-permute-start | bytes 1695752 | tf_op jit(solution)/shard_map/ppermute | solution.py:47
  59.0 15.7 %copy-start = (f32[1,8,256,256]{3,2,1,0:T(8,128)S(1)}, f32[1,8,256,256]{3,2,1,0:T(8,128)}, u32[]{:S(2)}) copy-start(f32[1,8,256,256]{3,2,1,0:T(8,128)} %param.9) | copy-start | bytes 6291460
  61.2 25.5 %collective-permute-start.26 = (bf16[8,256,256]{2,1,0:T(8,128)(2,1)S(1)}, bf16[8,256,256]{2,1,0:T(8,128)(2,1)S(1)}, u32[]{:S(2)}, u32[]{:S(2)}) collective-permute-start(bf16[8,256,256]{2,1,0:T(8,128)(2,1)S(1)} %get-tuple-element.19.refs_0_), channel_id=1, source_target_pairs={{96,0},{33,1},{98,2},{35,3},{100,4},{37,5},{102,6},{39,7},{104,8},... | collective-permute-start | bytes 3145736 | tf_op jit(solution)/shard_map/ppermute | solution.py:65
  62.2 26.0 %collective-permute-start.27 = (bf16[8,256,256]{2,1,0:T(8,128)(2,1)S(1)}, bf16[8,256,256]{2,1,0:T(8,128)(2,1)S(1)}, u32[]{:S(2)}, u32[]{:S(2)}) collective-permute-start(bf16[8,256,256]{2,1,0:T(8,128)(2,1)S(1)} %get-tuple-element.20), channel_id=1, source_target_pairs={{32,0},{97,1},{34,2},{99,3},{36,4},{101,5},{38,6},{103,7},{40,8},{... | collective-permute-start | bytes 3145736 | tf_op jit(solution)/shard_map/ppermute | solution.py:65
  65.5 11.6 %collective-permute-start.21 = (bf16[1104,256]{1,0:T(8,128)(2,1)S(1)}, bf16[1104,256]{1,0:T(8,128)(2,1)S(1)}, u32[]{:S(2)}, u32[]{:S(2)}) collective-permute-start(bf16[1104,256]{1,0:T(8,128)(2,1)S(1)} %collective-permute-done.20.refs_1_), channel_id=1, source_target_pairs={{1,0},{0,1},{3,2},{2,3},{5,4},{4,5},{7,6},{6,7},{9,8},{8,9},{11,10... | collective-permute-start | bytes 1695752 | tf_op jit(solution)/shard_map/ppermute | solution.py:56
  71.1 6.2 %collective-permute-start.23 = (bf16[1104,256]{1,0:T(8,128)(2,1)S(1)}, bf16[1104,256]{1,0:T(8,128)(2,1)S(1)}, u32[]{:S(2)}, u32[]{:S(2)}) collective-permute-start(bf16[1104,256]{1,0:T(8,128)(2,1)S(1)} %collective-permute-done.22.refs_1_), channel_id=1, source_target_pairs={{1,0},{0,1},{3,2},{2,3},{5,4},{4,5},{7,6},{6,7},{9,8},{8,9},{11,10... | collective-permute-start | bytes 1695752 | tf_op jit(solution)/shard_map/ppermute | solution.py:56
  74.3 3.2 %collective-permute-start.25 = (bf16[1104,256]{1,0:T(8,128)(2,1)S(1)}, bf16[1104,256]{1,0:T(8,128)(2,1)S(1)}, u32[]{:S(2)}, u32[]{:S(2)}) collective-permute-start(bf16[1104,256]{1,0:T(8,128)(2,1)S(1)} %collective-permute-done.24.refs_1_), channel_id=1, source_target_pairs={{1,0},{0,1},{3,2},{2,3},{5,4},{4,5},{7,6},{6,7},{9,8},{8,9},{11,10... | collective-permute-start | bytes 1695752 | tf_op jit(solution)/shard_map/ppermute | solution.py:56

commit v7 on v5

--- a/solution.py
+++ b/solution.py
@@ -395,25 +395,62 @@
 ]
 
 
-def send_call(next_list, last_list, factors, *after):
-    def kernel(next_list, last_list, factors, *refs):
-        to_next, to_last, scales, lefts, rights, totals = refs[len(after) :]
+def expand2(lists, factors, scales, lefts, rights, totals):
+    def chunk(pairs, q, side):
+        for k in range(PER_CHUNK):
+            spot = q * PER_CHUNK + k
+            left, right = pairs[0, spot], pairs[1, spot]
+            weight = scales[pl.ds(left, 1), :] * scales[pl.ds(right, 1), :]
+            weight = jnp.broadcast_to(weight, (RANK, 128)).astype(bf16)
+            weight = jnp.concatenate([weight, weight], axis=1)
+            here = slice(k * RANK, (k + 1) * RANK)
+            lefts[side, here, :] = block_at(factors, pairs[4, spot]) * weight
+            rights[side, here, :] = block_at(factors, pairs[5, spot])
+
+    def couple(n, last):
+        for l in range(2):
+            for i in range(4):
+                chunk(lists[l], 4 * n + i, l * 4 + i)
+        terms = [
+            lax.dot_general(lefts[side], rights[side], TN, preferred_element_type=f32)
+            for side in range(8)
+        ]
+        last = list(last)
+        for l in range(2):
+            for i in range(4):
+                t = lists[l][2, 4 * n + i]
+                totals[l, t] = jnp.where(t == last[l], totals[l, t], 0.0) + terms[l * 4 + i]
+                last[l] = t
+        return tuple(last)
+
+    most = jnp.maximum(lists[0][3, 0], lists[1][3, 0])
+    lax.fori_loop(0, (most + 3) // 4, couple, (-1, -1))
+
+
+def send_call(next_list, last_list, factors):
+    def kernel(next_list, last_list, factors, to_next, to_last, scales, lefts, rights, totals):
         spread(factors, scales)
-        for pairs, out in ((next_list, to_next), (last_list, to_last)):
-            expand(pairs, factors, scales, lefts, rights, totals)
+        expand2((next_list, last_list), factors, scales, lefts, rights, totals)
+        for l, (pairs, out) in enumerate(((next_list, to_next), (last_list, to_last))):
             for t in range(NT_DEV):
-                out[t] = total_of(pairs, t, totals).astype(bf16)
+                out[t] = total_of(pairs, t, totals.at[l]).astype(bf16)
 
     out = jax.ShapeDtypeStruct((NT_DEV, BLOCK, BLOCK), bf16)
+    work = [
+        pltpu.VMEM((ZERO + 8, 128), f32),
+        pltpu.VMEM((8, RANK * PER_CHUNK, BLOCK), bf16),
+        pltpu.VMEM((8, RANK * PER_CHUNK, BLOCK), bf16),
+        pltpu.VMEM((2, NT_DEV, BLOCK, BLOCK), f32),
+    ]
     return pl.pallas_call(
         kernel,
         out_shape=(out, out),
-        in_specs=[SMEM, SMEM, VMEM] + [ANY] * len(after),
+        in_specs=[SMEM, SMEM, VMEM],
         out_specs=(VMEM, VMEM),
-        scratch_shapes=WORK,
+        scratch_shapes=work,
         compiler_params=params(),
         name="send_pairs",
-    )(next_list, last_list, factors, *after)
+    )(next_list, last_list, factors)
 
 
 def keep_call(pairs, base, factors, *after):

time: 91.8 us -> 91.7 us (level)
  waiting for transfers between devices: 42.6 us -> 44.4 us
  Pallas kernels: 18.1 us -> 16.5 us
    ppermute x3, waiting for transfers between devices: 14.4 us -> 16.5 us  [from_set(): lax.ppermute(x, 'set', [((me + d) % N_SET, me) for me in range(N_SET)])]
    pallas_call x2, Pallas kernels: 4.37 us -> 2.55 us  [keep_call(): pl.pallas_call(kernel, out_shape=jax.ShapeDtypeStruct((NT_DEV, BLOCK, BLO...]
  transfers between devices with their start and end apart: 28 -> 28, of which waited for: 19 -> 19; matrix products, arithmetic and copies ran while one was open for 1% -> 1% of each run, Pallas kernels for 11% -> 9%
where the time goes in v7:
time: 91.7 us; the launch traced here: 90.8 us
  waiting for transfers between devices  44.4 us (48%)
  starting transfers between devices  28 us (31%)
  Pallas kernels  16.5 us (18%)
    ppermute x15, waiting for transfers between devices, from_cand(): return lax.ppermute(x, 'cand', pairs)  26.2 us
    ppermute x15, starting transfers between devices, from_cand(): return lax.ppermute(x, 'cand', pairs)  18.7 us
    ppermute x3, waiting for transfers between devices, from_set(): lax.ppermute(x, 'set', [((me + d) % N_SET, me) for me in range(N_SET)])  16.5 us
    ppermute x10, starting transfers between devices, from_core(): return lax.ppermute(x, 'cand', [(me ^ 1, me) for me in range(N_CAND)])  5.69 us
    ppermute x3, starting transfers between devices, from_set(): lax.ppermute(x, 'set', [((me + d) % N_SET, me) for me in range(N_SET)])  3.56 us
    pallas_call x1, Pallas kernels, factor_call(): pl.pallas_call(factor_kernel, out_shape=jax.ShapeDtypeStruct((MSG, BLOCK)...  3.45 us
    pallas_call x1, Pallas kernels, send_call(): pl.pallas_call(kernel, out_shape=(out, out), in_specs=[SMEM, SMEM, VMEM],...  3.29 us
    pallas_call x1, Pallas kernels, sketch_call(): pl.pallas_call(sketch_kernel, out_shape=(half, half), in_specs=[SMEM, HBM...  3.05 us
  transfers between devices with their start and end apart: 28, of which 19 were waited for; matrix products, arithmetic and copies ran while one was open for 1% of the time, Pallas kernels for 9%

profile of v7, /device:TPU:6, one launch (start us, length us, event | category | flops | bytes accessed | tf_op | source)
XLA Modules:
  0.0 90.8 jit_solution(16805057950828418583)
XLA Ops:
  0.8 3.1 %sketch.1 = (f32[16,512]{1,0:T(8,128)S(1)}, f32[16,512]{1,0:T(8,128)S(1)}) custom-call(s32[2]{0:T(128)S(1)} %pad_add_fusion.place.refs_0_, bf16[2048,512]{1,0:T(8,128)(2,1)} %bitcast.22, bf16[32,512]{1,0:T(8,128)(2,1)S(1)} %bitcast.21), custom_call_target="tpu_custom_call" | custom-call | tf_op jit(solution)/shard_map/sketch/pallas_call | solution.py:78
  5.2 3.0 %collective-permute-start.1 = (f32[24,512]{1,0:T(8,128)S(1)}, f32[24,512]{1,0:T(8,128)S(1)}, u32[]{:S(2)}, u32[]{:S(2)}) collective-permute-start(f32[24,512]{1,0:T(8,128)S(1)} %sum_core.1.r0), channel_id=1, source_target_pairs={{2,0},{9,1},{4,2},{11,3},{6,4},{13,5},{0,6},{15,7},{10,8},{17,9},{... | collective-permute-start | bytes 147464 | tf_op jit(solution)/shard_map/ppermute | solution.py:47
  8.8 1.0 %collective-permute-start.3 = (f32[24,512]{1,0:T(8,128)S(1)}, f32[24,512]{1,0:T(8,128)S(1)}, u32[]{:S(2)}, u32[]{:S(2)}) collective-permute-start(f32[24,512]{1,0:T(8,128)S(1)} %sum_core.1.r0), channel_id=1, source_target_pairs={{6,0},{25,1},{0,2},{27,3},{2,4},{29,5},{4,6},{31,7},{14,8},{1,9},{... | collective-permute-start | bytes 147464 | tf_op jit(solution)/shard_map/ppermute | solution.py:47
  10.0 3.9 %collective-permute-done.2.r2 = f32[24,512]{1,0:T(8,128)S(1)} collective-permute-done((f32[24,512]{1,0:T(8,128)S(1)}, f32[24,512]{1,0:T(8,128)S(1)}, u32[]{:S(2)}, u32[]{:S(2)}) %collective-permute-start.2) | collective-permute-done | bytes 49184 | tf_op jit(solution)/shard_map/ppermute | solution.py:47
  14.3 4.1 %collective-permute-start.4 = (f32[24,512]{1,0:T(8,128)S(1)}, f32[24,512]{1,0:T(8,128)S(1)}, u32[]{:S(2)}, u32[]{:S(2)}) collective-permute-start(f32[24,512]{1,0:T(8,128)S(1)} %sum_first.1.r0), channel_id=1, source_target_pairs={{8,0},{3,1},{10,2},{5,3},{12,4},{7,5},{14,6},{1,7},{16,8},{11,9},{... | collective-permute-start | bytes 147464 | tf_op jit(solution)/shard_map/ppermute | solution.py:47
  18.4 1.3 %collective-permute-start.6 = (f32[24,512]{1,0:T(8,128)S(1)}, f32[24,512]{1,0:T(8,128)S(1)}, u32[]{:S(2)}, u32[]{:S(2)}) collective-permute-start(f32[24,512]{1,0:T(8,128)S(1)} %sum_first.1.r0), channel_id=1, source_target_pairs={{24,0},{7,1},{26,2},{1,3},{28,4},{3,5},{30,6},{5,7},{0,8},{15,9},{... | collective-permute-start | bytes 147464 | tf_op jit(solution)/shard_map/ppermute | solution.py:47
  20.2 3.9 %collective-permute-done.5.r2 = f32[24,512]{1,0:T(8,128)S(1)} collective-permute-done((f32[24,512]{1,0:T(8,128)S(1)}, f32[24,512]{1,0:T(8,128)S(1)}, u32[]{:S(2)}, u32[]{:S(2)}) %collective-permute-start.5) | collective-permute-done | bytes 49184 | tf_op jit(solution)/shard_map/ppermute | solution.py:47
  24.4 1.3 %collective-permute-done.7.other.refs_2_ = f32[48,512]{1,0:T(8,128)S(1)} collective-permute-done((f32[48,512]{1,0:T(8,128)S(1)}, f32[48,512]{1,0:T(8,128)S(1)}, u32[]{:S(2)}, u32[]{:S(2)}) %collective-permute-start.7) | collective-permute-done | bytes 98336 | tf_op jit(solution)/shard_map/ppermute | solution.py:51
  25.7 3.5 %factor.1.refs_3_.refs_0_ = bf16[272,256]{1,0:T(8,128)(2,1)S(1)} custom-call(s32[2]{0:T(128)S(1)} %pad_add_fusion.place.refs_0_, f32[48,512]{1,0:T(8,128)S(1)} %sum_second.1.own.refs_1_, f32[48,512]{1,0:T(8,128)S(1)} %collective-permute-done.7.other.refs_2_, bf16[2048,512]{1,0:T(8,128)(2,1)} %bitcast.23), custom_call_target="tpu_custom_call" | custom-call | tf_op jit(solution)/shard_map/factor/pallas_call | solution.py:171
  29.8 1.1 %collective-permute-start.9 = (bf16[272,256]{1,0:T(8,128)(2,1)S(1)}, bf16[272,256]{1,0:T(8,128)(2,1)S(1)}, u32[]{:S(2)}, u32[]{:S(2)}) collective-permute-start(bf16[272,256]{1,0:T(8,128)(2,1)S(1)} %factor.1.refs_3_.refs_0_), channel_id=1, source_target_pairs={{4,0},{17,1},{6,2},{19,3},{0,4},{21,5},{2,6},{23,7},{12,8},{25,9},... | collective-permute-start | bytes 417800 | tf_op jit(solution)/shard_map/ppermute | solution.py:47
  30.8 1.3 %collective-permute-start.10 = (bf16[272,256]{1,0:T(8,128)(2,1)S(1)}, bf16[272,256]{1,0:T(8,128)(2,1)S(1)}, u32[]{:S(2)}, u32[]{:S(2)}) collective-permute-start(bf16[272,256]{1,0:T(8,128)(2,1)S(1)} %factor.1.refs_3_.refs_0_), channel_id=1, source_target_pairs={{6,0},{25,1},{0,2},{27,3},{2,4},{29,5},{4,6},{31,7},{14,8},{1,9},{... | collective-permute-start | bytes 417800 | tf_op jit(solution)/shard_map/ppermute | solution.py:47
  32.1 1.2 %plan.1 = (s32[8,128]{1,0:T(8,128)S(1)}, s32[8,128]{1,0:T(8,128)S(1)}, bf16[16,256]{1,0:T(8,128)(2,1)S(1)}, s32[8,128]{1,0:T(8,128)S(1)}) custom-call(s32[2]{0:T(128)S(1)} %pad_add_fusion.place.refs_0_, f32[48,512]{1,0:T(8,128)S(1)} %sum_second.1.own.refs_1_, f32[48,512]{1,0:T(8,128)S(1)} %collective-permute-done.7.other.refs_2_, ...), custom_call_target="tpu_custom_call" | custom-call | tf_op jit(solution)/shard_map/plan/pallas_call | solution.py:321
  34.3 2.1 %collective-permute-done.9.refs_2_ = bf16[272,256]{1,0:T(8,128)(2,1)S(1)} collective-permute-done((bf16[272,256]{1,0:T(8,128)(2,1)S(1)}, bf16[272,256]{1,0:T(8,128)(2,1)S(1)}, u32[]{:S(2)}, u32[]{:S(2)}) %collective-permute-start.9) | collective-permute-done | bytes 139296 | tf_op jit(solution)/shard_map/ppermute | solution.py:47
  36.4 1.4 %collective-permute-done.10.refs_3_ = bf16[272,256]{1,0:T(8,128)(2,1)S(1)} collective-permute-done((bf16[272,256]{1,0:T(8,128)(2,1)S(1)}, bf16[272,256]{1,0:T(8,128)(2,1)S(1)}, u32[]{:S(2)}, u32[]{:S(2)}) %collective-permute-start.10) | collective-permute-done | bytes 139296 | tf_op jit(solution)/shard_map/ppermute | solution.py:47
  37.9 0.9 %collective-permute-start.13 = (bf16[1088,256]{1,0:T(8,128)(2,1)S(1)}, bf16[1088,256]{1,0:T(8,128)(2,1)S(1)}, u32[]{:S(2)}, u32[]{:S(2)}) collective-permute-start(bf16[1088,256]{1,0:T(8,128)(2,1)S(1)} %join_line.1.refs_0_), channel_id=1, source_target_pairs={{8,0},{3,1},{10,2},{5,3},{12,4},{7,5},{14,6},{1,7},{16,8},{11,9},{... | collective-permute-start | bytes 1671176 | tf_op jit(solution)/shard_map/ppermute | solution.py:47
  38.8 1.0 %collective-permute-start.15 = (bf16[1088,256]{1,0:T(8,128)(2,1)S(1)}, bf16[1088,256]{1,0:T(8,128)(2,1)S(1)}, u32[]{:S(2)}, u32[]{:S(2)}) collective-permute-start(bf16[1088,256]{1,0:T(8,128)(2,1)S(1)} %join_line.1.refs_0_), channel_id=1, source_target_pairs={{16,0},{5,1},{18,2},{7,3},{20,4},{1,5},{22,6},{3,7},{24,8},{13,9},... | collective-permute-start | bytes 1671176 | tf_op jit(solution)/shard_map/ppermute | solution.py:47
  39.9 1.5 %collective-permute-start.11 = (bf16[1104,256]{1,0:T(8,128)(2,1)S(1)}, bf16[1104,256]{1,0:T(8,128)(2,1)S(1)}, u32[]{:S(2)}, u32[]{:S(2)}) collective-permute-start(bf16[1104,256]{1,0:T(8,128)(2,1)S(1)} %join_far.1), channel_id=1, source_target_pairs={{64,0},{96,32},{0,64},{32,96},{65,1},{97,33},{1,65},{33,97},{66,2}... | collective-permute-start | bytes 1695752 | tf_op jit(solution)/shard_map/ppermute | solution.py:55
  41.3 1.3 %collective-permute-start.17 = (bf16[1088,256]{1,0:T(8,128)(2,1)S(1)}, bf16[1088,256]{1,0:T(8,128)(2,1)S(1)}, u32[]{:S(2)}, u32[]{:S(2)}) collective-permute-start(bf16[1088,256]{1,0:T(8,128)(2,1)S(1)} %join_line.1.refs_0_), channel_id=1, source_target_pairs={{24,0},{7,1},{26,2},{1,3},{28,4},{3,5},{30,6},{5,7},{0,8},{15,9},{... | collective-permute-start | bytes 1671176 | tf_op jit(solution)/shard_map/ppermute | solution.py:47
  42.7 4.8 %collective-permute-done.13.refs_1_ = bf16[1088,256]{1,0:T(8,128)(2,1)S(1)} collective-permute-done((bf16[1088,256]{1,0:T(8,128)(2,1)S(1)}, bf16[1088,256]{1,0:T(8,128)(2,1)S(1)}, u32[]{:S(2)}, u32[]{:S(2)}) %collective-permute-start.13) | collective-permute-done | bytes 557088 | tf_op jit(solution)/shard_map/ppermute | solution.py:47
  47.5 2.5 %collective-permute-done.15.refs_1_ = bf16[1088,256]{1,0:T(8,128)(2,1)S(1)} collective-permute-done((bf16[1088,256]{1,0:T(8,128)(2,1)S(1)}, bf16[1088,256]{1,0:T(8,128)(2,1)S(1)}, u32[]{:S(2)}, u32[]{:S(2)}) %collective-permute-start.15) | collective-permute-done | bytes 557088 | tf_op jit(solution)/shard_map/ppermute | solution.py:47
  49.9 4.7 %collective-permute-done.11.message.refs_0_ = bf16[1104,256]{1,0:T(8,128)(2,1)S(1)} collective-permute-done((bf16[1104,256]{1,0:T(8,128)(2,1)S(1)}, bf16[1104,256]{1,0:T(8,128)(2,1)S(1)}, u32[]{:S(2)}, u32[]{:S(2)}) %collective-permute-start.11) | collective-permute-done | bytes 565280 | tf_op jit(solution)/shard_map/ppermute | solution.py:55
  54.6 1.2 %collective-permute-done.17.refs_1_ = bf16[1088,256]{1,0:T(8,128)(2,1)S(1)} collective-permute-done((bf16[1088,256]{1,0:T(8,128)(2,1)S(1)}, bf16[1088,256]{1,0:T(8,128)(2,1)S(1)}, u32[]{:S(2)}, u32[]{:S(2)}) %collective-permute-start.17) | collective-permute-done | bytes 557088 | tf_op jit(solution)/shard_map/ppermute | solution.py:47
  59.1 3.3 %send_pairs.1 = (bf16[8,256,256]{2,1,0:T(8,128)(2,1)S(1)}, bf16[8,256,256]{2,1,0:T(8,128)(2,1)S(1)}) custom-call(s32[8,128]{1,0:T(8,128)S(1)} %get-tuple-element.15.refs_4_.next_list, s32[8,128]{1,0:T(8,128)S(1)} %get-tuple-element.18.last_list, bf16[8704,256]{1,0:T(8,128)(2,1)S(1)} %put.23.factors), custom_call_target="tpu_custom_call" | custom-call | tf_op jit(solution)/shard_map/send_pairs/pallas_call | solution.py:445
  62.4 2.0 %collective-permute-start.27 = (bf16[8,256,256]{2,1,0:T(8,128)(2,1)S(1)}, bf16[8,256,256]{2,1,0:T(8,128)(2,1)S(1)}, u32[]{:S(2)}, u32[]{:S(2)}) collective-permute-start(bf16[8,256,256]{2,1,0:T(8,128)(2,1)S(1)} %get-tuple-element.20), channel_id=1, source_target_pairs={{32,0},{64,32},{96,64},{0,96},{33,1},{65,33},{97,65},{1,97},{34,2}... | collective-permute-start | bytes 3145736 | tf_op jit(solution)/shard_map/ppermute | solution.py:55
  64.5 1.0 %collective-permute-done.20.refs_1_ = bf16[1104,256]{1,0:T(8,128)(2,1)S(1)} collective-permute-done((bf16[1104,256]{1,0:T(8,128)(2,1)S(1)}, bf16[1104,256]{1,0:T(8,128)(2,1)S(1)}, u32[]{:S(2)}, u32[]{:S(2)}) %collective-permute-start.20) | collective-permute-done | bytes 565280 | tf_op jit(solution)/shard_map/ppermute | solution.py:47
  65.4 5.2 %collective-permute-start.21 = (bf16[1104,256]{1,0:T(8,128)(2,1)S(1)}, bf16[1104,256]{1,0:T(8,128)(2,1)S(1)}, u32[]{:S(2)}, u32[]{:S(2)}) collective-permute-start(bf16[1104,256]{1,0:T(8,128)(2,1)S(1)} %collective-permute-done.20.refs_1_), channel_id=1, source_target_pairs={{1,0},{0,1},{3,2},{2,3},{5,4},{4,5},{7,6},{6,7},{9,8},{8,9},{11,10... | collective-permute-start | bytes 1695752 | tf_op jit(solution)/shard_map/ppermute | solution.py:51
  70.7 3.2 %collective-permute-done.24.refs_1_ = bf16[1104,256]{1,0:T(8,128)(2,1)S(1)} collective-permute-done((bf16[1104,256]{1,0:T(8,128)(2,1)S(1)}, bf16[1104,256]{1,0:T(8,128)(2,1)S(1)}, u32[]{:S(2)}, u32[]{:S(2)}) %collective-permute-start.24) | collective-permute-done | bytes 565280 | tf_op jit(solution)/shard_map/ppermute | solution.py:47
  74.3 1.3 %keep_pairs.2.base = f32[8,256,256]{2,1,0:T(8,128)S(1)} custom-call(s32[8,128]{1,0:T(8,128)S(1)} %get-tuple-element.17.pairs, f32[8,256,256]{2,1,0:T(8,128)S(1)} %bitcast.20, bf16[8704,256]{1,0:T(8,128)(2,1)S(1)} %put.23.factors, bf16[8,256,256]{2,1,0:T(8,128)(2,1)S(1)} %get-tuple-element.19.refs_0_), custom_call_target="tpu_custom_call" | custom-call | tf_op jit(solution)/shard_map/keep_pairs/pallas_call | solution.py:464
  76.3 1.3 %keep_pairs.3.base = f32[8,256,256]{2,1,0:T(8,128)S(1)} custom-call(s32[8,128]{1,0:T(8,128)S(1)} %unpack.1.pairs, f32[8,256,256]{2,1,0:T(8,128)S(1)} %keep_pairs.2.base, bf16[8704,256]{1,0:T(8,128)(2,1)S(1)} %put.31.factors), custom_call_target="tpu_custom_call" | custom-call | tf_op jit(solution)/shard_map/keep_pairs/pallas_call | solution.py:464
  77.5 9.6 %collective-permute-done.26.refs_0_ = bf16[8,256,256]{2,1,0:T(8,128)(2,1)S(1)} collective-permute-done((bf16[8,256,256]{2,1,0:T(8,128)(2,1)S(1)}, bf16[8,256,256]{2,1,0:T(8,128)(2,1)S(1)}, u32[]{:S(2)}, u32[]{:S(2)}) %collective-permute-start.26) | collective-permute-done | bytes 1048608 | tf_op jit(solution)/shard_map/ppermute | solution.py:55
  87.1 2.2 %collective-permute-done.27.refs_0_ = bf16[8,256,256]{2,1,0:T(8,128)(2,1)S(1)} collective-permute-done((bf16[8,256,256]{2,1,0:T(8,128)(2,1)S(1)}, bf16[8,256,256]{2,1,0:T(8,128)(2,1)S(1)}, u32[]{:S(2)}, u32[]{:S(2)}) %collective-permute-start.27) | collective-permute-done | bytes 1048608 | tf_op jit(solution)/shard_map/ppermute | solution.py:55
  89.4 1.4 %final.1 = f32[8,256,256]{2,1,0:T(8,128)} custom-call(f32[8,256,256]{2,1,0:T(8,128)S(1)} %keep_pairs.3.base, bf16[8,256,256]{2,1,0:T(8,128)(2,1)S(1)} %touch.2.one, bf16[8,256,256]{2,1,0:T(8,128)(2,1)S(1)} %touch.3.two), custom_call_target="tpu_custom_call" | custom-call | tf_op jit(solution)/shard_map/final/pallas_call | solution.py:485
  (61 shorter events, 10.0 us)
Async XLA Ops:
  0.1 0.8 copy-start.1
  3.9 1.3 %collective-permute-start = (f32[16,512]{1,0:T(8,128)S(1)}, f32[16,512]{1,0:T(8,128)S(1)}, u32[]{:S(2)}, u32[]{:S(2)}) collective-permute-start(f32[16,512]{1,0:T(8,128)S(1)} %get-tuple-element.14), channel_id=1, source_target_pairs={{1,0},{0,1},{3,2},{2,3},{5,4},{4,5},{7,6},{6,7},{9,8},{8,9},{11,10... | collective-permute-start | bytes 98312 | tf_op jit(solution)/shard_map/ppermute | solution.py:51
  5.2 4.8 %collective-permute-start.1 = (f32[24,512]{1,0:T(8,128)S(1)}, f32[24,512]{1,0:T(8,128)S(1)}, u32[]{:S(2)}, u32[]{:S(2)}) collective-permute-start(f32[24,512]{1,0:T(8,128)S(1)} %sum_core.1.r0), channel_id=1, source_target_pairs={{2,0},{9,1},{4,2},{11,3},{6,4},{13,5},{0,6},{15,7},{10,8},{17,9},{... | collective-permute-start | bytes 147464 | tf_op jit(solution)/shard_map/ppermute | solution.py:47
  8.2 5.6 %collective-permute-start.2 = (f32[24,512]{1,0:T(8,128)S(1)}, f32[24,512]{1,0:T(8,128)S(1)}, u32[]{:S(2)}, u32[]{:S(2)}) collective-permute-start(f32[24,512]{1,0:T(8,128)S(1)} %sum_core.1.r0), channel_id=1, source_target_pairs={{4,0},{17,1},{6,2},{19,3},{0,4},{21,5},{2,6},{23,7},{12,8},{25,9},... | collective-permute-start | bytes 147464 | tf_op jit(solution)/shard_map/ppermute | solution.py:47
  8.8 5.5 %collective-permute-start.3 = (f32[24,512]{1,0:T(8,128)S(1)}, f32[24,512]{1,0:T(8,128)S(1)}, u32[]{:S(2)}, u32[]{:S(2)}) collective-permute-start(f32[24,512]{1,0:T(8,128)S(1)} %sum_core.1.r0), channel_id=1, source_target_pairs={{6,0},{25,1},{0,2},{27,3},{2,4},{29,5},{4,6},{31,7},{14,8},{1,9},{... | collective-permute-start | bytes 147464 | tf_op jit(solution)/shard_map/ppermute | solution.py:47
  14.3 5.9 %collective-permute-start.4 = (f32[24,512]{1,0:T(8,128)S(1)}, f32[24,512]{1,0:T(8,128)S(1)}, u32[]{:S(2)}, u32[]{:S(2)}) collective-permute-start(f32[24,512]{1,0:T(8,128)S(1)} %sum_first.1.r0), channel_id=1, source_target_pairs={{8,0},{3,1},{10,2},{5,3},{12,4},{7,5},{14,6},{1,7},{16,8},{11,9},{... | collective-permute-start | bytes 147464 | tf_op jit(solution)/shard_map/ppermute | solution.py:47
  18.4 5.7 %collective-permute-start.5 = (f32[24,512]{1,0:T(8,128)S(1)}, f32[24,512]{1,0:T(8,128)S(1)}, u32[]{:S(2)}, u32[]{:S(2)}) collective-permute-start(f32[24,512]{1,0:T(8,128)S(1)} %sum_first.1.r0), channel_id=1, source_target_pairs={{16,0},{5,1},{18,2},{7,3},{20,4},{1,5},{22,6},{3,7},{24,8},{13,9},... | collective-permute-start | bytes 147464 | tf_op jit(solution)/shard_map/ppermute | solution.py:47
  18.4 5.8 %collective-permute-start.6 = (f32[24,512]{1,0:T(8,128)S(1)}, f32[24,512]{1,0:T(8,128)S(1)}, u32[]{:S(2)}, u32[]{:S(2)}) collective-permute-start(f32[24,512]{1,0:T(8,128)S(1)} %sum_first.1.r0), channel_id=1, source_target_pairs={{24,0},{7,1},{26,2},{1,3},{28,4},{3,5},{30,6},{5,7},{0,8},{15,9},{... | collective-permute-start | bytes 147464 | tf_op jit(solution)/shard_map/ppermute | solution.py:47
  24.3 1.4 %collective-permute-start.7 = (f32[48,512]{1,0:T(8,128)S(1)}, f32[48,512]{1,0:T(8,128)S(1)}, u32[]{:S(2)}, u32[]{:S(2)}) collective-permute-start(f32[48,512]{1,0:T(8,128)S(1)} %sum_second.1.own.refs_1_), channel_id=1, source_target_pairs={{1,0},{0,1},{3,2},{2,3},{5,4},{4,5},{7,6},{6,7},{9,8},{8,9},{11,10... | collective-permute-start | bytes 294920 | tf_op jit(solution)/shard_map/ppermute | solution.py:51
  29.1 5.1 %collective-permute-start.8 = (bf16[272,256]{1,0:T(8,128)(2,1)S(1)}, bf16[272,256]{1,0:T(8,128)(2,1)S(1)}, u32[]{:S(2)}, u32[]{:S(2)}) collective-permute-start(bf16[272,256]{1,0:T(8,128)(2,1)S(1)} %factor.1.refs_3_.refs_0_), channel_id=1, source_target_pairs={{2,0},{9,1},{4,2},{11,3},{6,4},{13,5},{0,6},{15,7},{10,8},{17,9},{... | collective-permute-start | bytes 417800 | tf_op jit(solution)/shard_map/ppermute | solution.py:47
  29.8 6.6 %collective-permute-start.9 = (bf16[272,256]{1,0:T(8,128)(2,1)S(1)}, bf16[272,256]{1,0:T(8,128)(2,1)S(1)}, u32[]{:S(2)}, u32[]{:S(2)}) collective-permute-start(bf16[272,256]{1,0:T(8,128)(2,1)S(1)} %factor.1.refs_3_.refs_0_), channel_id=1, source_target_pairs={{4,0},{17,1},{6,2},{19,3},{0,4},{21,5},{2,6},{23,7},{12,8},{25,9},... | collective-permute-start | bytes 417800 | tf_op jit(solution)/shard_map/ppermute | solution.py:47
  30.8 7.0 %collective-permute-start.10 = (bf16[272,256]{1,0:T(8,128)(2,1)S(1)}, bf16[272,256]{1,0:T(8,128)(2,1)S(1)}, u32[]{:S(2)}, u32[]{:S(2)}) collective-permute-start(bf16[272,256]{1,0:T(8,128)(2,1)S(1)} %factor.1.refs_3_.refs_0_), channel_id=1, source_target_pairs={{6,0},{25,1},{0,2},{27,3},{2,4},{29,5},{4,6},{31,7},{14,8},{1,9},{... | collective-permute-start | bytes 417800 | tf_op jit(solution)/shard_map/ppermute | solution.py:47
  37.9 9.6 %collective-permute-start.13 = (bf16[1088,256]{1,0:T(8,128)(2,1)S(1)}, bf16[1088,256]{1,0:T(8,128)(2,1)S(1)}, u32[]{:S(2)}, u32[]{:S(2)}) collective-permute-start(bf16[1088,256]{1,0:T(8,128)(2,1)S(1)} %join_line.1.refs_0_), channel_id=1, source_target_pairs={{8,0},{3,1},{10,2},{5,3},{12,4},{7,5},{14,6},{1,7},{16,8},{11,9},{... | collective-permute-start | bytes 1671176 | tf_op jit(solution)/shard_map/ppermute | solution.py:47
  38.8 11.1 %collective-permute-start.15 = (bf16[1088,256]{1,0:T(8,128)(2,1)S(1)}, bf16[1088,256]{1,0:T(8,128)(2,1)S(1)}, u32[]{:S(2)}, u32[]{:S(2)}) collective-permute-start(bf16[1088,256]{1,0:T(8,128)(2,1)S(1)} %join_line.1.refs_0_), channel_id=1, source_target_pairs={{16,0},{5,1},{18,2},{7,3},{20,4},{1,5},{22,6},{3,7},{24,8},{13,9},... | collective-permute-start | bytes 1671176 | tf_op jit(solution)/shard_map/ppermute | solution.py:47
  39.9 14.7 %collective-permute-start.11 = (bf16[1104,256]{1,0:T(8,128)(2,1)S(1)}, bf16[1104,256]{1,0:T(8,128)(2,1)S(1)}, u32[]{:S(2)}, u32[]{:S(2)}) collective-permute-start(bf16[1104,256]{1,0:T(8,128)(2,1)S(1)} %join_far.1), channel_id=1, source_target_pairs={{64,0},{96,32},{0,64},{32,96},{65,1},{97,33},{1,65},{33,97},{66,2}... | collective-permute-start | bytes 1695752 | tf_op jit(solution)/shard_map/ppermute | solution.py:55
  41.3 14.4 %collective-permute-start.17 = (bf16[1088,256]{1,0:T(8,128)(2,1)S(1)}, bf16[1088,256]{1,0:T(8,128)(2,1)S(1)}, u32[]{:S(2)}, u32[]{:S(2)}) collective-permute-start(bf16[1088,256]{1,0:T(8,128)(2,1)S(1)} %join_line.1.refs_0_), channel_id=1, source_target_pairs={{24,0},{7,1},{26,2},{1,3},{28,4},{3,5},{30,6},{5,7},{0,8},{15,9},{... | collective-permute-start | bytes 1671176 | tf_op jit(solution)/shard_map/ppermute | solution.py:47
  42.7 13.1 %collective-permute-start.12 = (bf16[1088,256]{1,0:T(8,128)(2,1)S(1)}, bf16[1088,256]{1,0:T(8,128)(2,1)S(1)}, u32[]{:S(2)}, u32[]{:S(2)}) collective-permute-start(bf16[1088,256]{1,0:T(8,128)(2,1)S(1)} %join_line.1.refs_0_), channel_id=1, source_target_pairs={{1,0},{0,1},{3,2},{2,3},{5,4},{4,5},{7,6},{6,7},{9,8},{8,9},{11,10... | collective-permute-start | bytes 1671176 | tf_op jit(solution)/shard_map/ppermute | solution.py:51
  47.5 9.3 %collective-permute-start.14 = (bf16[1088,256]{1,0:T(8,128)(2,1)S(1)}, bf16[1088,256]{1,0:T(8,128)(2,1)S(1)}, u32[]{:S(2)}, u32[]{:S(2)}) collective-permute-start(bf16[1088,256]{1,0:T(8,128)(2,1)S(1)} %collective-permute-done.13.refs_1_), channel_id=1, source_target_pairs={{1,0},{0,1},{3,2},{2,3},{5,4},{4,5},{7,6},{6,7},{9,8},{8,9},{11,10... | collective-permute-start | bytes 1671176 | tf_op jit(solution)/shard_map/ppermute | solution.py:51
  49.9 7.5 %collective-permute-start.16 = (bf16[1088,256]{1,0:T(8,128)(2,1)S(1)}, bf16[1088,256]{1,0:T(8,128)(2,1)S(1)}, u32[]{:S(2)}, u32[]{:S(2)}) collective-permute-start(bf16[1088,256]{1,0:T(8,128)(2,1)S(1)} %collective-permute-done.15.refs_1_), channel_id=1, source_target_pairs={{1,0},{0,1},{3,2},{2,3},{5,4},{4,5},{7,6},{6,7},{9,8},{8,9},{11,10... | collective-permute-start | bytes 1671176 | tf_op jit(solution)/shard_map/ppermute | solution.py:51
  54.6 7.9 %collective-permute-start.19 = (bf16[1104,256]{1,0:T(8,128)(2,1)S(1)}, bf16[1104,256]{1,0:T(8,128)(2,1)S(1)}, u32[]{:S(2)}, u32[]{:S(2)}) collective-permute-start(bf16[1104,256]{1,0:T(8,128)(2,1)S(1)} %collective-permute-done.11.message.refs_0_), channel_id=1, source_target_pairs={{1,0},{0,1},{3,2},{2,3},{5,4},{4,5},{7,6},{6,7},{9,8},{8,9},{11,10... | collective-permute-start | bytes 1695752 | tf_op jit(solution)/shard_map/ppermute | solution.py:51
  55.8 3.2 %collective-permute-start.18 = (bf16[1088,256]{1,0:T(8,128)(2,1)S(1)}, bf16[1088,256]{1,0:T(8,128)(2,1)S(1)}, u32[]{:S(2)}, u32[]{:S(2)}) collective-permute-start(bf16[1088,256]{1,0:T(8,128)(2,1)S(1)} %collective-permute-done.17.refs_1_), channel_id=1, source_target_pairs={{1,0},{0,1},{3,2},{2,3},{5,4},{4,5},{7,6},{6,7},{9,8},{8,9},{11,10... | collective-permute-start | bytes 1671176 | tf_op jit(solution)/shard_map/ppermute | solution.py:51
  55.8 9.6 %collective-permute-start.20 = (bf16[1104,256]{1,0:T(8,128)(2,1)S(1)}, bf16[1104,256]{1,0:T(8,128)(2,1)S(1)}, u32[]{:S(2)}, u32[]{:S(2)}) collective-permute-start(bf16[1104,256]{1,0:T(8,128)(2,1)S(1)} %collective-permute-done.11.message.refs_0_), channel_id=1, source_target_pairs={{8,0},{3,1},{10,2},{5,3},{12,4},{7,5},{14,6},{1,7},{16,8},{11,9},{... | collective-permute-start | bytes 1695752 | tf_op jit(solution)/shard_map/ppermute | solution.py:47
  56.7 13.9 %collective-permute-start.22 = (bf16[1104,256]{1,0:T(8,128)(2,1)S(1)}, bf16[1104,256]{1,0:T(8,128)(2,1)S(1)}, u32[]{:S(2)}, u32[]{:S(2)}) collective-permute-start(bf16[1104,256]{1,0:T(8,128)(2,1)S(1)} %collective-permute-done.11.message.refs_0_), channel_id=1, source_target_pairs={{16,0},{5,1},{18,2},{7,3},{20,4},{1,5},{22,6},{3,7},{24,8},{13,9},... | collective-permute-start | bytes 1695752 | tf_op jit(solution)/shard_map/ppermute | solution.py:47
  57.4 16.5 %collective-permute-start.24 = (bf16[1104,256]{1,0:T(8,128)(2,1)S(1)}, bf16[1104,256]{1,0:T(8,128)(2,1)S(1)}, u32[]{:S(2)}, u32[]{:S(2)}) collective-permute-start(bf16[1104,256]{1,0:T(8,128)(2,1)S(1)} %collective-permute-done.11.message.refs_0_), channel_id=1, source_target_pairs={{24,0},{7,1},{26,2},{1,3},{28,4},{3,5},{30,6},{5,7},{0,8},{15,9},{... | collective-permute-start | bytes 1695752 | tf_op jit(solution)/shard_map/ppermute | solution.py:47
  59.0 15.2 %copy-start = (f32[1,8,256,256]{3,2,1,0:T(8,128)S(1)}, f32[1,8,256,256]{3,2,1,0:T(8,128)}, u32[]{:S(2)}) copy-start(f32[1,8,256,256]{3,2,1,0:T(8,128)} %param.9) | copy-start | bytes 6291460
  62.4 24.8 %collective-permute-start.26 = (bf16[8,256,256]{2,1,0:T(8,128)(2,1)S(1)}, bf16[8,256,256]{2,1,0:T(8,128)(2,1)S(1)}, u32[]{:S(2)}, u32[]{:S(2)}) collective-permute-start(bf16[8,256,256]{2,1,0:T(8,128)(2,1)S(1)} %get-tuple-element.19.refs_0_), channel_id=1, source_target_pairs={{96,0},{0,32},{32,64},{64,96},{97,1},{1,33},{33,65},{65,97},{98,2}... | collective-permute-start | bytes 3145736 | tf_op jit(solution)/shard_map/ppermute | solution.py:55
  62.4 26.9 %collective-permute-start.27 = (bf16[8,256,256]{2,1,0:T(8,128)(2,1)S(1)}, bf16[8,256,256]{2,1,0:T(8,128)(2,1)S(1)}, u32[]{:S(2)}, u32[]{:S(2)}) collective-permute-start(bf16[8,256,256]{2,1,0:T(8,128)(2,1)S(1)} %get-tuple-element.20), channel_id=1, source_target_pairs={{32,0},{64,32},{96,64},{0,96},{33,1},{65,33},{97,65},{1,97},{34,2}... | collective-permute-start | bytes 3145736 | tf_op jit(solution)/shard_map/ppermute | solution.py:55
  65.4 10.3 %collective-permute-start.21 = (bf16[1104,256]{1,0:T(8,128)(2,1)S(1)}, bf16[1104,256]{1,0:T(8,128)(2,1)S(1)}, u32[]{:S(2)}, u32[]{:S(2)}) collective-permute-start(bf16[1104,256]{1,0:T(8,128)(2,1)S(1)} %collective-permute-done.20.refs_1_), channel_id=1, source_target_pairs={{1,0},{0,1},{3,2},{2,3},{5,4},{4,5},{7,6},{6,7},{9,8},{8,9},{11,10... | collective-permute-start | bytes 1695752 | tf_op jit(solution)/shard_map/ppermute | solution.py:51
  70.7 5.3 %collective-permute-start.23 = (bf16[1104,256]{1,0:T(8,128)(2,1)S(1)}, bf16[1104,256]{1,0:T(8,128)(2,1)S(1)}, u32[]{:S(2)}, u32[]{:S(2)}) collective-permute-start(bf16[1104,256]{1,0:T(8,128)(2,1)S(1)} %collective-permute-done.22.refs_1_), channel_id=1, source_target_pairs={{1,0},{0,1},{3,2},{2,3},{5,4},{4,5},{7,6},{6,7},{9,8},{8,9},{11,10... | collective-permute-start | bytes 1695752 | tf_op jit(solution)/shard_map/ppermute | solution.py:51
  73.9 2.3 %collective-permute-start.25 = (bf16[1104,256]{1,0:T(8,128)(2,1)S(1)}, bf16[1104,256]{1,0:T(8,128)(2,1)S(1)}, u32[]{:S(2)}, u32[]{:S(2)}) collective-permute-start(bf16[1104,256]{1,0:T(8,128)(2,1)S(1)} %collective-permute-done.24.refs_1_), channel_id=1, source_target_pairs={{1,0},{0,1},{3,2},{2,3},{5,4},{4,5},{7,6},{6,7},{9,8},{8,9},{11,10... | collective-permute-start | bytes 1695752 | tf_op jit(solution)/shard_map/ppermute | solution.py:51
